TPU v7x, 32 devices: a whole 2x2x4 slice. The times are simulated.
32 devices in a mesh: rep: 2 (over x), seq: 16 (over z, y, core).
Axes of the slice: x: 2, y: 2, z: 4, core: 2. Of those that a mesh axis runs over, the one named last changes fastest.
Arguments:
- qkv: bfloat16 [4096, 40, 3, 128], P(('rep', 'seq')), parts along dimension 0, may hold values from -10 to 10, as said below
- block_ids: int32 [32, 40, 4], P(('rep', 'seq')), parts along dimension 0, may hold values from 0 to 15, as said below
- counts: int32 [32, 40], P(('rep', 'seq')), parts along dimension 0, may hold values from 1 to 4, as said below
Outputs:
- attended: bfloat16 [4096, 40, 128], P(('rep', 'seq')), parts along dimension 0
There are 2 independent parts, one for each index of `rep`. A program takes and returns all parts, laid end to end along the dimension named above; each array names one. Nothing has to cross between parts.
Inputs may be any that keep to these rules, and one draw needn't show every extreme that they name: `qkv`: real values; a few queries may nearly coincide with scaled keys of their own block. `block_ids`: the entries of one list are distinct, and entry 0 is the query block itself. Entries at positions counts and beyond are padding and are ignored. Live counts vary from head to head; the most, 4, is reached in every draw.
All inputs are finite; a program needn't handle non-finite values.
Results may differ from a plain program's by a relative error of at most 0.0044.
Values may be sent and summed in bfloat16 or wider, within the bound.
No kernel may reach another device: no remote copies, remote signals or barrier semaphores. Data moves between devices by JAX's collectives and lax.ppermute only.
A program may use at most 128 MiB of HBM per device.

v0:
```python
import math

import jax
import jax.numpy as jnp
from jax import lax
from jax.sharding import PartitionSpec as P


def attend(query_rows, key_rows, value_rows, key_ids, live_count):
    longest = jnp.max(live_count)
    row_blocks = query_rows.shape[0]
    width = query_rows.shape[1]
    root = math.sqrt(query_rows.shape[2])

    def scores_at(step):
        column = lax.dynamic_index_in_dim(key_ids, step, 1, keepdims=False)
        picked = jnp.take(key_rows, column, axis=0)
        scores = (
            jnp.einsum("qid,qjd->qij", query_rows, picked, preferred_element_type=jnp.float32)
            / root
        )
        is_live = (step < live_count)[:, None, None]
        return (scores, column, is_live)

    def first_pass(step, peak_row):
        scores, column, is_live = scores_at(step)
        return jnp.where(
            is_live[:, :, 0], jnp.maximum(peak_row, jnp.max(scores, axis=-1)), peak_row
        )

    peak_row = lax.fori_loop(
        0, longest, first_pass, jnp.full((row_blocks, width), -1e30, jnp.float32)
    )

    def second_pass(step, state):
        totals, summed = state
        scores, column, is_live = scores_at(step)
        picked_values = jnp.take(value_rows, column, axis=0)
        weights = jnp.where(is_live, jnp.exp(scores - peak_row[:, :, None]), 0.0)
        totals = totals + jnp.sum(weights, axis=-1)
        summed = summed + jnp.einsum(
            "qij,qjd->qid",
            weights.astype(jnp.bfloat16),
            picked_values,
            preferred_element_type=jnp.float32,
        )
        return (totals, summed)

    start_state = (
        jnp.zeros((row_blocks, width), jnp.float32),
        jnp.zeros(query_rows.shape, jnp.float32),
    )
    totals, summed = lax.fori_loop(0, longest, second_pass, start_state)
    safe_totals = jnp.where(totals > 0.0, totals, 1.0)
    attended = (summed / safe_totals[:, :, None]).astype(jnp.bfloat16)
    return attended.reshape(row_blocks * width, query_rows.shape[2])


def body(qkv, block_ids, counts):
    tok_rows = qkv.shape[0]
    heads = qkv.shape[1]
    head_dim = qkv.shape[3]
    local_blocks = block_ids.shape[0]
    list_len = block_ids.shape[2]
    block_rows = tok_rows // local_blocks
    seq_count = lax.axis_size("seq")
    total_rows = tok_rows * seq_count
    all_blocks = local_blocks * seq_count
    per_device = -(-heads // seq_count)
    head_index = jnp.arange(heads, dtype=jnp.int32)
    position = head_index % seq_count * per_device + head_index // seq_count
    owner_table = jnp.full((seq_count * per_device,), -1, jnp.int32).at[position].set(head_index)
    filled = owner_table >= 0
    chosen = jnp.maximum(owner_table, 0)
    all_send = jnp.take(qkv, chosen, axis=1).reshape(tok_rows, seq_count, per_device * 3 * head_dim)
    id_send = jnp.take(block_ids, chosen, axis=1).reshape(
        local_blocks, seq_count, per_device * list_len
    )
    count_send = jnp.where(filled[None, :], jnp.take(counts, chosen, axis=1), 0).reshape(
        local_blocks, seq_count, per_device
    )
    all_recv, id_recv, count_recv = (
        lax.all_to_all(all_send, "seq", split_axis=1, concat_axis=0, tiled=True),
        lax.all_to_all(id_send, "seq", split_axis=1, concat_axis=0, tiled=True),
        lax.all_to_all(count_send, "seq", split_axis=1, concat_axis=0, tiled=True),
    )
    all_recv = all_recv.reshape(total_rows, per_device, 3, head_dim)
    id_recv = id_recv.reshape(all_blocks, per_device, list_len)
    count_recv = count_recv.reshape(all_blocks, per_device)
    outputs = []
    for inner in range(per_device):
        query_rows = all_recv[:, inner, 0].reshape(all_blocks, block_rows, head_dim)
        key_rows = all_recv[:, inner, 1].reshape(all_blocks, block_rows, head_dim)
        value_rows = all_recv[:, inner, 2].reshape(all_blocks, block_rows, head_dim)
        outputs.append(
            attend(query_rows, key_rows, value_rows, id_recv[:, inner], count_recv[:, inner])
        )
    result = jnp.stack(outputs, axis=1).reshape(total_rows, 1, per_device * head_dim)
    returned = lax.all_to_all(result, "seq", split_axis=0, concat_axis=1, tiled=True)
    returned = returned.reshape(tok_rows, seq_count * per_device, head_dim)
    return jnp.take(returned, position, axis=1)


def solution(mesh):
    in_specs = (
        P(("rep", "seq"), None, None, None),
        P(("rep", "seq"), None, None),
        P(("rep", "seq"), None),
    )
    out_specs = P(("rep", "seq"), None, None)
    return jax.shard_map(body, mesh=mesh, in_specs=in_specs, out_specs=out_specs, check_vma=False)
```

profile of v0, /device:TPU:15, one launch (start us, length us, event | category | flops | bytes accessed | tf_op | source)
XLA Modules:
  0.0 338.9 jit_solution(15120817240804188791)
XLA Ops:
  2.2 6.6 %all-to-all-start = ((s32[1,16,3]{2,0,1:T(1,128)}), s32[1,16,3]{2,0,1:T(1,128)S(1)}, u32[]{:S(2)}, u32[]{:S(2)}) async-start(s32[1,16,3]{2,0,1:T(1,128)} %bitcast.11), calls=%async_computation | async-start | bytes 16384 | tf_op jit(solution)/shard_map/all_to_all | solution.py:85
  11.0 24.8 %gather_fusion.11 = bf16[48,128,3,128]{3,0,2,1:T(8,128)(2,1)} fusion(bf16[128,40,3,128]{3,1,2,0:T(8,128)(2,1)} %param.17, s32[1024]{0:T(1024)S(1)} %pad_clamp_fusion.7), kind=kCustom, calls=%fused_computation.11 | custom fusion | bytes 9437376 | tf_op jit(solution)/shard_map/jit(_take)/gather | solution.py:75
  35.8 7.1 %copy.48 = bf16[128,48,3,128]{0,3,2,1:T(8,128)(2,1)} copy(bf16[128,48,3,128]{3,1,2,0:T(8,128)(2,1)} %bitcast.106) | data formatting | bytes 9437184 | tf_op jit(solution)/shard_map/jit(_take)/gather | solution.py:75
  43.1 6.0 %all-to-all-start.1 = ((s32[1,16,12]{2,0,1:T(1,128)}), s32[1,16,12]{2,0,1:T(1,128)S(1)}, u32[]{:S(2)}, u32[]{:S(2)}) async-start(s32[1,16,12]{2,0,1:T(1,128)} %bitcast.15), calls=%async_computation.1 | async-start | bytes 16384 | tf_op jit(solution)/shard_map/all_to_all | solution.py:84
  49.1 10.2 %broadcast_select_fusion = bf16[128,16,1152]{0,2,1:T(8,128)(2,1)} fusion(bf16[128,16,1152]{0,2,1:T(8,128)(2,1)} %bitcast.107, pred[16,1152]{1,0:T(8,128)(4,1)S(1)} %broadcast_in_dim.134), kind=kLoop, calls=%fused_computation.104 | loop fusion | flops 2359296 | bytes 9455616 | tf_op jit(solution)/shard_map/jit(_take)/select_n | solution.py:75
  59.3 6.0 %all-to-all-start.2 = ((bf16[128,16,1152]{0,2,1:T(8,128)(2,1)}), bf16[128,16,1152]{0,2,1:T(8,128)(2,1)}, u32[]{:S(2)}, u32[]{:S(2)}) async-start(bf16[128,16,1152]{0,2,1:T(8,128)(2,1)} %broadcast_select_fusion), calls=%async_computation.2 | async-start | bytes 9437184 | tf_op jit(solution)/shard_map/all_to_all | solution.py:83
  66.3 102.8 %all-to-all-done.2 = bf16[128,16,1152]{0,2,1:T(8,128)(2,1)} async-done(((bf16[128,16,1152]{0,2,1:T(8,128)(2,1)}), bf16[128,16,1152]{0,2,1:T(8,128)(2,1)}, u32[]{:S(2)}, u32[]{:S(2)}) %all-to-all-start.2) | async-done | bytes 4718624 | tf_op jit(solution)/shard_map/all_to_all | solution.py:83
  169.1 14.7 %copy.49 = bf16[16,128,1,1152]{1,0,3,2:T(8,128)(2,1)} copy(bf16[16,128,1,1152]{1,3,0,2:T(8,128)(2,1)} %bitcast.20) | data formatting | bytes 9437184 | tf_op jit(solution)/shard_map/all_to_all | solution.py:83
  183.8 8.2 %reshape.170 = bf16[2048,3,3,128]{0,3,2,1:T(8,128)(2,1)} reshape(bf16[16,128,1,1152]{1,0,3,2:T(8,128)(2,1)} %copy.49) | data formatting | bytes 9437184 | tf_op jit(solution)/shard_map/reshape | solution.py:87
  192.0 4.1 %fusion.64 = (bf16[2048,1,1,128]{0,3,2,1:T(8,128)(2,1)S(1)}, bf16[2048,1,1,128]{0,3,2,1:T(8,128)(2,1)}, bf16[2048,1,1,128]{0,3,2,1:T(8,128)(2,1)}, bf16[2048,1,1...) fusion(bf16[2048,3,3,128]{0,3,2,1:T(8,128)(2,1)} %reshape.170), kind=kLoop, calls=%fused_computation.151 | loop fusion | bytes 9437184 | tf_op jit(solution)/shard_map/slice | solution.py:94
  197.4 3.6 %while.66 = (s32[]{:T(128)}, f32[16,128]{1,0:T(8,128)S(1)}, s32[]{:T(128)}, s32[16]{0:T(128)S(1)}, s32[16,4]{0,1:T(4,128)S(1)}, /*index=5*/bf16[16,128,128]{2,1,...) while((s32[]{:T(128)}, f32[16,128]{1,0:T(8,128)S(1)}, s32[]{:T(128)}, ...), condition=%wide.region_4.6_spmd, body=%wide.region_2.5_spmd.sunk | while | flops 67898480 | bytes 2134543 | solution.py:31
  198.7 1.6 fusion.97
  201.4 4.7 %while.67 = (s32[]{:T(128)}, f32[16,128]{1,0:T(8,128)S(1)}, f32[16,128,128]{2,1,0:T(8,128)S(1)}, s32[]{:T(128)}, s32[16]{0:T(128)S(1)}, /*index=5*/s32[16,4]{0,1...) while((s32[]{:T(128)}, f32[16,128]{1,0:T(8,128)S(1)}, ...), condition=%wide.region_7.9_spmd, body=%wide.region_5.8_spmd.sunk | while | flops 136316016 | bytes 6861431 | solution.py:53
  202.8 1.6 fusion.101
  208.2 8.5 %while.68 = (s32[]{:T(128)}, f32[16,128]{1,0:T(8,128)S(1)}, s32[]{:T(128)}, s32[16]{0:T(128)S(1)}, s32[16,4]{0,1:T(4,128)S(1)}, /*index=5*/bf16[16,128,128]{2,1,...) while((s32[]{:T(128)}, f32[16,128]{1,0:T(8,128)S(1)}, s32[]{:T(128)}, ...), condition=%wide.region_11.13_spmd, body=%wide.region_9.12_spmd.sunk | while | flops 67898480 | bytes 2134543 | solution.py:31
  217.9 17.3 %while.69 = (s32[]{:T(128)}, f32[16,128]{1,0:T(8,128)S(1)}, f32[16,128,128]{2,1,0:T(8,128)S(1)}, s32[]{:T(128)}, s32[16]{0:T(128)S(1)}, /*index=5*/s32[16,4]{0,1...) while((s32[]{:T(128)}, f32[16,128]{1,0:T(8,128)S(1)}, ...), condition=%wide.region_14.16_spmd, body=%wide.region_12.15_spmd.sunk | while | flops 136316016 | bytes 6861431 | solution.py:53
  219.5 1.6 fusion.108
  223.6 1.6 fusion.108
  227.7 1.6 fusion.108
  231.8 1.6 fusion.108
  235.6 1.0 copy.78
  237.2 2.7 while.70
  241.2 4.8 %while.71 = (s32[]{:T(128)}, f32[16,128]{1,0:T(8,128)S(1)}, f32[16,128,128]{2,1,0:T(8,128)S(1)}, s32[]{:T(128)}, s32[16]{0:T(128)S(1)}, /*index=5*/s32[16,4]{0,1...) while((s32[]{:T(128)}, f32[16,128]{1,0:T(8,128)S(1)}, ...), condition=%wide.region_21.23_spmd, body=%wide.region_19.22_spmd.sunk | while | flops 136316016 | bytes 6861431 | solution.py:53
  242.6 1.6 fusion.115
  247.9 1.9 reduce.6
  250.7 1.4 reshape.323
  252.0 35.3 %all-to-all-start.3 = ((bf16[16,2,24576]{2,1,0:T(2,128)(2,1)}), bf16[16,2,24576]{2,1,0:T(2,128)(2,1)}, u32[]{:S(2)}, u32[]{:S(2)}) async-start(bf16[16,2,24576]{2,1,0:T(2,128)(2,1)} %reshape.323), calls=%async_computation.3 | async-start | bytes 3145728 | tf_op jit(solution)/shard_map/all_to_all | solution.py:99
  287.4 36.3 %all-to-all-done.3 = bf16[16,2,24576]{2,1,0:T(2,128)(2,1)} async-done(((bf16[16,2,24576]{2,1,0:T(2,128)(2,1)}), bf16[16,2,24576]{2,1,0:T(2,128)(2,1)}, u32[]{:S(2)}, u32[]{:S(2)}) %all-to-all-start.3) | async-done | bytes 1572896 | tf_op jit(solution)/shard_map/all_to_all | solution.py:99
  323.7 8.1 %reshape.324 = bf16[2048,1,384]{2,1,0:T(2,128)(2,1)S(1)} reshape(bf16[16,2,24576]{2,1,0:T(2,128)(2,1)} %all-to-all-done.3) | data formatting | bytes 3145728
  331.8 1.4 copy.87
  333.2 1.9 copy.69
  337.0 1.9 copy.71
  (147 shorter events, 34.9 us)
Async XLA Ops:
  0.0 0.8 copy-start
  2.2 40.9 %all-to-all-start = ((s32[1,16,3]{2,0,1:T(1,128)}), s32[1,16,3]{2,0,1:T(1,128)S(1)}, u32[]{:S(2)}, u32[]{:S(2)}) async-start(s32[1,16,3]{2,0,1:T(1,128)} %bitcast.11), calls=%async_computation | async-start | bytes 16384 | tf_op jit(solution)/shard_map/all_to_all | solution.py:85
  43.1 16.2 %all-to-all-start.1 = ((s32[1,16,12]{2,0,1:T(1,128)}), s32[1,16,12]{2,0,1:T(1,128)S(1)}, u32[]{:S(2)}, u32[]{:S(2)}) async-start(s32[1,16,12]{2,0,1:T(1,128)} %bitcast.15), calls=%async_computation.1 | async-start | bytes 16384 | tf_op jit(solution)/shard_map/all_to_all | solution.py:84
  59.3 109.7 %all-to-all-start.2 = ((bf16[128,16,1152]{0,2,1:T(8,128)(2,1)}), bf16[128,16,1152]{0,2,1:T(8,128)(2,1)}, u32[]{:S(2)}, u32[]{:S(2)}) async-start(bf16[128,16,1152]{0,2,1:T(8,128)(2,1)} %broadcast_select_fusion), calls=%async_computation.2 | async-start | bytes 9437184 | tf_op jit(solution)/shard_map/all_to_all | solution.py:83
  206.2 1.4 copy-start.7
  206.2 1.7 copy-start.6
  208.2 9.3 %copy-start.5 = (bf16[2048,1,1,128]{0,3,2,1:T(8,128)(2,1)S(1)}, bf16[2048,1,1,128]{0,3,2,1:T(8,128)(2,1)}, u32[]{:S(2)}) copy-start(bf16[2048,1,1,128]{0,3,2,1:T(8,128)(2,1)} %get-tuple-element.526) | copy-start | bytes 1572868
  216.7 0.8 copy-start.11
  235.2 1.4 copy-start.4
  235.2 1.7 copy-start.3
  237.2 3.6 %copy-start.2 = (bf16[2048,1,1,128]{0,3,2,1:T(8,128)(2,1)S(1)}, bf16[2048,1,1,128]{0,3,2,1:T(8,128)(2,1)}, u32[]{:S(2)}) copy-start(bf16[2048,1,1,128]{0,3,2,1:T(8,128)(2,1)} %get-tuple-element.523) | copy-start | bytes 1572868
  240.0 0.8 copy-start.10
  246.0 1.0 copy-start.8
  246.0 1.2 copy-start.9
  252.0 71.6 %all-to-all-start.3 = ((bf16[16,2,24576]{2,1,0:T(2,128)(2,1)}), bf16[16,2,24576]{2,1,0:T(2,128)(2,1)}, u32[]{:S(2)}, u32[]{:S(2)}) async-start(bf16[16,2,24576]{2,1,0:T(2,128)(2,1)} %reshape.323), calls=%async_computation.3 | async-start | bytes 3145728 | tf_op jit(solution)/shard_map/all_to_all | solution.py:99
  336.8 2.1 copy-start.1
where the time goes:
time: 336 us; the launch traced here: 339 us
  waiting for transfers between devices  139 us (41%)
  local copies, waits for them, and re-layouts  101 us (30%)
  starting transfers between devices  53.9 us (16%)
  matrix products  16.8 us (5%)
  other arithmetic  15.5 us (5%)
  loops' own time  12.6 us (4%)
    all_to_all x1, waiting for transfers between devices, body(): lax.all_to_all(all_send, 'seq', split_axis=1, concat_axis=0, tiled=True)  103 us
    all_to_all x1, waiting for transfers between devices, body(): lax.all_to_all(result, 'seq', split_axis=0, concat_axis=1, tiled=True)  36.3 us
    all_to_all x1, starting transfers between devices, body(): lax.all_to_all(result, 'seq', split_axis=0, concat_axis=1, tiled=True)  35.3 us
    gather x2, local copies, waits for them, and re-layouts, body(): jnp.take(qkv, chosen, axis=1)  31.9 us
    unnamed x29, local copies, waits for them, and re-layouts  14.8 us
    all_to_all x1, local copies, waits for them, and re-layouts, body(): lax.all_to_all(all_send, 'seq', split_axis=1, concat_axis=0, tiled=True)  14.7 us
    dot_general x12, matrix products, scores_at(): jnp.einsum('qid,qjd->qij', query_rows, picked, preferred_element_type=jnp...  13.9 us
    select_n x1, other arithmetic, body(): jnp.take(qkv, chosen, axis=1)  10.2 us
  transfers between devices with their start and end apart: 4, of which 2 were waited for; matrix products, arithmetic and copies ran while one was open for 13% of the time, Pallas kernels for 0%

commit v1 on v0

v1 whole, which is shorter than its diff:
```python
import functools
import math

import jax
import jax.numpy as jnp
from jax import lax
from jax.experimental import pallas as pl
from jax.experimental.pallas import tpu as pltpu
from jax.sharding import PartitionSpec as P

F32, BF16 = jnp.float32, jnp.bfloat16
DEAD = -1e30
VMEM_BYTES = 48 << 20


def params(cost=None):
    return pltpu.CompilerParams(vmem_limit_bytes=VMEM_BYTES)


def slots(heads, per_chip, chips):
    even = per_chip // 2
    whole, shared = [], []
    for head in range(heads):
        chip, inner = divmod(head, per_chip)
        if inner < 2 * even:
            whole.append((head, 2 * chip + inner // even, inner % even))
        else:
            shared.append((head, 2 * chip))
    return whole, shared


def pack_kernel(whole, shared, even, x_ref, out_ref, wide):
    rows, _, heads, dim = x_ref.shape

    def widen(t, carry):
        wide[pl.ds(pl.multiple_of(t * heads, 8), heads), :] = x_ref[t, 0].astype(F32)
        return carry

    lax.fori_loop(0, rows, widen, 0, unroll=8)
    half = rows // 2
    for head, device, slot in whole:
        out_ref[device, 0, slot * rows : (slot + 1) * rows, :] = wide[
            pl.ds(head, rows, stride=heads), :
        ].astype(BF16)
    for head, device in shared:
        for core in range(2):
            out_ref[device + core, 0, even * rows : even * rows + half, :] = wide[
                pl.ds(core * half * heads + head, half, stride=heads), :
            ].astype(BF16)


def unpack_kernel(whole, shared, even, x_ref, out_ref, wide):
    rows, heads, dim = out_ref.shape
    half = rows // 2
    for head, device, slot in whole:
        wide[pl.ds(head, rows, stride=heads), :] = x_ref[
            device, slot * rows : (slot + 1) * rows, :
        ].astype(F32)
    for head, device in shared:
        for core in range(2):
            wide[pl.ds(core * half * heads + head, half, stride=heads), :] = x_ref[
                device + core, even * rows : even * rows + half, :
            ].astype(F32)

    def narrow(t, carry):
        out_ref[t] = wide[pl.ds(pl.multiple_of(t * heads, 8), heads), :].astype(BF16)
        return carry

    lax.fori_loop(0, rows, narrow, 0, unroll=8)


def attend_block(queries, keys, values, count, scale):
    picked = jnp.concatenate(keys, axis=0)
    scores = lax.dot_general(
        queries, picked, (((1,), (1,)), ((), ())), preferred_element_type=F32
    )
    width = keys[0].shape[0]
    parts = []
    for j in range(len(keys)):
        part = scores[:, j * width : (j + 1) * width] * scale
        if j:
            part = part + jnp.where(j < count, 0.0, DEAD).astype(F32)
        parts.append(part)
    peak = functools.reduce(jnp.maximum, parts)
    peak = jnp.max(peak, axis=1, keepdims=True)
    weights = [jnp.exp2(part - peak) for part in parts]
    total = jnp.sum(functools.reduce(jnp.add, weights), axis=1, keepdims=True)
    rounded = jnp.concatenate([w.astype(BF16) for w in weights], axis=1)
    mixed = jnp.dot(rounded, jnp.concatenate(values, axis=0), preferred_element_type=F32)
    return (mixed / total).astype(BF16)


def whole_kernel(lists, heads, scale, info_ref, owned_ref, x_ref, out_ref):
    blocks = x_ref.shape[0]
    head = owned_ref[pl.program_id(0)]

    def one(b, carry):
        base = (b * heads + head) * (lists + 1)
        ids = [info_ref[base + j] for j in range(lists)]
        out_ref[b] = attend_block(
            x_ref[b, 0],
            [x_ref[c, 1] for c in ids],
            [x_ref[c, 2] for c in ids],
            info_ref[base + lists],
            scale,
        )
        return carry

    lax.fori_loop(0, blocks, one, 0, unroll=2)


def shared_kernel(lists, heads, scale, info_ref, owned_ref, x_ref, far_ref, held_ref, out_ref):
    blocks = x_ref.shape[0]
    head = owned_ref[0]

    def one(b, carry):
        base = (b * heads + head) * (lists + 1)
        ids = [info_ref[base + j] for j in range(lists)]
        keys, values = [], []
        for c in ids:
            keys.append(jnp.concatenate([x_ref[c, 1], far_ref[c, 0]], axis=0))
            values.append(jnp.concatenate([x_ref[c, 2], far_ref[c, 1]], axis=0))
        out_ref[b] = attend_block(x_ref[b, 0], keys, values, info_ref[base + lists], scale)
        return carry

    lax.fori_loop(0, blocks, one, 0, unroll=2)


def body(seq, qkv, block_ids, counts):
    rows, heads, _, dim = qkv.shape
    lists = block_ids.shape[2]
    chips = seq // 2
    per_chip = -(-heads // chips)
    even, odd = divmod(per_chip, 2)
    half = rows // 2
    depth = even * rows + odd * half
    whole, shared = slots(heads, per_chip, chips)
    scale = math.log2(math.e) / math.sqrt(dim)

    info = jnp.concatenate([block_ids, counts[:, :, None]], axis=2).reshape(1, -1)
    info = lax.all_gather(info, "seq", axis=0, tiled=True).reshape(-1)

    by_kind = jnp.transpose(qkv, (0, 2, 1, 3))
    sent = pl.pallas_call(
        functools.partial(pack_kernel, whole, shared, even),
        grid=(3,),
        in_specs=[pl.BlockSpec((rows, 1, heads, dim), lambda s: (0, s, 0, 0))],
        out_specs=pl.BlockSpec((seq, 1, depth, dim), lambda s: (0, s, 0, 0)),
        out_shape=jax.ShapeDtypeStruct((seq, 3, depth, dim), BF16),
        scratch_shapes=[pltpu.VMEM((rows * heads, dim), F32)],
        compiler_params=params(),
        name="pack",
    )(by_kind)
    came = lax.all_to_all(sent, "seq", split_axis=0, concat_axis=0, tiled=True)

    me = lax.axis_index("seq")
    first = me // 2 * per_chip
    owned = first + me % 2 * even + jnp.arange(even, dtype=jnp.int32)
    owned = jnp.minimum(owned, heads - 1)
    result = pl.pallas_call(
        functools.partial(whole_kernel, lists, heads, scale),
        grid_spec=pltpu.PrefetchScalarGridSpec(
            num_scalar_prefetch=2,
            grid=(even,),
            in_specs=[pl.BlockSpec((seq, 3, rows, dim), lambda e, *_: (0, 0, e, 0))],
            out_specs=pl.BlockSpec((seq, rows, dim), lambda e, *_: (0, e, 0)),
        ),
        out_shape=jax.ShapeDtypeStruct((seq, depth, dim), BF16),
        compiler_params=params(),
        name="attend_whole",
    )(info, owned, came)
    if odd:
        mine = came[:, 1:, even * rows :, :]
        pairs = [(d, d ^ 1) for d in range(seq)]
        far = lax.ppermute(mine, "seq", pairs)
        owned = jnp.minimum(first + 2 * even, heads - 1).reshape(1)
        result = pl.pallas_call(
            functools.partial(shared_kernel, lists, heads, scale),
            grid_spec=pltpu.PrefetchScalarGridSpec(
                num_scalar_prefetch=2,
                grid=(1,),
                in_specs=[
                    pl.BlockSpec((seq, 3, half, dim), lambda e, *_: (0, 0, 2 * even, 0)),
                    pl.BlockSpec((seq, 2, half, dim), lambda e, *_: (0, 0, 0, 0)),
                    pl.BlockSpec(memory_space=pl.ANY),
                ],
                out_specs=pl.BlockSpec((seq, half, dim), lambda e, *_: (0, 2 * even, 0)),
            ),
            out_shape=jax.ShapeDtypeStruct((seq, depth, dim), BF16),
            input_output_aliases={4: 0},
            compiler_params=params(),
            name="attend_shared",
        )(info, owned, came, far, result)

    back = lax.all_to_all(result, "seq", split_axis=0, concat_axis=0, tiled=True)
    return pl.pallas_call(
        functools.partial(unpack_kernel, whole, shared, even),
        out_shape=jax.ShapeDtypeStruct((rows, heads, dim), BF16),
        scratch_shapes=[pltpu.VMEM((rows * heads, dim), F32)],
        compiler_params=params(),
        name="unpack",
    )(back)


def solution(mesh):
    in_specs = (
        P(("rep", "seq"), None, None, None),
        P(("rep", "seq"), None, None),
        P(("rep", "seq"), None),
    )
    out_specs = P(("rep", "seq"), None, None)
    return jax.shard_map(
        functools.partial(body, mesh.shape["seq"]),
        mesh=mesh,
        in_specs=in_specs,
        out_specs=out_specs,
        check_vma=False,
    )
```

time: 336 us -> 179 us (0.53)
  the two profiles are of different devices: /device:TPU:15 before, /device:TPU:0 now
where the time goes in v1:
time: 179 us; the launch traced here: 178 us
  blocking collectives  148 us (83%)
  Pallas kernels  24.5 us (14%)
  local copies, waits for them, and re-layouts  4.31 us (2%)
    all_to_all x1, blocking collectives, body(): came = lax.all_to_all(sent, 'seq', split_axis=0, concat_axis=0, tiled=True)  94.9 us
    all_to_all x1, blocking collectives, body(): lax.all_to_all(result, 'seq', split_axis=0, concat_axis=0, tiled=True)  34.1 us
    all_gather x1, blocking collectives, body(): info = lax.all_gather(info, 'seq', axis=0, tiled=True).reshape(-1)  19.5 us
    pallas_call x1, Pallas kernels, body(): pl.pallas_call(functools.partial(whole_kernel, lists, heads, scale), grid...  12.5 us
    pallas_call x1, Pallas kernels, body(): pl.pallas_call(functools.partial(shared_kernel, lists, heads, scale), gri...  5.99 us
    pallas_call x1, Pallas kernels, body(): pl.pallas_call(functools.partial(pack_kernel, whole, shared, even), grid=...  4.09 us
    unnamed x11, local copies, waits for them, and re-layouts  4.08 us
  transfers between devices with their start and end apart: 1, of which 0 were waited for; matrix products, arithmetic and copies ran while one was open for 0% of the time, Pallas kernels for 7%

profile of v1, /device:TPU:0, one launch (start us, length us, event | category | flops | bytes accessed | tf_op | source)
XLA Modules:
  0.0 178.1 jit_solution(14905667976840057802)
XLA Ops:
  0.0 4.1 %pack.1 = bf16[16,3,320,128]{3,2,1,0:T(8,128)(2,1)S(1)} custom-call(bf16[128,3,40,128]{3,2,1,0:T(8,128)(2,1)} %bitcast.3), custom_call_target="tpu_custom_call" | custom-call | tf_op jit(solution)/shard_map/pack/pallas_call | solution.py:144
  4.1 0.0 copy-start.3
  4.1 0.0 copy-start.4
  4.1 94.9 %all_to_all.10.x_ref = bf16[16,3,320,128]{3,2,1,0:T(8,128)(2,1)S(1)} all-to-all(bf16[16,3,320,128]{3,2,1,0:T(8,128)(2,1)S(1)} %pack.1), channel_id=1, replica_groups=mesh['rep'=2,'seq'=16] {'seq'}, dimensions={0} | all-to-all | bytes 7864320 | tf_op jit(solution)/shard_map/all_to_all | solution.py:154
  99.0 0.0 copy-start
  99.1 1.8 %copy-done = bf16[16,3,320,128]{3,2,1,0:T(8,128)(2,1)} copy-done((bf16[16,3,320,128]{3,2,1,0:T(8,128)(2,1)}, bf16[16,3,320,128]{3,2,1,0:T(8,128)(2,1)S(1)}, u32[]{:S(2)}) %copy-start) | copy-done | bytes 3932184
  100.9 0.8 collective-permute-start
  101.7 0.0 copy-done.3
  101.7 0.0 copy-done.4
  101.7 0.1 copy.6
  101.8 0.1 reshape.12
  101.9 19.5 %all-gather = s32[16,1,200]{2,1,0:T(1,128)S(1)} all-gather(s32[1,1,200]{2,1,0:T(1,128)S(1)} %reshape.12), channel_id=1, replica_groups=mesh['rep'=2,'seq'=16] {'seq'}, dimensions={0}, use_global_device_ids=true | all-gather | bytes 13600 | tf_op jit(solution)/shard_map/all_gather | solution.py:141
  121.4 0.1 reshape.10.info_ref
  121.5 0.0 copy-start.1
  121.5 2.1 %copy-done.1 = bf16[16,3,320,128]{3,2,1,0:T(8,128)(2,1)S(1)} copy-done((bf16[16,3,320,128]{3,2,1,0:T(8,128)(2,1)S(1)}, bf16[16,3,320,128]{3,2,1,0:T(8,128)(2,1)}, u32[]{:S(2)}) %copy-start.1) | copy-done | bytes 3932184
  123.6 0.0 copy-start.2
  123.6 12.5 %attend_whole.1.held_ref = bf16[16,320,128]{2,1,0:T(8,128)(2,1)S(1)} custom-call(s32[3200]{0:T(1024)S(1)} %reshape.10.info_ref, s32[2]{0:T(128)S(1)} %add_minimum_fusion.owned_ref, bf16[16,3,320,128]{3,2,1,0:T(8,128)(2,1)S(1)} %copy-done.1), custom_call_target="tpu_custom_call" | custom-call | tf_op jit(solution)/shard_map/attend_whole/pallas_call | solution.py:160
  136.1 0.0 collective-permute-done.far_ref
  136.1 0.0 copy-done.2
  136.1 6.0 %attend_shared.1 = bf16[16,320,128]{2,1,0:T(8,128)(2,1)S(1)} custom-call(s32[3200]{0:T(1024)S(1)} %reshape.10.info_ref, s32[1]{0:T(128)} %bitcast.1.owned_ref, bf16[16,3,320,128]{3,2,1,0:T(8,128)(2,1)S(1)} %copy-done.2, bf16[16,2,64,128]{3,2,1,0:T(8,128)(2,1)S(1)} %collective-permute-done.far_ref, ...), custom_call_target="tpu_custom_call", output_to_operand_aliasing={{}: (4, {})} | custom-call | tf_op jit(solution)/shard_map/attend_shared/pallas_call | solution.py:177
  142.1 34.1 %all_to_all.11.x_ref = bf16[16,320,128]{2,1,0:T(8,128)(2,1)S(1)} all-to-all(bf16[16,320,128]{2,1,0:T(8,128)(2,1)S(1)} %attend_shared.1), channel_id=1, replica_groups=mesh['rep'=2,'seq'=16] {'seq'}, dimensions={0} | all-to-all | bytes 2621440 | tf_op jit(solution)/shard_map/all_to_all | solution.py:195
  176.2 1.9 %unpack.1 = bf16[128,40,128]{2,1,0:T(8,128)(2,1)} custom-call(bf16[16,320,128]{2,1,0:T(8,128)(2,1)S(1)} %all_to_all.11.x_ref), custom_call_target="tpu_custom_call" | custom-call | tf_op jit(solution)/shard_map/unpack/pallas_call | solution.py:196
  (4 shorter events, 0.1 us)
Async XLA Ops:
  4.1 97.6 %copy-start.3 = (s32[1,40,4]{1,2,0:T(4,128)S(1)}, s32[1,40,4]{1,2,0:T(4,128)}, u32[]{:S(2)}) copy-start(s32[1,40,4]{1,2,0:T(4,128)} %param.4) | copy-start | bytes 1924
  4.1 97.6 %copy-start.4 = (s32[1,40]{1,0:T(1,128)S(1)}, s32[1,40]{1,0:T(1,128)}, u32[]{:S(2)}) copy-start(s32[1,40]{1,0:T(1,128)} %param.5) | copy-start | bytes 484
  99.0 1.9 %copy-start = (bf16[16,3,320,128]{3,2,1,0:T(8,128)(2,1)}, bf16[16,3,320,128]{3,2,1,0:T(8,128)(2,1)S(1)}, u32[]{:S(2)}) copy-start(bf16[16,3,320,128]{3,2,1,0:T(8,128)(2,1)S(1)} %all_to_all.10.x_ref) | copy-start | bytes 11796484
  100.9 35.2 %collective-permute-start = (bf16[16,2,64,128]{3,2,1,0:T(8,128)(2,1)S(1)}, bf16[16,2,64,128]{3,2,1,0:T(8,128)(2,1)S(1)}, u32[]{:S(2)}, u32[]{:S(2)}) collective-permute-start(bf16[16,2,64,128]{3,2,1,0:T(8,128)(2,1)S(1)} %slice.4), channel_id=1, source_target_pairs={{0,1},{1,0},{2,3},{3,2},{4,5},{5,4},{6,7},{7,6},{8,9},{9,8},{10,11... | collective-permute-start | bytes 1572872 | tf_op jit(solution)/shard_map/ppermute | solution.py:175
  121.5 2.1 %copy-start.1 = (bf16[16,3,320,128]{3,2,1,0:T(8,128)(2,1)S(1)}, bf16[16,3,320,128]{3,2,1,0:T(8,128)(2,1)}, u32[]{:S(2)}) copy-start(bf16[16,3,320,128]{3,2,1,0:T(8,128)(2,1)} %copy-done) | copy-start | bytes 11796484
  123.6 12.5 %copy-start.2 = (bf16[16,3,320,128]{3,2,1,0:T(8,128)(2,1)S(1)}, bf16[16,3,320,128]{3,2,1,0:T(8,128)(2,1)}, u32[]{:S(2)}) copy-start(bf16[16,3,320,128]{3,2,1,0:T(8,128)(2,1)} %copy-done) | copy-start | bytes 11796484

commit v2 on v0

v2 whole, which is shorter than its diff:
```python
import functools
import math

import jax
import jax.numpy as jnp
from jax import lax
from jax.experimental import pallas as pl
from jax.experimental.pallas import tpu as pltpu
from jax.sharding import PartitionSpec as P

F32, BF16, I32 = jnp.float32, jnp.bfloat16, jnp.int32
DEAD = -1e30
VMEM_BYTES = 48 << 20
INFO_ROWS = 16
GROUP = 4
WINDOW = 6
LATE = 4


def params():
    return pltpu.CompilerParams(vmem_limit_bytes=VMEM_BYTES)


def cost(flops, count):
    return pl.CostEstimate(flops=flops, bytes_accessed=count, transcendentals=0)


class Piece:
    def __init__(self, seq, heads, rows, dim, lists, blocks, first, size):
        self.seq, self.heads, self.rows, self.dim = seq, heads, rows, dim
        self.chips = seq // 2
        self.per_chip = -(-heads // self.chips)
        self.padded = self.per_chip * self.chips > heads
        self.lists, self.first, self.size = lists, first, size
        self.depth = size * rows
        self.bits = max(1, (blocks - 1).bit_length())
        assert self.chips & (self.chips - 1) == 0
        assert lists * self.bits + lists.bit_length() < 31 and lists < INFO_ROWS

    def head(self, chip, slot):
        return chip * self.per_chip + self.first + slot


def pack_kernel(piece, me_ref, x_ref, ids_ref, counts_ref, *refs):
    outs, (wide, info) = refs[: piece.chips], refs[piece.chips :]
    rows, _, heads, _ = x_ref.shape
    chip = me_ref[0] // 2

    def widen(t, carry):
        wide[pl.ds(pl.multiple_of(t * heads, 8), heads), :] = x_ref[t, 0].astype(F32)
        return carry

    lax.fori_loop(0, rows, widen, 0, unroll=8)
    info[...] = jnp.zeros_like(info)
    info[: piece.lists, :heads] = ids_ref[0].astype(F32)
    info[piece.lists : piece.lists + 1, :heads] = counts_ref[...].astype(F32)
    for step, out in enumerate(outs):
        for slot in range(piece.size):
            head = jnp.minimum(piece.head(chip ^ step, slot), heads - 1)
            out[0, slot * rows : (slot + 1) * rows, :] = wide[
                pl.ds(head, rows, stride=heads), :
            ].astype(BF16)
        out[0, piece.depth :, :] = info[...].astype(BF16)


def pack(piece, me, by_kind, block_ids, counts):
    rows, kinds, heads, dim = by_kind.shape
    depth = piece.depth + INFO_ROWS
    return pl.pallas_call(
        functools.partial(pack_kernel, piece),
        grid_spec=pltpu.PrefetchScalarGridSpec(
            num_scalar_prefetch=1,
            grid=(kinds,),
            in_specs=[
                pl.BlockSpec((rows, 1, heads, dim), lambda s, *_: (0, s, 0, 0)),
                pl.BlockSpec((1, piece.lists, heads), lambda s, *_: (0, 0, 0)),
                pl.BlockSpec((1, heads), lambda s, *_: (0, 0)),
            ],
            out_specs=[pl.BlockSpec((1, depth, dim), lambda s, *_: (s, 0, 0))] * piece.chips,
            scratch_shapes=[
                pltpu.VMEM((rows * heads, dim), F32),
                pltpu.VMEM((INFO_ROWS, dim), F32),
            ],
        ),
        out_shape=[jax.ShapeDtypeStruct((kinds, depth, dim), BF16)] * piece.chips,
        compiler_params=params(),
        cost_estimate=cost(0, 8 << 20),
        name="pack",
    )(me, by_kind, jnp.transpose(block_ids, (0, 2, 1)), counts)


def gather_kernel(piece, *refs):
    rows_refs, out_ref, sem = refs[:-2], refs[-2], refs[-1]
    copies = [
        pltpu.make_async_copy(ref.at[1:3, : piece.depth], out_ref.at[step], sem.at[step])
        for step, ref in enumerate(rows_refs)
    ]
    for copy in copies:
        copy.start()
    for copy in copies:
        copy.wait()


def gather_keys(piece, came):
    return pl.pallas_call(
        functools.partial(gather_kernel, piece),
        in_specs=[pl.BlockSpec(memory_space=pl.ANY)] * piece.chips,
        out_specs=pl.BlockSpec(memory_space=pl.ANY),
        out_shape=jax.ShapeDtypeStruct((piece.chips, 2, piece.depth, piece.dim), BF16),
        scratch_shapes=[pltpu.SemaphoreType.DMA((piece.chips,))],
        compiler_params=params(),
        cost_estimate=cost(0, 4 << 20),
        name="gather_keys",
    )(*came)


def attend_group(units, scale):
    scores = [
        lax.dot_general(q, k, (((1,), (1,)), ((), ())), preferred_element_type=F32)
        for q, k, _, _ in units
    ]
    scores = [s * scale + bias for s, (_, _, _, bias) in zip(scores, units)]
    peaks = [jnp.max(s, axis=1, keepdims=True) for s in scores]
    weights = [jnp.exp2(s - peak) for s, peak in zip(scores, peaks)]
    totals = [jnp.sum(w, axis=1, keepdims=True) for w in weights]
    mixed = [
        jnp.dot(w.astype(BF16), v, preferred_element_type=F32)
        for w, (_, _, v, _) in zip(weights, units)
    ]
    return [(m / t).astype(BF16) for m, t in zip(mixed, totals)]


def attend_kernel(piece, scale, me_ref, *refs):
    chips, rows, lists, bits = piece.chips, piece.rows, piece.lists, piece.bits
    near, far_ref, outs = refs[:chips], refs[chips], refs[chips + 1 : 2 * chips + 1]
    queries, keys, values, info, bias, code, scalars, sem = refs[2 * chips + 1 :]
    chip, core = me_ref[0] // 2, me_ref[0] % 2

    copies = []
    for step, ref in enumerate(near):
        inside = slice(0, piece.depth)
        moves = [
            (ref.at[0, piece.depth :], info.at[step]),
            (ref.at[0, inside], queries.at[step]),
            (ref.at[1, inside], keys.at[2 * step]),
            (ref.at[2, inside], values.at[2 * step]),
            (far_ref.at[step, 0], keys.at[2 * step + 1]),
            (far_ref.at[step, 1], values.at[2 * step + 1]),
        ]
        copies += [
            pltpu.make_async_copy(source, target, sem.at[step, at])
            for at, (source, target) in enumerate(moves)
        ]
    for copy in copies:
        copy.start()

    width = lists * rows
    count = lax.broadcasted_iota(I32, bias.shape, 0)
    entry = lax.broadcasted_iota(I32, bias.shape, 1) // rows
    bias[...] = jnp.where((entry < count) | (entry == 0), 0.0, DEAD).astype(F32)
    for copy in copies:
        copy.wait()

    for step in range(chips):
        row = info[step].astype(F32).astype(I32)
        total = row[:1]
        for j in range(1, lists + 1):
            total = total + (row[j : j + 1] << (j * bits))
        code[step : step + 1, :] = total
    copy = pltpu.make_async_copy(code, scalars, sem.at[0, 0])
    copy.start()
    copy.wait()

    mask = (1 << bits) - 1

    def place(block):
        return ((block // 2) ^ chip) * 2 + ((block % 2) ^ core)

    def one_slot(slot, carry):
        head = jnp.minimum(piece.head(chip, slot), piece.heads - 1)
        span = pl.ds(pl.multiple_of(slot * rows, rows), rows)
        for start in range(0, chips, GROUP):
            steps, units = range(start, min(start + GROUP, chips)), []
            for step in steps:
                number = scalars[step, head]
                places = [place((number >> (j * bits)) & mask) for j in range(lists)]
                live = number >> (lists * bits)
                units.append(
                    (
                        queries[step, span, :],
                        jnp.concatenate([keys[c, span, :] for c in places], axis=0),
                        jnp.concatenate([values[c, span, :] for c in places], axis=0),
                        bias[pl.ds(live, 1), :],
                    )
                )
            for step, result in zip(steps, attend_group(units, scale)):
                outs[step][span, :] = result
        return carry

    lax.fori_loop(0, piece.size, one_slot, 0)


def attend(piece, me, came, far, scale):
    chips, depth, dim = piece.chips, piece.depth, piece.dim
    bias_rows = -(-(piece.lists + 1) // 8) * 8
    any_spec = pl.BlockSpec(memory_space=pl.ANY)
    return pl.pallas_call(
        functools.partial(attend_kernel, piece, scale),
        in_specs=[pl.BlockSpec(memory_space=pltpu.SMEM)] + [any_spec] * (chips + 1),
        out_specs=[pl.BlockSpec(memory_space=pltpu.VMEM)] * chips,
        out_shape=[jax.ShapeDtypeStruct((depth, dim), BF16)] * chips,
        scratch_shapes=[
            pltpu.VMEM((chips, depth, dim), BF16),
            pltpu.VMEM((2 * chips, depth, dim), BF16),
            pltpu.VMEM((2 * chips, depth, dim), BF16),
            pltpu.VMEM((chips, INFO_ROWS, dim), BF16),
            pltpu.VMEM((bias_rows, piece.lists * piece.rows), F32),
            pltpu.VMEM((chips, dim), I32),
            pltpu.SMEM((chips, dim), I32),
            pltpu.SemaphoreType.DMA((chips, 6)),
        ],
        compiler_params=params(),
        cost_estimate=cost(4 << 30, 8 << 20),
        name="attend",
    )(me, *came, far)


def unpack_kernel(pieces, me_ref, *refs):
    backs, (out_ref, wide) = refs[:-2], refs[-2:]
    rows, heads, _ = out_ref.shape
    chip, at = me_ref[0] // 2, 0
    for piece in pieces:
        for step in range(piece.chips):
            for slot in range(piece.size):
                head = piece.head(chip ^ step, slot)

                def spread(ref=backs[at], head=head, slot=slot):
                    wide[pl.ds(head, rows, stride=heads), :] = ref[
                        slot * rows : (slot + 1) * rows, :
                    ].astype(F32)

                if piece.padded:
                    pl.when(head < heads)(spread)
                else:
                    spread()
            at += 1

    def narrow(t, carry):
        out_ref[t] = wide[pl.ds(pl.multiple_of(t * heads, 8), heads), :].astype(BF16)
        return carry

    lax.fori_loop(0, rows, narrow, 0, unroll=8)


def unpack(pieces, me, backs):
    first = pieces[0]
    rows, heads, dim = first.rows, first.heads, first.dim
    flat = [back for group in backs for back in group]
    return pl.pallas_call(
        functools.partial(unpack_kernel, pieces),
        in_specs=[pl.BlockSpec(memory_space=pltpu.SMEM)]
        + [pl.BlockSpec(memory_space=pltpu.VMEM)] * len(flat),
        out_specs=pl.BlockSpec(memory_space=pltpu.VMEM),
        out_shape=jax.ShapeDtypeStruct((rows, heads, dim), BF16),
        scratch_shapes=[pltpu.VMEM((rows * heads, dim), F32)],
        compiler_params=params(),
        cost_estimate=cost(0, 4 << 20),
        name="unpack",
    )(me, *flat)


def order_of(chips):
    far = list(range(chips // 2, chips))
    near = list(range(1, chips // 2))
    mixed = [step for pair in zip(far, near) for step in pair]
    return mixed + far[len(near) :]


class Sender:
    def __init__(self, seq):
        self.seq, self.ended = seq, []

    def exchange(self, arrays, after=None, late=None):
        got = list(arrays)
        for at, m in enumerate(order_of(self.seq // 2)):
            a = arrays[m]
            if after is not None and at == late:
                a, _ = lax.optimization_barrier((a, after))
            if len(self.ended) >= WINDOW:
                a, _ = lax.optimization_barrier((a, self.ended[-WINDOW]))
            got[m] = lax.ppermute(a, "seq", [(d, d ^ (2 * m)) for d in range(self.seq)])
            self.ended.append(got[m])
        return got


def body(seq, qkv, block_ids, counts):
    rows, heads, _, dim = qkv.shape
    per_chip = -(-heads // (seq // 2))
    make = functools.partial(
        Piece, seq, heads, rows, dim, block_ids.shape[2], seq * block_ids.shape[0]
    )
    cut = -(-per_chip * 3 // 5)
    pieces = [make(0, cut)] + ([make(cut, per_chip - cut)] if cut < per_chip else [])
    scale = math.log2(math.e) / math.sqrt(dim)
    me = lax.axis_index("seq").astype(I32).reshape(1)
    by_kind = jnp.transpose(qkv, (0, 2, 1, 3))

    packed = [pack(piece, me, by_kind, block_ids, counts) for piece in pieces]
    sender, outs, backs, after = Sender(seq), [], [], packed[-1][0]
    for piece, rows_of in zip(pieces, packed):
        rows_of = sender.exchange(rows_of, after, WINDOW)
        mine = gather_keys(piece, rows_of)
        far = lax.ppermute(mine, "seq", [(d, d ^ 1) for d in range(seq)])
        outs.append(attend(piece, me, rows_of, far, scale))
        after = outs[-1][0]
    backs = [sender.exchange(out, outs[-1][0], LATE) for out in outs]
    return unpack(pieces, me, backs)


def solution(mesh):
    in_specs = (
        P(("rep", "seq"), None, None, None),
        P(("rep", "seq"), None, None),
        P(("rep", "seq"), None),
    )
    out_specs = P(("rep", "seq"), None, None)
    return jax.shard_map(
        functools.partial(body, mesh.shape["seq"]),
        mesh=mesh,
        in_specs=in_specs,
        out_specs=out_specs,
        check_vma=False,
    )
```

time: 336 us -> 148 us (0.44)
  the two profiles are of different devices: /device:TPU:15 before, /device:TPU:0 now
where the time goes in v2:
time: 148 us
  starting transfers between devices  61.3 us (41%)
  waiting for transfers between devices  59.3 us (40%)
  Pallas kernels  25.6 us (17%)
    ppermute x28, starting transfers between devices, exchange(): got[m] = lax.ppermute(a, 'seq', [(d, d ^ 2 * m) for d in range(self.seq)])  61.2 us
    ppermute x28, waiting for transfers between devices, exchange(): got[m] = lax.ppermute(a, 'seq', [(d, d ^ 2 * m) for d in range(self.seq)])  59.3 us
    pallas_call x2, Pallas kernels, attend(): pl.pallas_call(functools.partial(attend_kernel, piece, scale), in_specs=[...  15.9 us
    pallas_call x2, Pallas kernels, pack(): pl.pallas_call(functools.partial(pack_kernel, piece), grid_spec=pltpu.Pre...  6.01 us
  transfers between devices with their start and end apart: 30, of which 12 were waited for; matrix products, arithmetic and copies ran while one was open for 0% of the time, Pallas kernels for 12%

profile of v2, /device:TPU:0, one launch (start us, length us, event | category | flops | bytes accessed | tf_op | source)
XLA Modules:
  0.0 147.7 jit_solution(14069638218228152891)
XLA Ops:
  1.3 4.1 %pack.2 = (bf16[3,400,128]{2,1,0:T(8,128)(2,1)S(1)}, bf16[3,400,128]{2,1,0:T(8,128)(2,1)S(1)}, bf16[3,400,128]{2,1,0:T(8,128)(2,1)S(1)}, bf16[3,400,128]{2,1,0:T...) custom-call(s32[1]{0:T(128)} %bitcast.me_ref, ...), custom_call_target="tpu_custom_call" | custom-call | bytes 8388608 | tf_op jit(solution)/shard_map/pack/pallas_call | solution.py:69
  5.5 4.1 %collective-permute-start.3 = (bf16[3,400,128]{2,1,0:T(8,128)(2,1)S(1)}, bf16[3,400,128]{2,1,0:T(8,128)(2,1)S(1)}, u32[]{:S(2)}, u32[]{:S(2)}) collective-permute-start(bf16[3,400,128]{2,1,0:T(8,128)(2,1)S(1)} %get-tuple-element.67), channel_id=1, source_target_pairs={{0,8},{1,9},{2,10},{3,11},{4,12},{5,13},{6,14},{7,15},{8,0},{9,1},... | collective-permute-start | bytes 921608 | tf_op jit(solution)/shard_map/ppermute | solution.py:291
  9.6 1.5 %collective-permute-start = (bf16[3,400,128]{2,1,0:T(8,128)(2,1)S(1)}, bf16[3,400,128]{2,1,0:T(8,128)(2,1)S(1)}, u32[]{:S(2)}, u32[]{:S(2)}) collective-permute-start(bf16[3,400,128]{2,1,0:T(8,128)(2,1)S(1)} %get-tuple-element.64), channel_id=1, source_target_pairs={{0,2},{1,3},{2,0},{3,1},{4,6},{5,7},{6,4},{7,5},{8,10},{9,11},{10,... | collective-permute-start | bytes 921608 | tf_op jit(solution)/shard_map/ppermute | solution.py:291
  11.1 1.6 %collective-permute-start.1 = (bf16[3,400,128]{2,1,0:T(8,128)(2,1)S(1)}, bf16[3,400,128]{2,1,0:T(8,128)(2,1)S(1)}, u32[]{:S(2)}, u32[]{:S(2)}) collective-permute-start(bf16[3,400,128]{2,1,0:T(8,128)(2,1)S(1)} %get-tuple-element.65), channel_id=1, source_target_pairs={{0,4},{1,5},{2,6},{3,7},{4,0},{5,1},{6,2},{7,3},{8,12},{9,13},{10,... | collective-permute-start | bytes 921608 | tf_op jit(solution)/shard_map/ppermute | solution.py:291
  13.0 1.3 collective-permute-start.4
  14.3 1.9 %pack.3 = (bf16[3,272,128]{2,1,0:T(8,128)(2,1)S(1)}, bf16[3,272,128]{2,1,0:T(8,128)(2,1)S(1)}, bf16[3,272,128]{2,1,0:T(8,128)(2,1)S(1)}, bf16[3,272,128]{2,1,0:T...) custom-call(s32[1]{0:T(128)} %bitcast.me_ref, ...), custom_call_target="tpu_custom_call" | custom-call | bytes 8388608 | tf_op jit(solution)/shard_map/pack/pallas_call | solution.py:69
  16.3 8.1 %collective-permute-done.3.refs_4_ = bf16[3,400,128]{2,1,0:T(8,128)(2,1)S(1)} collective-permute-done((bf16[3,400,128]{2,1,0:T(8,128)(2,1)S(1)}, bf16[3,400,128]{2,1,0:T(8,128)(2,1)S(1)}, u32[]{:S(2)}, u32[]{:S(2)}) %collective-permute-start.3) | collective-permute-done | bytes 307232 | tf_op jit(solution)/shard_map/ppermute | solution.py:291
  24.3 2.8 %collective-permute-start.5 = (bf16[3,400,128]{2,1,0:T(8,128)(2,1)S(1)}, bf16[3,400,128]{2,1,0:T(8,128)(2,1)S(1)}, u32[]{:S(2)}, u32[]{:S(2)}) collective-permute-start(bf16[3,400,128]{2,1,0:T(8,128)(2,1)S(1)} %get-tuple-element.69), channel_id=1, source_target_pairs={{0,12},{1,13},{2,14},{3,15},{4,8},{5,9},{6,10},{7,11},{8,4},{9,5},... | collective-permute-start | bytes 921608 | tf_op jit(solution)/shard_map/ppermute | solution.py:291
  27.1 2.3 %collective-permute-start.6 = (bf16[3,400,128]{2,1,0:T(8,128)(2,1)S(1)}, bf16[3,400,128]{2,1,0:T(8,128)(2,1)S(1)}, u32[]{:S(2)}, u32[]{:S(2)}) collective-permute-start(bf16[3,400,128]{2,1,0:T(8,128)(2,1)S(1)} %get-tuple-element.73), channel_id=1, source_target_pairs={{0,14},{1,15},{2,12},{3,13},{4,10},{5,11},{6,8},{7,9},{8,6},{9,7},... | collective-permute-start | bytes 921608 | tf_op jit(solution)/shard_map/ppermute | solution.py:291
  29.5 3.8 %collective-permute-done.1.refs_2_ = bf16[3,400,128]{2,1,0:T(8,128)(2,1)S(1)} collective-permute-done((bf16[3,400,128]{2,1,0:T(8,128)(2,1)S(1)}, bf16[3,400,128]{2,1,0:T(8,128)(2,1)S(1)}, u32[]{:S(2)}, u32[]{:S(2)}) %collective-permute-start.1) | collective-permute-done | bytes 307232 | tf_op jit(solution)/shard_map/ppermute | solution.py:291
  33.3 5.3 %collective-permute-done.2.refs_3_ = bf16[3,400,128]{2,1,0:T(8,128)(2,1)S(1)} collective-permute-done((bf16[3,400,128]{2,1,0:T(8,128)(2,1)S(1)}, bf16[3,400,128]{2,1,0:T(8,128)(2,1)S(1)}, u32[]{:S(2)}, u32[]{:S(2)}) %collective-permute-start.2) | collective-permute-done | bytes 307232 | tf_op jit(solution)/shard_map/ppermute | solution.py:291
  38.6 13.4 %collective-permute-done.4.refs_5_ = bf16[3,400,128]{2,1,0:T(8,128)(2,1)S(1)} collective-permute-done((bf16[3,400,128]{2,1,0:T(8,128)(2,1)S(1)}, bf16[3,400,128]{2,1,0:T(8,128)(2,1)S(1)}, u32[]{:S(2)}, u32[]{:S(2)}) %collective-permute-start.4) | collective-permute-done | bytes 307232 | tf_op jit(solution)/shard_map/ppermute | solution.py:291
  53.1 14.7 %collective-permute-start.12 = (bf16[3,272,128]{2,1,0:T(8,128)(2,1)S(1)}, bf16[3,272,128]{2,1,0:T(8,128)(2,1)S(1)}, u32[]{:S(2)}, u32[]{:S(2)}) collective-permute-start(bf16[3,272,128]{2,1,0:T(8,128)(2,1)S(1)} %get-tuple-element.87), channel_id=1, source_target_pairs={{0,8},{1,9},{2,10},{3,11},{4,12},{5,13},{6,14},{7,15},{8,0},{9,1},... | collective-permute-start | bytes 626696 | tf_op jit(solution)/shard_map/ppermute | solution.py:291
  68.3 1.4 collective-permute-start.15
  69.7 3.1 %collective-permute-start.17 = (bf16[3,272,128]{2,1,0:T(8,128)(2,1)S(1)}, bf16[3,272,128]{2,1,0:T(8,128)(2,1)S(1)}, u32[]{:S(2)}, u32[]{:S(2)}) collective-permute-start(bf16[3,272,128]{2,1,0:T(8,128)(2,1)S(1)} %get-tuple-element.96), channel_id=1, source_target_pairs={{0,4},{1,5},{2,6},{3,7},{4,0},{5,1},{6,2},{7,3},{8,12},{9,13},{10,... | collective-permute-start | bytes 626696 | tf_op jit(solution)/shard_map/ppermute | solution.py:291
  72.7 9.3 %attend.2 = (bf16[384,128]{1,0:T(8,128)(2,1)S(1)}, bf16[384,128]{1,0:T(8,128)(2,1)S(1)}, bf16[384,128]{1,0:T(8,128)(2,1)S(1)}, bf16[384,128]{1,0:T(8,128)(2,1)S(...) custom-call(s32[1]{0:T(128)} %bitcast.me_ref, ...), custom_call_target="tpu_custom_call" | custom-call | flops 4294967296 | bytes 8388608 | tf_op jit(solution)/shard_map/attend/pallas_call | solution.py:207
  82.0 5.1 %collective-permute-done.12.refs_4_ = bf16[3,272,128]{2,1,0:T(8,128)(2,1)S(1)} collective-permute-done((bf16[3,272,128]{2,1,0:T(8,128)(2,1)S(1)}, bf16[3,272,128]{2,1,0:T(8,128)(2,1)S(1)}, u32[]{:S(2)}, u32[]{:S(2)}) %collective-permute-start.12) | collective-permute-done | bytes 208928 | tf_op jit(solution)/shard_map/ppermute | solution.py:291
  87.1 4.5 %collective-permute-done.8.refs_5_ = bf16[3,272,128]{2,1,0:T(8,128)(2,1)S(1)} collective-permute-done((bf16[3,272,128]{2,1,0:T(8,128)(2,1)S(1)}, bf16[3,272,128]{2,1,0:T(8,128)(2,1)S(1)}, u32[]{:S(2)}, u32[]{:S(2)}) %collective-permute-start.8) | collective-permute-done | bytes 208928 | tf_op jit(solution)/shard_map/ppermute | solution.py:291
  91.6 1.3 collective-permute-start.13
  93.0 2.9 %collective-permute-done.19.refs_3_ = bf16[3,272,128]{2,1,0:T(8,128)(2,1)S(1)} collective-permute-done((bf16[3,272,128]{2,1,0:T(8,128)(2,1)S(1)}, bf16[3,272,128]{2,1,0:T(8,128)(2,1)S(1)}, u32[]{:S(2)}, u32[]{:S(2)}) %collective-permute-start.19) | collective-permute-done | bytes 208928 | tf_op jit(solution)/shard_map/ppermute | solution.py:291
  95.9 5.3 %collective-permute-done.13.refs_7_ = bf16[3,272,128]{2,1,0:T(8,128)(2,1)S(1)} collective-permute-done((bf16[3,272,128]{2,1,0:T(8,128)(2,1)S(1)}, bf16[3,272,128]{2,1,0:T(8,128)(2,1)S(1)}, u32[]{:S(2)}, u32[]{:S(2)}) %collective-permute-start.13) | collective-permute-done | bytes 208928 | tf_op jit(solution)/shard_map/ppermute | solution.py:291
  101.9 3.4 %collective-permute-start.16 = (bf16[384,128]{1,0:T(8,128)(2,1)S(1)}, bf16[384,128]{1,0:T(8,128)(2,1)S(1)}, u32[]{:S(2)}, u32[]{:S(2)}) collective-permute-start(bf16[384,128]{1,0:T(8,128)(2,1)S(1)} %get-tuple-element.93), channel_id=1, source_target_pairs={{0,8},{1,9},{2,10},{3,11},{4,12},{5,13},{6,14},{7,15},{8,0},{9,1},... | collective-permute-start | bytes 294920 | tf_op jit(solution)/shard_map/ppermute | solution.py:291
  106.2 4.0 %collective-permute-start.11 = (bf16[384,128]{1,0:T(8,128)(2,1)S(1)}, bf16[384,128]{1,0:T(8,128)(2,1)S(1)}, u32[]{:S(2)}, u32[]{:S(2)}) collective-permute-start(bf16[384,128]{1,0:T(8,128)(2,1)S(1)} %get-tuple-element.82), channel_id=1, source_target_pairs={{0,4},{1,5},{2,6},{3,7},{4,0},{5,1},{6,2},{7,3},{8,12},{9,13},{10,... | collective-permute-start | bytes 294920 | tf_op jit(solution)/shard_map/ppermute | solution.py:291
  110.7 6.7 %collective-permute-start.22 = (bf16[384,128]{1,0:T(8,128)(2,1)S(1)}, bf16[384,128]{1,0:T(8,128)(2,1)S(1)}, u32[]{:S(2)}, u32[]{:S(2)}) collective-permute-start(bf16[384,128]{1,0:T(8,128)(2,1)S(1)} %get-tuple-element.105), channel_id=1, source_target_pairs={{0,14},{1,15},{2,12},{3,13},{4,10},{5,11},{6,8},{7,9},{8,6},{9,7},... | collective-permute-start | bytes 294920 | tf_op jit(solution)/shard_map/ppermute | solution.py:291
  117.4 6.6 %attend.3 = (bf16[256,128]{1,0:T(8,128)(2,1)S(1)}, bf16[256,128]{1,0:T(8,128)(2,1)S(1)}, bf16[256,128]{1,0:T(8,128)(2,1)S(1)}, bf16[256,128]{1,0:T(8,128)(2,1)S(...) custom-call(s32[1]{0:T(128)} %bitcast.me_ref, ...), custom_call_target="tpu_custom_call" | custom-call | flops 4294967296 | bytes 8388608 | tf_op jit(solution)/shard_map/attend/pallas_call | solution.py:207
  124.1 3.4 %collective-permute-start.26 = (bf16[256,128]{1,0:T(8,128)(2,1)S(1)}, bf16[256,128]{1,0:T(8,128)(2,1)S(1)}, u32[]{:S(2)}, u32[]{:S(2)}) collective-permute-start(bf16[256,128]{1,0:T(8,128)(2,1)S(1)} %get-tuple-element.113), channel_id=1, source_target_pairs={{0,8},{1,9},{2,10},{3,11},{4,12},{5,13},{6,14},{7,15},{8,0},{9,1},... | collective-permute-start | bytes 196616 | tf_op jit(solution)/shard_map/ppermute | solution.py:291
  128.5 1.4 collective-permute-start.27
  129.9 2.9 %collective-permute-start.25 = (bf16[256,128]{1,0:T(8,128)(2,1)S(1)}, bf16[256,128]{1,0:T(8,128)(2,1)S(1)}, u32[]{:S(2)}, u32[]{:S(2)}) collective-permute-start(bf16[256,128]{1,0:T(8,128)(2,1)S(1)} %get-tuple-element.111), channel_id=1, source_target_pairs={{0,6},{1,7},{2,4},{3,5},{4,2},{5,3},{6,0},{7,1},{8,14},{9,15},{10,... | collective-permute-start | bytes 196616 | tf_op jit(solution)/shard_map/ppermute | solution.py:291
  132.8 5.1 %collective-permute-done.26.refs_12_ = bf16[256,128]{1,0:T(8,128)(2,1)S(1)} collective-permute-done((bf16[256,128]{1,0:T(8,128)(2,1)S(1)}, bf16[256,128]{1,0:T(8,128)(2,1)S(1)}, u32[]{:S(2)}, u32[]{:S(2)}) %collective-permute-start.26) | collective-permute-done | bytes 65568 | tf_op jit(solution)/shard_map/ppermute | solution.py:291
  140.9 1.3 collective-permute-done.23.refs_9_
  142.2 3.5 %collective-permute-done.29.refs_15_ = bf16[256,128]{1,0:T(8,128)(2,1)S(1)} collective-permute-done((bf16[256,128]{1,0:T(8,128)(2,1)S(1)}, bf16[256,128]{1,0:T(8,128)(2,1)S(1)}, u32[]{:S(2)}, u32[]{:S(2)}) %collective-permute-start.29) | collective-permute-done | bytes 65568 | tf_op jit(solution)/shard_map/ppermute | solution.py:291
  145.8 1.9 %unpack.1 = bf16[128,40,128]{2,1,0:T(8,128)(2,1)} custom-call(s32[1]{0:T(128)} %bitcast.me_ref, bf16[384,128]{1,0:T(8,128)(2,1)S(1)} %get-tuple-element.74.refs_0_, bf16[384,128]{1,0:T(8,128)(2,1)S(1)} %collective-permute-done.9.refs_1_, bf16[384,128]{1,0:T(8,128)(2,1)S(1)} %collective-permute-done.11.refs_2_, ...), custom_call_target="tpu_custom_call" | custom-call | bytes 4194304 | tf_op jit(solution)/shard_map/unpack/pallas_call | solution.py:259
  (45 shorter events, 9.7 us)
Async XLA Ops:
  1.3 13.0 %copy-start.2 = (s32[1,40,4]{1,2,0:T(4,128)S(1)}, s32[1,40,4]{1,2,0:T(4,128)}, u32[]{:S(2)}) copy-start(s32[1,40,4]{1,2,0:T(4,128)} %param.4) | copy-start | bytes 1924
  1.3 13.0 %copy-start.4 = (s32[1,40]{1,0:T(1,128)S(1)}, s32[1,40]{1,0:T(1,128)}, u32[]{:S(2)}) copy-start(s32[1,40]{1,0:T(1,128)} %counts_ref.3) | copy-start | bytes 484
  5.5 18.9 %collective-permute-start.3 = (bf16[3,400,128]{2,1,0:T(8,128)(2,1)S(1)}, bf16[3,400,128]{2,1,0:T(8,128)(2,1)S(1)}, u32[]{:S(2)}, u32[]{:S(2)}) collective-permute-start(bf16[3,400,128]{2,1,0:T(8,128)(2,1)S(1)} %get-tuple-element.67), channel_id=1, source_target_pairs={{0,8},{1,9},{2,10},{3,11},{4,12},{5,13},{6,14},{7,15},{8,0},{9,1},... | collective-permute-start | bytes 921608 | tf_op jit(solution)/shard_map/ppermute | solution.py:291
  9.6 17.6 %collective-permute-start = (bf16[3,400,128]{2,1,0:T(8,128)(2,1)S(1)}, bf16[3,400,128]{2,1,0:T(8,128)(2,1)S(1)}, u32[]{:S(2)}, u32[]{:S(2)}) collective-permute-start(bf16[3,400,128]{2,1,0:T(8,128)(2,1)S(1)} %get-tuple-element.64), channel_id=1, source_target_pairs={{0,2},{1,3},{2,0},{3,1},{4,6},{5,7},{6,4},{7,5},{8,10},{9,11},{10,... | collective-permute-start | bytes 921608 | tf_op jit(solution)/shard_map/ppermute | solution.py:291
  11.1 22.2 %collective-permute-start.1 = (bf16[3,400,128]{2,1,0:T(8,128)(2,1)S(1)}, bf16[3,400,128]{2,1,0:T(8,128)(2,1)S(1)}, u32[]{:S(2)}, u32[]{:S(2)}) collective-permute-start(bf16[3,400,128]{2,1,0:T(8,128)(2,1)S(1)} %get-tuple-element.65), channel_id=1, source_target_pairs={{0,4},{1,5},{2,6},{3,7},{4,0},{5,1},{6,2},{7,3},{8,12},{9,13},{10,... | collective-permute-start | bytes 921608 | tf_op jit(solution)/shard_map/ppermute | solution.py:291
  12.7 25.9 %collective-permute-start.2 = (bf16[3,400,128]{2,1,0:T(8,128)(2,1)S(1)}, bf16[3,400,128]{2,1,0:T(8,128)(2,1)S(1)}, u32[]{:S(2)}, u32[]{:S(2)}) collective-permute-start(bf16[3,400,128]{2,1,0:T(8,128)(2,1)S(1)} %get-tuple-element.66), channel_id=1, source_target_pairs={{0,6},{1,7},{2,4},{3,5},{4,2},{5,3},{6,0},{7,1},{8,14},{9,15},{10,... | collective-permute-start | bytes 921608 | tf_op jit(solution)/shard_map/ppermute | solution.py:291
  13.0 38.9 %collective-permute-start.4 = (bf16[3,400,128]{2,1,0:T(8,128)(2,1)S(1)}, bf16[3,400,128]{2,1,0:T(8,128)(2,1)S(1)}, u32[]{:S(2)}, u32[]{:S(2)}) collective-permute-start(bf16[3,400,128]{2,1,0:T(8,128)(2,1)S(1)} %get-tuple-element.68), channel_id=1, source_target_pairs={{0,10},{1,11},{2,8},{3,9},{4,14},{5,15},{6,12},{7,13},{8,2},{9,3},... | collective-permute-start | bytes 921608 | tf_op jit(solution)/shard_map/ppermute | solution.py:291
  24.3 27.6 %collective-permute-start.5 = (bf16[3,400,128]{2,1,0:T(8,128)(2,1)S(1)}, bf16[3,400,128]{2,1,0:T(8,128)(2,1)S(1)}, u32[]{:S(2)}, u32[]{:S(2)}) collective-permute-start(bf16[3,400,128]{2,1,0:T(8,128)(2,1)S(1)} %get-tuple-element.69), channel_id=1, source_target_pairs={{0,12},{1,13},{2,14},{3,15},{4,8},{5,9},{6,10},{7,11},{8,4},{9,5},... | collective-permute-start | bytes 921608 | tf_op jit(solution)/shard_map/ppermute | solution.py:291
  27.1 24.8 %collective-permute-start.6 = (bf16[3,400,128]{2,1,0:T(8,128)(2,1)S(1)}, bf16[3,400,128]{2,1,0:T(8,128)(2,1)S(1)}, u32[]{:S(2)}, u32[]{:S(2)}) collective-permute-start(bf16[3,400,128]{2,1,0:T(8,128)(2,1)S(1)} %get-tuple-element.73), channel_id=1, source_target_pairs={{0,14},{1,15},{2,12},{3,13},{4,10},{5,11},{6,8},{7,9},{8,6},{9,7},... | collective-permute-start | bytes 921608 | tf_op jit(solution)/shard_map/ppermute | solution.py:291
  53.0 16.6 %collective-permute-start.7 = (bf16[8,2,384,128]{3,2,1,0:T(8,128)(2,1)S(1)}, bf16[8,2,384,128]{3,2,1,0:T(8,128)(2,1)S(1)}, u32[]{:S(2)}, u32[]{:S(2)}) collective-permute-start(bf16[8,2,384,128]{3,2,1,0:T(8,128)(2,1)S(1)} %gather_keys.2), channel_id=1, source_target_pairs={{0,1},{1,0},{2,3},{3,2},{4,5},{5,4},{6,7},{7,6},{8,9},{9,8},{10,11... | collective-permute-start | bytes 4718600 | tf_op jit(solution)/shard_map/ppermute | solution.py:313
  53.1 34.0 %collective-permute-start.12 = (bf16[3,272,128]{2,1,0:T(8,128)(2,1)S(1)}, bf16[3,272,128]{2,1,0:T(8,128)(2,1)S(1)}, u32[]{:S(2)}, u32[]{:S(2)}) collective-permute-start(bf16[3,272,128]{2,1,0:T(8,128)(2,1)S(1)} %get-tuple-element.87), channel_id=1, source_target_pairs={{0,8},{1,9},{2,10},{3,11},{4,12},{5,13},{6,14},{7,15},{8,0},{9,1},... | collective-permute-start | bytes 626696 | tf_op jit(solution)/shard_map/ppermute | solution.py:291
  67.8 23.9 %collective-permute-start.8 = (bf16[3,272,128]{2,1,0:T(8,128)(2,1)S(1)}, bf16[3,272,128]{2,1,0:T(8,128)(2,1)S(1)}, u32[]{:S(2)}, u32[]{:S(2)}) collective-permute-start(bf16[3,272,128]{2,1,0:T(8,128)(2,1)S(1)} %get-tuple-element.77), channel_id=1, source_target_pairs={{0,10},{1,11},{2,8},{3,9},{4,14},{5,15},{6,12},{7,13},{8,2},{9,3},... | collective-permute-start | bytes 626696 | tf_op jit(solution)/shard_map/ppermute | solution.py:291
  67.8 25.2 %collective-permute-start.10 = (bf16[3,272,128]{2,1,0:T(8,128)(2,1)S(1)}, bf16[3,272,128]{2,1,0:T(8,128)(2,1)S(1)}, u32[]{:S(2)}, u32[]{:S(2)}) collective-permute-start(bf16[3,272,128]{2,1,0:T(8,128)(2,1)S(1)} %get-tuple-element.81), channel_id=1, source_target_pairs={{0,12},{1,13},{2,14},{3,15},{4,8},{5,9},{6,10},{7,11},{8,4},{9,5},... | collective-permute-start | bytes 626696 | tf_op jit(solution)/shard_map/ppermute | solution.py:291
  68.3 24.7 %collective-permute-start.15 = (bf16[3,272,128]{2,1,0:T(8,128)(2,1)S(1)}, bf16[3,272,128]{2,1,0:T(8,128)(2,1)S(1)}, u32[]{:S(2)}, u32[]{:S(2)}) collective-permute-start(bf16[3,272,128]{2,1,0:T(8,128)(2,1)S(1)} %get-tuple-element.92), channel_id=1, source_target_pairs={{0,2},{1,3},{2,0},{3,1},{4,6},{5,7},{6,4},{7,5},{8,10},{9,11},{10,... | collective-permute-start | bytes 626696 | tf_op jit(solution)/shard_map/ppermute | solution.py:291
  69.7 23.3 %collective-permute-start.17 = (bf16[3,272,128]{2,1,0:T(8,128)(2,1)S(1)}, bf16[3,272,128]{2,1,0:T(8,128)(2,1)S(1)}, u32[]{:S(2)}, u32[]{:S(2)}) collective-permute-start(bf16[3,272,128]{2,1,0:T(8,128)(2,1)S(1)} %get-tuple-element.96), channel_id=1, source_target_pairs={{0,4},{1,5},{2,6},{3,7},{4,0},{5,1},{6,2},{7,3},{8,12},{9,13},{10,... | collective-permute-start | bytes 626696 | tf_op jit(solution)/shard_map/ppermute | solution.py:291
  87.1 8.7 %collective-permute-start.19 = (bf16[3,272,128]{2,1,0:T(8,128)(2,1)S(1)}, bf16[3,272,128]{2,1,0:T(8,128)(2,1)S(1)}, u32[]{:S(2)}, u32[]{:S(2)}) collective-permute-start(bf16[3,272,128]{2,1,0:T(8,128)(2,1)S(1)} %get-tuple-element.100), channel_id=1, source_target_pairs={{0,6},{1,7},{2,4},{3,5},{4,2},{5,3},{6,0},{7,1},{8,14},{9,15},{10,... | collective-permute-start | bytes 626696 | tf_op jit(solution)/shard_map/ppermute | solution.py:291
  91.6 9.5 %collective-permute-start.13 = (bf16[3,272,128]{2,1,0:T(8,128)(2,1)S(1)}, bf16[3,272,128]{2,1,0:T(8,128)(2,1)S(1)}, u32[]{:S(2)}, u32[]{:S(2)}) collective-permute-start(bf16[3,272,128]{2,1,0:T(8,128)(2,1)S(1)} %get-tuple-element.88), channel_id=1, source_target_pairs={{0,14},{1,15},{2,12},{3,13},{4,10},{5,11},{6,8},{7,9},{8,6},{9,7},... | collective-permute-start | bytes 626696 | tf_op jit(solution)/shard_map/ppermute | solution.py:291
  101.9 15.5 %collective-permute-start.20 = (bf16[8,2,256,128]{3,2,1,0:T(8,128)(2,1)S(1)}, bf16[8,2,256,128]{3,2,1,0:T(8,128)(2,1)S(1)}, u32[]{:S(2)}, u32[]{:S(2)}) collective-permute-start(bf16[8,2,256,128]{3,2,1,0:T(8,128)(2,1)S(1)} %gather_keys.3), channel_id=1, source_target_pairs={{0,1},{1,0},{2,3},{3,2},{4,5},{5,4},{6,7},{7,6},{8,9},{9,8},{10,11... | collective-permute-start | bytes 3145736 | tf_op jit(solution)/shard_map/ppermute | solution.py:313
  101.9 8.7 %collective-permute-start.16 = (bf16[384,128]{1,0:T(8,128)(2,1)S(1)}, bf16[384,128]{1,0:T(8,128)(2,1)S(1)}, u32[]{:S(2)}, u32[]{:S(2)}) collective-permute-start(bf16[384,128]{1,0:T(8,128)(2,1)S(1)} %get-tuple-element.93), channel_id=1, source_target_pairs={{0,8},{1,9},{2,10},{3,11},{4,12},{5,13},{6,14},{7,15},{8,0},{9,1},... | collective-permute-start | bytes 294920 | tf_op jit(solution)/shard_map/ppermute | solution.py:291
  105.3 22.2 %collective-permute-start.18 = (bf16[384,128]{1,0:T(8,128)(2,1)S(1)}, bf16[384,128]{1,0:T(8,128)(2,1)S(1)}, u32[]{:S(2)}, u32[]{:S(2)}) collective-permute-start(bf16[384,128]{1,0:T(8,128)(2,1)S(1)} %get-tuple-element.97), channel_id=1, source_target_pairs={{0,10},{1,11},{2,8},{3,9},{4,14},{5,15},{6,12},{7,13},{8,2},{9,3},... | collective-permute-start | bytes 294920 | tf_op jit(solution)/shard_map/ppermute | solution.py:291
  106.2 22.3 %collective-permute-start.11 = (bf16[384,128]{1,0:T(8,128)(2,1)S(1)}, bf16[384,128]{1,0:T(8,128)(2,1)S(1)}, u32[]{:S(2)}, u32[]{:S(2)}) collective-permute-start(bf16[384,128]{1,0:T(8,128)(2,1)S(1)} %get-tuple-element.82), channel_id=1, source_target_pairs={{0,4},{1,5},{2,6},{3,7},{4,0},{5,1},{6,2},{7,3},{8,12},{9,13},{10,... | collective-permute-start | bytes 294920 | tf_op jit(solution)/shard_map/ppermute | solution.py:291
  110.2 13.8 %collective-permute-start.9 = (bf16[384,128]{1,0:T(8,128)(2,1)S(1)}, bf16[384,128]{1,0:T(8,128)(2,1)S(1)}, u32[]{:S(2)}, u32[]{:S(2)}) collective-permute-start(bf16[384,128]{1,0:T(8,128)(2,1)S(1)} %get-tuple-element.78), channel_id=1, source_target_pairs={{0,2},{1,3},{2,0},{3,1},{4,6},{5,7},{6,4},{7,5},{8,10},{9,11},{10,... | collective-permute-start | bytes 294920 | tf_op jit(solution)/shard_map/ppermute | solution.py:291
  110.7 17.9 %collective-permute-start.22 = (bf16[384,128]{1,0:T(8,128)(2,1)S(1)}, bf16[384,128]{1,0:T(8,128)(2,1)S(1)}, u32[]{:S(2)}, u32[]{:S(2)}) collective-permute-start(bf16[384,128]{1,0:T(8,128)(2,1)S(1)} %get-tuple-element.105), channel_id=1, source_target_pairs={{0,14},{1,15},{2,12},{3,13},{4,10},{5,11},{6,8},{7,9},{8,6},{9,7},... | collective-permute-start | bytes 294920 | tf_op jit(solution)/shard_map/ppermute | solution.py:291
  117.4 6.8 %collective-permute-start.14 = (bf16[384,128]{1,0:T(8,128)(2,1)S(1)}, bf16[384,128]{1,0:T(8,128)(2,1)S(1)}, u32[]{:S(2)}, u32[]{:S(2)}) collective-permute-start(bf16[384,128]{1,0:T(8,128)(2,1)S(1)} %get-tuple-element.89), channel_id=1, source_target_pairs={{0,6},{1,7},{2,4},{3,5},{4,2},{5,3},{6,0},{7,1},{8,14},{9,15},{10,... | collective-permute-start | bytes 294920 | tf_op jit(solution)/shard_map/ppermute | solution.py:291
  124.0 14.7 %collective-permute-start.21 = (bf16[384,128]{1,0:T(8,128)(2,1)S(1)}, bf16[384,128]{1,0:T(8,128)(2,1)S(1)}, u32[]{:S(2)}, u32[]{:S(2)}) collective-permute-start(bf16[384,128]{1,0:T(8,128)(2,1)S(1)} %get-tuple-element.103), channel_id=1, source_target_pairs={{0,12},{1,13},{2,14},{3,15},{4,8},{5,9},{6,10},{7,11},{8,4},{9,5},... | collective-permute-start | bytes 294920 | tf_op jit(solution)/shard_map/ppermute | solution.py:291
  124.1 13.8 %collective-permute-start.26 = (bf16[256,128]{1,0:T(8,128)(2,1)S(1)}, bf16[256,128]{1,0:T(8,128)(2,1)S(1)}, u32[]{:S(2)}, u32[]{:S(2)}) collective-permute-start(bf16[256,128]{1,0:T(8,128)(2,1)S(1)} %get-tuple-element.113), channel_id=1, source_target_pairs={{0,8},{1,9},{2,10},{3,11},{4,12},{5,13},{6,14},{7,15},{8,0},{9,1},... | collective-permute-start | bytes 196616 | tf_op jit(solution)/shard_map/ppermute | solution.py:291
  127.5 12.3 %collective-permute-start.28 = (bf16[256,128]{1,0:T(8,128)(2,1)S(1)}, bf16[256,128]{1,0:T(8,128)(2,1)S(1)}, u32[]{:S(2)}, u32[]{:S(2)}) collective-permute-start(bf16[256,128]{1,0:T(8,128)(2,1)S(1)} %get-tuple-element.118), channel_id=1, source_target_pairs={{0,12},{1,13},{2,14},{3,15},{4,8},{5,9},{6,10},{7,11},{8,4},{9,5},... | collective-permute-start | bytes 196616 | tf_op jit(solution)/shard_map/ppermute | solution.py:291
  128.5 12.4 %collective-permute-start.27 = (bf16[256,128]{1,0:T(8,128)(2,1)S(1)}, bf16[256,128]{1,0:T(8,128)(2,1)S(1)}, u32[]{:S(2)}, u32[]{:S(2)}) collective-permute-start(bf16[256,128]{1,0:T(8,128)(2,1)S(1)} %get-tuple-element.115), channel_id=1, source_target_pairs={{0,10},{1,11},{2,8},{3,9},{4,14},{5,15},{6,12},{7,13},{8,2},{9,3},... | collective-permute-start | bytes 196616 | tf_op jit(solution)/shard_map/ppermute | solution.py:291
  129.9 11.0 %collective-permute-start.25 = (bf16[256,128]{1,0:T(8,128)(2,1)S(1)}, bf16[256,128]{1,0:T(8,128)(2,1)S(1)}, u32[]{:S(2)}, u32[]{:S(2)}) collective-permute-start(bf16[256,128]{1,0:T(8,128)(2,1)S(1)} %get-tuple-element.111), channel_id=1, source_target_pairs={{0,6},{1,7},{2,4},{3,5},{4,2},{5,3},{6,0},{7,1},{8,14},{9,15},{10,... | collective-permute-start | bytes 196616 | tf_op jit(solution)/shard_map/ppermute | solution.py:291
  138.0 4.3 %collective-permute-start.23 = (bf16[256,128]{1,0:T(8,128)(2,1)S(1)}, bf16[256,128]{1,0:T(8,128)(2,1)S(1)}, u32[]{:S(2)}, u32[]{:S(2)}) collective-permute-start(bf16[256,128]{1,0:T(8,128)(2,1)S(1)} %get-tuple-element.107), channel_id=1, source_target_pairs={{0,2},{1,3},{2,0},{3,1},{4,6},{5,7},{6,4},{7,5},{8,10},{9,11},{10,... | collective-permute-start | bytes 196616 | tf_op jit(solution)/shard_map/ppermute | solution.py:291
  138.7 7.1 %collective-permute-start.29 = (bf16[256,128]{1,0:T(8,128)(2,1)S(1)}, bf16[256,128]{1,0:T(8,128)(2,1)S(1)}, u32[]{:S(2)}, u32[]{:S(2)}) collective-permute-start(bf16[256,128]{1,0:T(8,128)(2,1)S(1)} %get-tuple-element.120), channel_id=1, source_target_pairs={{0,14},{1,15},{2,12},{3,13},{4,10},{5,11},{6,8},{7,9},{8,6},{9,7},... | collective-permute-start | bytes 196616 | tf_op jit(solution)/shard_map/ppermute | solution.py:291
  139.8 6.0 %collective-permute-start.24 = (bf16[256,128]{1,0:T(8,128)(2,1)S(1)}, bf16[256,128]{1,0:T(8,128)(2,1)S(1)}, u32[]{:S(2)}, u32[]{:S(2)}) collective-permute-start(bf16[256,128]{1,0:T(8,128)(2,1)S(1)} %get-tuple-element.109), channel_id=1, source_target_pairs={{0,4},{1,5},{2,6},{3,7},{4,0},{5,1},{6,2},{7,3},{8,12},{9,13},{10,... | collective-permute-start | bytes 196616 | tf_op jit(solution)/shard_map/ppermute | solution.py:291
  (3 other events, 14.3 us)

commit v3 on v2

v3 whole, which is shorter than its diff:
```python
import functools
import math

import jax
import jax.numpy as jnp
from jax import lax
from jax.experimental import pallas as pl
from jax.experimental.pallas import tpu as pltpu
from jax.sharding import PartitionSpec as P

F32, BF16, I32 = jnp.float32, jnp.bfloat16, jnp.int32
DEAD = -1e30
VMEM_BYTES = 48 << 20
PACK_BYTES = 60 << 20
MIX_BACK = True
INFO_ROWS = 16
GROUP = 4
WINDOW = 8
LATE_A = 3
SEEN_A = 0
LATE_B = 3
SEEN_B = 2


def params(limit=VMEM_BYTES):
    return pltpu.CompilerParams(vmem_limit_bytes=limit)


def cost(flops, count):
    return pl.CostEstimate(flops=flops, bytes_accessed=count, transcendentals=0)


class Plan:
    def __init__(self, seq, heads, rows, dim, lists, blocks):
        self.seq, self.heads, self.rows, self.dim, self.lists = seq, heads, rows, dim, lists
        self.chips = seq // 2
        self.per_chip = -(-heads // self.chips)
        self.padded = self.per_chip * self.chips > heads
        self.bits = max(1, (blocks - 1).bit_length())
        assert self.chips & (self.chips - 1) == 0
        assert lists * self.bits + lists.bit_length() < 31 and lists < INFO_ROWS
        self.near = list(range(max(1, self.chips // 2)))
        self.far = list(range(len(self.near), self.chips))
        cut = -(-self.per_chip * 3 // 5)
        self.pieces = [(0, cut)]
        if cut < self.per_chip:
            self.pieces.append((cut, self.per_chip - cut))

    def head(self, chip, slot):
        return chip * self.per_chip + slot


def pack_kernel(plan, items, me_ref, x_ref, ids_ref, counts_ref, *refs):
    outs, (wide, ids, counts, info, sem) = refs[: len(items)], refs[len(items) :]
    rows, _, heads, _ = x_ref.shape
    chip, lists = me_ref[0] // 2, plan.lists
    first = pl.program_id(0) == 0
    copies = [
        pltpu.make_async_copy(ids_ref, ids, sem.at[0]),
        pltpu.make_async_copy(counts_ref, counts, sem.at[1]),
    ]

    @pl.when(first)
    def _():
        for copy in copies:
            copy.start()

    def widen(t, carry):
        wide[pl.ds(pl.multiple_of(t * heads, 8), heads), :] = x_ref[t, 0].astype(F32)
        return carry

    lax.fori_loop(0, rows, widen, 0, unroll=8)

    @pl.when(first)
    def _():
        for copy in copies:
            copy.wait()
        info[...] = jnp.zeros_like(info)
        info[:lists, :heads] = ids[0].astype(F32)
        info[lists : lists + 1, :heads] = counts[...].astype(F32)

    for (step, start, size), out in zip(items, outs):
        for slot in range(size):
            head = jnp.minimum(plan.head(chip ^ step, start + slot), heads - 1)
            out[0, slot * rows : (slot + 1) * rows, :] = wide[
                pl.ds(head, rows, stride=heads), :
            ].astype(BF16)
        out[0, size * rows :, :] = info[...].astype(BF16)


def pack(plan, items, me, by_kind, block_ids, counts):
    rows, kinds, heads, dim = by_kind.shape
    depths = [size * rows + INFO_ROWS for _, _, size in items]
    block_ids = jnp.transpose(block_ids, (0, 2, 1))
    return pl.pallas_call(
        functools.partial(pack_kernel, plan, items),
        grid_spec=pltpu.PrefetchScalarGridSpec(
            num_scalar_prefetch=1,
            grid=(kinds,),
            in_specs=[
                pl.BlockSpec((rows, 1, heads, dim), lambda s, *_: (0, s, 0, 0)),
                pl.BlockSpec(memory_space=pl.ANY),
                pl.BlockSpec(memory_space=pl.ANY),
            ],
            out_specs=[pl.BlockSpec((1, d, dim), lambda s, *_: (s, 0, 0)) for d in depths],
            scratch_shapes=[
                pltpu.VMEM((rows * heads, dim), F32),
                pltpu.VMEM(block_ids.shape, I32),
                pltpu.VMEM(counts.shape, I32),
                pltpu.VMEM((INFO_ROWS, dim), F32),
                pltpu.SemaphoreType.DMA((2,)),
            ],
        ),
        out_shape=[jax.ShapeDtypeStruct((kinds, d, dim), BF16) for d in depths],
        compiler_params=params(PACK_BYTES),
        cost_estimate=cost(0, 8 << 20),
        name="pack",
    )(me, by_kind, block_ids, counts)


def gather_kernel(plan, spans, *refs):
    rows_refs, out_ref, sem = refs[:-2], refs[-2], refs[-1]
    copies = [
        pltpu.make_async_copy(ref.at[1:3, begin:end], out_ref.at[step], sem.at[step])
        for step, (ref, (begin, end)) in enumerate(zip(rows_refs, spans))
    ]
    for copy in copies:
        copy.start()
    for copy in copies:
        copy.wait()


def spans_of(plan, piece):
    first, size = piece
    begins = [(first if step in plan.near else 0) * plan.rows for step in range(plan.chips)]
    return [(begin, begin + size * plan.rows) for begin in begins]


def gather_keys(plan, piece, came):
    return pl.pallas_call(
        functools.partial(gather_kernel, plan, spans_of(plan, piece)),
        in_specs=[pl.BlockSpec(memory_space=pl.ANY)] * plan.chips,
        out_specs=pl.BlockSpec(memory_space=pl.ANY),
        out_shape=jax.ShapeDtypeStruct((plan.chips, 2, piece[1] * plan.rows, plan.dim), BF16),
        scratch_shapes=[pltpu.SemaphoreType.DMA((plan.chips,))],
        compiler_params=params(),
        cost_estimate=cost(0, 4 << 20),
        name="gather_keys",
    )(*came)


def attend_group(units, scale):
    scores = [
        lax.dot_general(q, k, (((1,), (1,)), ((), ())), preferred_element_type=F32)
        for q, k, _, _ in units
    ]
    scores = [s * scale + bias for s, (_, _, _, bias) in zip(scores, units)]
    peaks = [jnp.max(s, axis=1, keepdims=True) for s in scores]
    weights = [jnp.exp2(s - peak) for s, peak in zip(scores, peaks)]
    totals = [jnp.sum(w, axis=1, keepdims=True) for w in weights]
    mixed = [
        jnp.dot(w.astype(BF16), v, preferred_element_type=F32)
        for w, (_, _, v, _) in zip(weights, units)
    ]
    return [(m / t).astype(BF16) for m, t in zip(mixed, totals)]


def attend_kernel(plan, piece, scale, held_rows, me_ref, *refs):
    chips, rows, lists, bits = plan.chips, plan.rows, plan.lists, plan.bits
    first, size = piece
    near, far_ref, refs = refs[:chips], refs[chips], refs[chips + 1 :]
    helds = refs[: len(plan.near)] if held_rows else []
    refs = refs[len(helds) :]
    outs, refs = refs[:chips], refs[chips:]
    queries, keys, values, info, bias, code, scalars, sem = refs
    chip, core = me_ref[0] // 2, me_ref[0] % 2

    copies = []
    for step, (ref, (begin, end)) in enumerate(zip(near, spans_of(plan, piece))):
        last = ref.shape[1] - INFO_ROWS
        moves = [
            (ref.at[0, last:], info.at[step]),
            (ref.at[0, begin:end], queries.at[step]),
            (ref.at[1, begin:end], keys.at[2 * step]),
            (ref.at[2, begin:end], values.at[2 * step]),
            (far_ref.at[step, 0], keys.at[2 * step + 1]),
            (far_ref.at[step, 1], values.at[2 * step + 1]),
        ]
        copies += [
            pltpu.make_async_copy(source, target, sem.at[step, at])
            for at, (source, target) in enumerate(moves)
        ]
    for copy in copies:
        copy.start()

    count = lax.broadcasted_iota(I32, bias.shape, 0)
    entry = lax.broadcasted_iota(I32, bias.shape, 1) // rows
    bias[...] = jnp.where((entry < count) | (entry == 0), 0.0, DEAD).astype(F32)
    for held, out in zip(helds, outs):
        out[:held_rows, :] = held[...]
    for copy in copies:
        copy.wait()

    for step in range(chips):
        row = info[step].astype(F32).astype(I32)
        total = row[:1]
        for j in range(1, lists + 1):
            total = total + (row[j : j + 1] << (j * bits))
        code[step : step + 1, :] = total
    copy = pltpu.make_async_copy(code, scalars, sem.at[0, 0])
    copy.start()
    copy.wait()

    mask = (1 << bits) - 1

    def place(block):
        return ((block // 2) ^ chip) * 2 + ((block % 2) ^ core)

    def one_slot(slot, carry):
        head = jnp.minimum(plan.head(chip, first + slot), plan.heads - 1)
        span = pl.ds(pl.multiple_of(slot * rows, rows), rows)
        below = pl.ds(pl.multiple_of(held_rows + slot * rows, rows), rows)
        for start in range(0, chips, GROUP):
            steps, units = range(start, min(start + GROUP, chips)), []
            for step in steps:
                number = scalars[step, head]
                places = [place((number >> (j * bits)) & mask) for j in range(lists)]
                live = number >> (lists * bits)
                units.append(
                    (
                        queries[step, span, :],
                        jnp.concatenate([keys[c, span, :] for c in places], axis=0),
                        jnp.concatenate([values[c, span, :] for c in places], axis=0),
                        bias[pl.ds(live, 1), :],
                    )
                )
            for step, result in zip(steps, attend_group(units, scale)):
                outs[step][below if step in plan.near else span, :] = result
        return carry

    lax.fori_loop(0, size, one_slot, 0)


def attend(plan, piece, me, came, far, helds, scale):
    chips, dim, depth = plan.chips, plan.dim, piece[1] * plan.rows
    held_rows = helds[0].shape[0] if helds else 0
    bias_rows = -(-(plan.lists + 1) // 8) * 8
    any_spec = pl.BlockSpec(memory_space=pl.ANY)
    vmem_spec = pl.BlockSpec(memory_space=pltpu.VMEM)
    depths = [depth + (held_rows if step in plan.near else 0) for step in range(chips)]
    return pl.pallas_call(
        functools.partial(attend_kernel, plan, piece, scale, held_rows),
        in_specs=[pl.BlockSpec(memory_space=pltpu.SMEM)]
        + [any_spec] * (chips + 1)
        + [vmem_spec] * len(helds),
        out_specs=[vmem_spec] * chips,
        out_shape=[jax.ShapeDtypeStruct((d, dim), BF16) for d in depths],
        scratch_shapes=[
            pltpu.VMEM((chips, depth, dim), BF16),
            pltpu.VMEM((2 * chips, depth, dim), BF16),
            pltpu.VMEM((2 * chips, depth, dim), BF16),
            pltpu.VMEM((chips, INFO_ROWS, dim), BF16),
            pltpu.VMEM((bias_rows, plan.lists * plan.rows), F32),
            pltpu.VMEM((chips, dim), I32),
            pltpu.SMEM((chips, dim), I32),
            pltpu.SemaphoreType.DMA((chips, 6)),
        ],
        compiler_params=params(),
        cost_estimate=cost(4 << 30, 8 << 20),
        name="attend",
    )(me, *came, far, *helds)


def unpack_kernel(plan, items, me_ref, *refs):
    backs, (out_ref, wide) = refs[:-2], refs[-2:]
    rows, heads, _ = out_ref.shape
    chip = me_ref[0] // 2
    for (step, first, size), back in zip(items, backs):
        for slot in range(size):
            head = plan.head(chip ^ step, first + slot)

            def spread(back=back, head=head, slot=slot):
                wide[pl.ds(head, rows, stride=heads), :] = back[
                    slot * rows : (slot + 1) * rows, :
                ].astype(F32)

            if plan.padded:
                pl.when(head < heads)(spread)
            else:
                spread()

    def narrow(t, carry):
        out_ref[t] = wide[pl.ds(pl.multiple_of(t * heads, 8), heads), :].astype(BF16)
        return carry

    lax.fori_loop(0, rows, narrow, 0, unroll=8)


def unpack(plan, items, me, backs):
    rows, heads, dim = plan.rows, plan.heads, plan.dim
    vmem_spec = pl.BlockSpec(memory_space=pltpu.VMEM)
    return pl.pallas_call(
        functools.partial(unpack_kernel, plan, items),
        in_specs=[pl.BlockSpec(memory_space=pltpu.SMEM)] + [vmem_spec] * len(backs),
        out_specs=vmem_spec,
        out_shape=jax.ShapeDtypeStruct((rows, heads, dim), BF16),
        scratch_shapes=[pltpu.VMEM((rows * heads, dim), F32)],
        compiler_params=params(),
        cost_estimate=cost(0, 4 << 20),
        name="unpack",
    )(me, *backs)


class Sender:
    def __init__(self, seq):
        self.seq, self.ended = seq, []

    def send(self, array, step, after=None):
        if after is not None:
            array, _ = lax.optimization_barrier((array, after))
        if len(self.ended) >= WINDOW:
            array, _ = lax.optimization_barrier((array, self.ended[-WINDOW]))
        got = lax.ppermute(array, "seq", [(d, d ^ (2 * step)) for d in range(self.seq)])
        self.ended.append(got)
        return got


def mixed(far, near):
    order, far, near = far[:2], far[2:], near[1:]
    while far or near:
        order += near[:1] + far[:1]
        near, far = near[1:], far[1:]
    return order


def body(seq, qkv, block_ids, counts):
    rows, heads, _, dim = qkv.shape
    plan = Plan(seq, heads, rows, dim, block_ids.shape[2], seq * block_ids.shape[0])
    scale = math.log2(math.e) / math.sqrt(dim)
    me = lax.axis_index("seq").astype(I32).reshape(1)
    by_kind = jnp.transpose(qkv, (0, 2, 1, 3))
    near, far, pieces = plan.near, plan.far, plan.pieces
    sender = Sender(seq)

    def work(piece, came, helds, sent):
        if sent is not None:
            came, _ = lax.optimization_barrier((came, sent))
        swapped = gather_keys(plan, piece, came)
        swapped = lax.ppermute(swapped, "seq", [(d, d ^ 1) for d in range(seq)])
        return attend(plan, piece, me, came, swapped, helds, scale)

    far_items = [[(step, *piece) for step in far] for piece in pieces]
    near_items = [(step, 0, plan.per_chip) for step in near]
    rest_items = near_items + [item for items in far_items[1:] for item in items]
    packed = pack(plan, far_items[0], me, by_kind, block_ids, counts)
    rest = pack(plan, rest_items, me, by_kind, block_ids, counts)
    leaving = dict(zip(near, rest)) | dict(zip(far, packed))
    got = {step: sender.send(leaving[step], step) for step in mixed(far, near)}
    got[0] = rest[0]
    came = [got[step] for step in range(plan.chips)]
    backs = []
    if len(pieces) == 1:
        outs = work(pieces[0], came, [], None)
    else:
        last = rest[len(near) :]
        got = [sender.send(a, step) for a, step in zip(last[:LATE_A], far)]
        held = work(pieces[0], came, [], got[SEEN_A])
        got += [sender.send(a, step, held[0]) for a, step in zip(last[LATE_A:], far[LATE_A:])]
        came = came[: len(near)] + got
        leaving = held[len(near) :]
        got = [sender.send(a, step) for a, step in zip(leaving[:LATE_B], far)]
        outs = work(pieces[1], came, held[: len(near)], got[SEEN_B])
        got += [sender.send(a, step, outs[0]) for a, step in zip(leaving[LATE_B:], far[LATE_B:])]
        backs += got
    got = {step: sender.send(outs[step], step) for step in (mixed(far, near) if MIX_BACK else far + near[1:])}
    got[0] = outs[0]
    items = near_items + (far_items[0] if len(pieces) > 1 else []) + far_items[-1]
    backs = [got[step] for step in near] + backs + [got[step] for step in far]
    return unpack(plan, items, me, backs)


def solution(mesh):
    in_specs = (
        P(("rep", "seq"), None, None, None),
        P(("rep", "seq"), None, None),
        P(("rep", "seq"), None),
    )
    out_specs = P(("rep", "seq"), None, None)
    return jax.shard_map(
        functools.partial(body, mesh.shape["seq"]),
        mesh=mesh,
        in_specs=in_specs,
        out_specs=out_specs,
        check_vma=False,
    )
```

time: 148 us -> 143 us (0.966)
  starting transfers between devices: 61.3 us -> 49.6 us
  Pallas kernels: 25.6 us -> 31 us
  waiting for transfers between devices: 59.3 us -> 62 us
    ppermute x30 -> x24, starting transfers between devices: 61.3 us -> 49.6 us  [the longest x22 49.4 us: send(): lax.ppermute(array, 'seq', [(d, d ^ 2 * step) for d in range(self.seq)])]
    pallas_call x7, Pallas kernels: 25.6 us -> 31 us  [the longest x2 16.1 us: attend(): pl.pallas_call(functools.partial(attend_kernel, plan, piece, scale, held_...]
    ppermute x30 -> x24, waiting for transfers between devices: 59.3 us -> 62 us  [the longest x22 62 us: send(): lax.ppermute(array, 'seq', [(d, d ^ 2 * step) for d in range(self.seq)])]
  transfers between devices with their start and end apart: 30 -> 24, of which waited for: 12 -> 12; matrix products, arithmetic and copies ran while one was open for 0% -> 0% of each run, Pallas kernels for 12% -> 15%
where the time goes in v3:
time: 143 us
  waiting for transfers between devices  62 us (43%)
  starting transfers between devices  49.6 us (35%)
  Pallas kernels  31 us (22%)
    ppermute x22, waiting for transfers between devices, send(): lax.ppermute(array, 'seq', [(d, d ^ 2 * step) for d in range(self.seq)])  62 us
    ppermute x22, starting transfers between devices, send(): lax.ppermute(array, 'seq', [(d, d ^ 2 * step) for d in range(self.seq)])  49.4 us
    pallas_call x2, Pallas kernels, attend(): pl.pallas_call(functools.partial(attend_kernel, plan, piece, scale, held_...  16.1 us
    pallas_call x2, Pallas kernels, pack(): pl.pallas_call(functools.partial(pack_kernel, plan, items), grid_spec=plt...  11.1 us
  transfers between devices with their start and end apart: 24, of which 12 were waited for; matrix products, arithmetic and copies ran while one was open for 0% of the time, Pallas kernels for 15%

profile of v3, /device:TPU:0, one launch (start us, length us, event | category | flops | bytes accessed | tf_op | source)
XLA Modules:
  0.0 142.8 jit_solution(8484439796430142512)
XLA Ops:
  0.0 5.9 %pack.2 = (bf16[3,656,128]{2,1,0:T(8,128)(2,1)}, bf16[3,656,128]{2,1,0:T(8,128)(2,1)}, bf16[3,656,128]{2,1,0:T(8,128)(2,1)}, bf16[3,656,128]{2,1,0:T(8,128)(2,1)...) custom-call(s32[1]{0:T(128)} %bitcast.me_ref, ...), custom_call_target="tpu_custom_call" | custom-call | bytes 8388608 | tf_op jit(solution)/shard_map/pack/pallas_call | solution.py:95
  6.0 4.1 %collective-permute-start.3 = (bf16[3,272,128]{2,1,0:T(8,128)(2,1)}, bf16[3,272,128]{2,1,0:T(8,128)(2,1)S(1)}, u32[]{:S(2)}, u32[]{:S(2)}) collective-permute-start(bf16[3,272,128]{2,1,0:T(8,128)(2,1)} %get-tuple-element.69), channel_id=1, source_target_pairs={{0,8},{1,9},{2,10},{3,11},{4,12},{5,13},{6,14},{7,15},{8,0},{9,1},... | collective-permute-start | bytes 626696 | tf_op jit(solution)/shard_map/ppermute | solution.py:323
  10.1 5.2 %pack.3 = (bf16[3,400,128]{2,1,0:T(8,128)(2,1)}, bf16[3,400,128]{2,1,0:T(8,128)(2,1)}, bf16[3,400,128]{2,1,0:T(8,128)(2,1)}, bf16[3,400,128]{2,1,0:T(8,128)(2,1)}) custom-call(s32[1]{0:T(128)} %bitcast.me_ref, bf16[128,3,40,128]{3,2,1,0:T(8,128)(2,1)} %bitcast.4, s32[1,4,40]{2,1,0:T(4,128)} %bitcast.6, s32[1,40]{1,0:T(1,128)} %counts_ref.3), custom_call_target="tpu_custom_call" | custom-call | bytes 8388608 | tf_op jit(solution)/shard_map/pack/pallas_call | solution.py:95
  15.5 3.7 %collective-permute-start.6 = (bf16[3,400,128]{2,1,0:T(8,128)(2,1)}, bf16[3,400,128]{2,1,0:T(8,128)(2,1)S(1)}, u32[]{:S(2)}, u32[]{:S(2)}) collective-permute-start(bf16[3,400,128]{2,1,0:T(8,128)(2,1)} %get-tuple-element.74), channel_id=1, source_target_pairs={{0,10},{1,11},{2,8},{3,9},{4,14},{5,15},{6,12},{7,13},{8,2},{9,3},... | collective-permute-start | bytes 921608 | tf_op jit(solution)/shard_map/ppermute | solution.py:323
  19.7 1.6 %collective-permute-start.1 = (bf16[3,656,128]{2,1,0:T(8,128)(2,1)S(1)}, bf16[3,656,128]{2,1,0:T(8,128)(2,1)S(1)}, u32[]{:S(2)}, u32[]{:S(2)}) collective-permute-start(bf16[3,656,128]{2,1,0:T(8,128)(2,1)S(1)} %copy-done.2), channel_id=1, source_target_pairs={{0,4},{1,5},{2,6},{3,7},{4,0},{5,1},{6,2},{7,3},{8,12},{9,13},{10,... | collective-permute-start | bytes 1511432 | tf_op jit(solution)/shard_map/ppermute | solution.py:323
  21.3 12.3 %collective-permute-done.3.refs_4_ = bf16[3,272,128]{2,1,0:T(8,128)(2,1)S(1)} collective-permute-done((bf16[3,272,128]{2,1,0:T(8,128)(2,1)}, bf16[3,272,128]{2,1,0:T(8,128)(2,1)S(1)}, u32[]{:S(2)}, u32[]{:S(2)}) %collective-permute-start.3) | collective-permute-done | bytes 208928 | tf_op jit(solution)/shard_map/ppermute | solution.py:323
  33.6 1.4 %collective-permute-start.2 = (bf16[3,656,128]{2,1,0:T(8,128)(2,1)S(1)}, bf16[3,656,128]{2,1,0:T(8,128)(2,1)S(1)}, u32[]{:S(2)}, u32[]{:S(2)}) collective-permute-start(bf16[3,656,128]{2,1,0:T(8,128)(2,1)S(1)} %copy-done.1), channel_id=1, source_target_pairs={{0,6},{1,7},{2,4},{3,5},{4,2},{5,3},{6,0},{7,1},{8,14},{9,15},{10,... | collective-permute-start | bytes 1511432 | tf_op jit(solution)/shard_map/ppermute | solution.py:323
  35.0 5.6 %collective-permute-done.4.refs_4_ = bf16[3,400,128]{2,1,0:T(8,128)(2,1)S(1)} collective-permute-done((bf16[3,400,128]{2,1,0:T(8,128)(2,1)}, bf16[3,400,128]{2,1,0:T(8,128)(2,1)S(1)}, u32[]{:S(2)}, u32[]{:S(2)}) %collective-permute-start.4) | collective-permute-done | bytes 307232 | tf_op jit(solution)/shard_map/ppermute | solution.py:323
  40.6 2.8 %collective-permute-start.8 = (bf16[3,400,128]{2,1,0:T(8,128)(2,1)}, bf16[3,400,128]{2,1,0:T(8,128)(2,1)S(1)}, u32[]{:S(2)}, u32[]{:S(2)}) collective-permute-start(bf16[3,400,128]{2,1,0:T(8,128)(2,1)} %get-tuple-element.77), channel_id=1, source_target_pairs={{0,12},{1,13},{2,14},{3,15},{4,8},{5,9},{6,10},{7,11},{8,4},{9,5},... | collective-permute-start | bytes 921608 | tf_op jit(solution)/shard_map/ppermute | solution.py:323
  43.4 5.0 %collective-permute-done.6.refs_5_ = bf16[3,400,128]{2,1,0:T(8,128)(2,1)S(1)} collective-permute-done((bf16[3,400,128]{2,1,0:T(8,128)(2,1)}, bf16[3,400,128]{2,1,0:T(8,128)(2,1)S(1)}, u32[]{:S(2)}, u32[]{:S(2)}) %collective-permute-start.6) | collective-permute-done | bytes 307232 | tf_op jit(solution)/shard_map/ppermute | solution.py:323
  48.4 2.4 %collective-permute-start.9 = (bf16[3,400,128]{2,1,0:T(8,128)(2,1)}, bf16[3,400,128]{2,1,0:T(8,128)(2,1)S(1)}, u32[]{:S(2)}, u32[]{:S(2)}) collective-permute-start(bf16[3,400,128]{2,1,0:T(8,128)(2,1)} %get-tuple-element.78), channel_id=1, source_target_pairs={{0,14},{1,15},{2,12},{3,13},{4,10},{5,11},{6,8},{7,9},{8,6},{9,7},... | collective-permute-start | bytes 921608 | tf_op jit(solution)/shard_map/ppermute | solution.py:323
  50.8 11.7 %collective-permute-done.8.refs_6_ = bf16[3,400,128]{2,1,0:T(8,128)(2,1)S(1)} collective-permute-done((bf16[3,400,128]{2,1,0:T(8,128)(2,1)}, bf16[3,400,128]{2,1,0:T(8,128)(2,1)S(1)}, u32[]{:S(2)}, u32[]{:S(2)}) %collective-permute-start.8) | collective-permute-done | bytes 307232 | tf_op jit(solution)/shard_map/ppermute | solution.py:323
  62.6 6.1 %collective-permute-done.9.refs_7_ = bf16[3,400,128]{2,1,0:T(8,128)(2,1)S(1)} collective-permute-done((bf16[3,400,128]{2,1,0:T(8,128)(2,1)}, bf16[3,400,128]{2,1,0:T(8,128)(2,1)S(1)}, u32[]{:S(2)}, u32[]{:S(2)}) %collective-permute-start.9) | collective-permute-done | bytes 307232 | tf_op jit(solution)/shard_map/ppermute | solution.py:323
  68.7 2.6 %collective-permute-done.2.refs_3_ = bf16[3,656,128]{2,1,0:T(8,128)(2,1)S(1)} collective-permute-done((bf16[3,656,128]{2,1,0:T(8,128)(2,1)S(1)}, bf16[3,656,128]{2,1,0:T(8,128)(2,1)S(1)}, u32[]{:S(2)}, u32[]{:S(2)}) %collective-permute-start.2) | collective-permute-done | bytes 503840 | tf_op jit(solution)/shard_map/ppermute | solution.py:323
  71.2 1.1 gather_keys.2
  72.4 3.7 %collective-permute-start.7 = (bf16[3,272,128]{2,1,0:T(8,128)(2,1)S(1)}, bf16[3,272,128]{2,1,0:T(8,128)(2,1)S(1)}, u32[]{:S(2)}, u32[]{:S(2)}) collective-permute-start(bf16[3,272,128]{2,1,0:T(8,128)(2,1)S(1)} %copy-done.6), channel_id=1, source_target_pairs={{0,12},{1,13},{2,14},{3,15},{4,8},{5,9},{6,10},{7,11},{8,4},{9,5},... | collective-permute-start | bytes 626696 | tf_op jit(solution)/shard_map/ppermute | solution.py:323
  76.1 1.5 %collective-permute-start.5 = (bf16[3,272,128]{2,1,0:T(8,128)(2,1)S(1)}, bf16[3,272,128]{2,1,0:T(8,128)(2,1)S(1)}, u32[]{:S(2)}, u32[]{:S(2)}) collective-permute-start(bf16[3,272,128]{2,1,0:T(8,128)(2,1)S(1)} %copy-done.5), channel_id=1, source_target_pairs={{0,10},{1,11},{2,8},{3,9},{4,14},{5,15},{6,12},{7,13},{8,2},{9,3},... | collective-permute-start | bytes 626696 | tf_op jit(solution)/shard_map/ppermute | solution.py:323
  77.6 9.3 %attend.2 = (bf16[384,128]{1,0:T(8,128)(2,1)S(1)}, bf16[384,128]{1,0:T(8,128)(2,1)S(1)}, bf16[384,128]{1,0:T(8,128)(2,1)S(1)}, bf16[384,128]{1,0:T(8,128)(2,1)S(...) custom-call(s32[1]{0:T(128)} %bitcast.me_ref, ...), custom_call_target="tpu_custom_call" | custom-call | flops 4294967296 | bytes 8388608 | tf_op jit(solution)/shard_map/attend/pallas_call | solution.py:251
  86.9 3.9 %collective-permute-start.11 = (bf16[3,272,128]{2,1,0:T(8,128)(2,1)S(1)}, bf16[3,272,128]{2,1,0:T(8,128)(2,1)S(1)}, u32[]{:S(2)}, u32[]{:S(2)}) collective-permute-start(bf16[3,272,128]{2,1,0:T(8,128)(2,1)S(1)} %copy-done.4), channel_id=1, source_target_pairs={{0,14},{1,15},{2,12},{3,13},{4,10},{5,11},{6,8},{7,9},{8,6},{9,7},... | collective-permute-start | bytes 626696 | tf_op jit(solution)/shard_map/ppermute | solution.py:323
  90.8 1.0 collective-permute-start.12
  91.8 10.0 %collective-permute-done.5.refs_5_ = bf16[3,272,128]{2,1,0:T(8,128)(2,1)S(1)} collective-permute-done((bf16[3,272,128]{2,1,0:T(8,128)(2,1)S(1)}, bf16[3,272,128]{2,1,0:T(8,128)(2,1)S(1)}, u32[]{:S(2)}, u32[]{:S(2)}) %collective-permute-start.5) | collective-permute-done | bytes 208928 | tf_op jit(solution)/shard_map/ppermute | solution.py:323
  102.7 9.2 %collective-permute-start.18 = (bf16[384,128]{1,0:T(8,128)(2,1)S(1)}, bf16[384,128]{1,0:T(8,128)(2,1)S(1)}, u32[]{:S(2)}, u32[]{:S(2)}) collective-permute-start(bf16[384,128]{1,0:T(8,128)(2,1)S(1)} %get-tuple-element.113), channel_id=1, source_target_pairs={{0,10},{1,11},{2,8},{3,9},{4,14},{5,15},{6,12},{7,13},{8,2},{9,3},... | collective-permute-start | bytes 294920 | tf_op jit(solution)/shard_map/ppermute | solution.py:323
  112.1 6.8 %attend.3 = (bf16[640,128]{1,0:T(8,128)(2,1)S(1)}, bf16[640,128]{1,0:T(8,128)(2,1)S(1)}, bf16[640,128]{1,0:T(8,128)(2,1)S(1)}, bf16[640,128]{1,0:T(8,128)(2,1)S(...) custom-call(s32[1]{0:T(128)} %bitcast.me_ref, ...), custom_call_target="tpu_custom_call" | custom-call | flops 4294967296 | bytes 8388608 | tf_op jit(solution)/shard_map/attend/pallas_call | solution.py:251
  120.3 1.4 collective-permute-done.15.refs_4_
  121.7 2.8 %collective-permute-start.22 = (bf16[256,128]{1,0:T(8,128)(2,1)S(1)}, bf16[256,128]{1,0:T(8,128)(2,1)S(1)}, u32[]{:S(2)}, u32[]{:S(2)}) collective-permute-start(bf16[256,128]{1,0:T(8,128)(2,1)S(1)} %get-tuple-element.122), channel_id=1, source_target_pairs={{0,12},{1,13},{2,14},{3,15},{4,8},{5,9},{6,10},{7,11},{8,4},{9,5},... | collective-permute-start | bytes 196616 | tf_op jit(solution)/shard_map/ppermute | solution.py:323
  124.5 2.0 %collective-permute-start.16 = (bf16[640,128]{1,0:T(8,128)(2,1)S(1)}, bf16[640,128]{1,0:T(8,128)(2,1)S(1)}, u32[]{:S(2)}, u32[]{:S(2)}) collective-permute-start(bf16[640,128]{1,0:T(8,128)(2,1)S(1)} %get-tuple-element.109), channel_id=1, source_target_pairs={{0,4},{1,5},{2,6},{3,7},{4,0},{5,1},{6,2},{7,3},{8,12},{9,13},{10,... | collective-permute-start | bytes 491528 | tf_op jit(solution)/shard_map/ppermute | solution.py:323
  126.5 1.5 %collective-permute-start.14 = (bf16[640,128]{1,0:T(8,128)(2,1)S(1)}, bf16[640,128]{1,0:T(8,128)(2,1)S(1)}, u32[]{:S(2)}, u32[]{:S(2)}) collective-permute-start(bf16[640,128]{1,0:T(8,128)(2,1)S(1)} %get-tuple-element.105), channel_id=1, source_target_pairs={{0,2},{1,3},{2,0},{3,1},{4,6},{5,7},{6,4},{7,5},{8,10},{9,11},{10,... | collective-permute-start | bytes 491528 | tf_op jit(solution)/shard_map/ppermute | solution.py:323
  128.8 2.6 %collective-permute-start.19 = (bf16[384,128]{1,0:T(8,128)(2,1)S(1)}, bf16[384,128]{1,0:T(8,128)(2,1)S(1)}, u32[]{:S(2)}, u32[]{:S(2)}) collective-permute-start(bf16[384,128]{1,0:T(8,128)(2,1)S(1)} %get-tuple-element.116), channel_id=1, source_target_pairs={{0,14},{1,15},{2,12},{3,13},{4,10},{5,11},{6,8},{7,9},{8,6},{9,7},... | collective-permute-start | bytes 294920 | tf_op jit(solution)/shard_map/ppermute | solution.py:323
  131.3 3.6 %collective-permute-done.21.refs_9_ = bf16[256,128]{1,0:T(8,128)(2,1)S(1)} collective-permute-done((bf16[256,128]{1,0:T(8,128)(2,1)S(1)}, bf16[256,128]{1,0:T(8,128)(2,1)S(1)}, u32[]{:S(2)}, u32[]{:S(2)}) %collective-permute-start.21) | collective-permute-done | bytes 65568 | tf_op jit(solution)/shard_map/ppermute | solution.py:323
  135.0 3.3 %collective-permute-start.20 = (bf16[256,128]{1,0:T(8,128)(2,1)S(1)}, bf16[256,128]{1,0:T(8,128)(2,1)S(1)}, u32[]{:S(2)}, u32[]{:S(2)}) collective-permute-start(bf16[256,128]{1,0:T(8,128)(2,1)S(1)} %get-tuple-element.118), channel_id=1, source_target_pairs={{0,8},{1,9},{2,10},{3,11},{4,12},{5,13},{6,14},{7,15},{8,0},{9,1},... | collective-permute-start | bytes 196616 | tf_op jit(solution)/shard_map/ppermute | solution.py:323
  138.3 2.5 %collective-permute-done.20.refs_8_ = bf16[256,128]{1,0:T(8,128)(2,1)S(1)} collective-permute-done((bf16[256,128]{1,0:T(8,128)(2,1)S(1)}, bf16[256,128]{1,0:T(8,128)(2,1)S(1)}, u32[]{:S(2)}, u32[]{:S(2)}) %collective-permute-start.20) | collective-permute-done | bytes 65568 | tf_op jit(solution)/shard_map/ppermute | solution.py:323
  140.8 1.9 %unpack.1 = bf16[128,40,128]{2,1,0:T(8,128)(2,1)} custom-call(s32[1]{0:T(128)} %bitcast.me_ref, bf16[640,128]{1,0:T(8,128)(2,1)S(1)} %get-tuple-element.103.refs_0_, bf16[640,128]{1,0:T(8,128)(2,1)S(1)} %collective-permute-done.14.refs_1_, bf16[640,128]{1,0:T(8,128)(2,1)S(1)} %collective-permute-done.16.refs_2_, ...), custom_call_target="tpu_custom_call" | custom-call | bytes 4194304 | tf_op jit(solution)/shard_map/unpack/pallas_call | solution.py:302
  (37 shorter events, 4.1 us)
Async XLA Ops:
  5.9 13.3 %copy-start.3 = (bf16[3,656,128]{2,1,0:T(8,128)(2,1)S(1)}, bf16[3,656,128]{2,1,0:T(8,128)(2,1)}, u32[]{:S(2)}) copy-start(bf16[3,656,128]{2,1,0:T(8,128)(2,1)} %get-tuple-element.66) | copy-start | bytes 1511428
  5.9 13.8 %copy-start.2 = (bf16[3,656,128]{2,1,0:T(8,128)(2,1)S(1)}, bf16[3,656,128]{2,1,0:T(8,128)(2,1)}, u32[]{:S(2)}) copy-start(bf16[3,656,128]{2,1,0:T(8,128)(2,1)} %get-tuple-element.67) | copy-start | bytes 1511428
  5.9 27.6 %copy-start.1 = (bf16[3,656,128]{2,1,0:T(8,128)(2,1)S(1)}, bf16[3,656,128]{2,1,0:T(8,128)(2,1)}, u32[]{:S(2)}) copy-start(bf16[3,656,128]{2,1,0:T(8,128)(2,1)} %get-tuple-element.68) | copy-start | bytes 1511428
  6.0 65.3 %copy-start = (bf16[3,656,128]{2,1,0:T(8,128)(2,1)S(1)}, bf16[3,656,128]{2,1,0:T(8,128)(2,1)}, u32[]{:S(2)}) copy-start(bf16[3,656,128]{2,1,0:T(8,128)(2,1)} %get-tuple-element.92.refs_0_) | copy-start | bytes 1511428
  6.0 27.6 %collective-permute-start.3 = (bf16[3,272,128]{2,1,0:T(8,128)(2,1)}, bf16[3,272,128]{2,1,0:T(8,128)(2,1)S(1)}, u32[]{:S(2)}, u32[]{:S(2)}) collective-permute-start(bf16[3,272,128]{2,1,0:T(8,128)(2,1)} %get-tuple-element.69), channel_id=1, source_target_pairs={{0,8},{1,9},{2,10},{3,11},{4,12},{5,13},{6,14},{7,15},{8,0},{9,1},... | collective-permute-start | bytes 626696 | tf_op jit(solution)/shard_map/ppermute | solution.py:323
  15.3 25.3 %collective-permute-start.4 = (bf16[3,400,128]{2,1,0:T(8,128)(2,1)}, bf16[3,400,128]{2,1,0:T(8,128)(2,1)S(1)}, u32[]{:S(2)}, u32[]{:S(2)}) collective-permute-start(bf16[3,400,128]{2,1,0:T(8,128)(2,1)} %get-tuple-element.71), channel_id=1, source_target_pairs={{0,8},{1,9},{2,10},{3,11},{4,12},{5,13},{6,14},{7,15},{8,0},{9,1},... | collective-permute-start | bytes 921608 | tf_op jit(solution)/shard_map/ppermute | solution.py:323
  15.5 33.0 %collective-permute-start.6 = (bf16[3,400,128]{2,1,0:T(8,128)(2,1)}, bf16[3,400,128]{2,1,0:T(8,128)(2,1)S(1)}, u32[]{:S(2)}, u32[]{:S(2)}) collective-permute-start(bf16[3,400,128]{2,1,0:T(8,128)(2,1)} %get-tuple-element.74), channel_id=1, source_target_pairs={{0,10},{1,11},{2,8},{3,9},{4,14},{5,15},{6,12},{7,13},{8,2},{9,3},... | collective-permute-start | bytes 921608 | tf_op jit(solution)/shard_map/ppermute | solution.py:323
  19.2 49.5 %collective-permute-start = (bf16[3,656,128]{2,1,0:T(8,128)(2,1)S(1)}, bf16[3,656,128]{2,1,0:T(8,128)(2,1)S(1)}, u32[]{:S(2)}, u32[]{:S(2)}) collective-permute-start(bf16[3,656,128]{2,1,0:T(8,128)(2,1)S(1)} %copy-done.3), channel_id=1, source_target_pairs={{0,2},{1,3},{2,0},{3,1},{4,6},{5,7},{6,4},{7,5},{8,10},{9,11},{10,... | collective-permute-start | bytes 1511432 | tf_op jit(solution)/shard_map/ppermute | solution.py:323
  19.7 49.0 %collective-permute-start.1 = (bf16[3,656,128]{2,1,0:T(8,128)(2,1)S(1)}, bf16[3,656,128]{2,1,0:T(8,128)(2,1)S(1)}, u32[]{:S(2)}, u32[]{:S(2)}) collective-permute-start(bf16[3,656,128]{2,1,0:T(8,128)(2,1)S(1)} %copy-done.2), channel_id=1, source_target_pairs={{0,4},{1,5},{2,6},{3,7},{4,0},{5,1},{6,2},{7,3},{8,12},{9,13},{10,... | collective-permute-start | bytes 1511432 | tf_op jit(solution)/shard_map/ppermute | solution.py:323
  33.6 37.7 %collective-permute-start.2 = (bf16[3,656,128]{2,1,0:T(8,128)(2,1)S(1)}, bf16[3,656,128]{2,1,0:T(8,128)(2,1)S(1)}, u32[]{:S(2)}, u32[]{:S(2)}) collective-permute-start(bf16[3,656,128]{2,1,0:T(8,128)(2,1)S(1)} %copy-done.1), channel_id=1, source_target_pairs={{0,6},{1,7},{2,4},{3,5},{4,2},{5,3},{6,0},{7,1},{8,14},{9,15},{10,... | collective-permute-start | bytes 1511432 | tf_op jit(solution)/shard_map/ppermute | solution.py:323
  40.6 21.9 %collective-permute-start.8 = (bf16[3,400,128]{2,1,0:T(8,128)(2,1)}, bf16[3,400,128]{2,1,0:T(8,128)(2,1)S(1)}, u32[]{:S(2)}, u32[]{:S(2)}) collective-permute-start(bf16[3,400,128]{2,1,0:T(8,128)(2,1)} %get-tuple-element.77), channel_id=1, source_target_pairs={{0,12},{1,13},{2,14},{3,15},{4,8},{5,9},{6,10},{7,11},{8,4},{9,5},... | collective-permute-start | bytes 921608 | tf_op jit(solution)/shard_map/ppermute | solution.py:323
  48.4 20.2 %collective-permute-start.9 = (bf16[3,400,128]{2,1,0:T(8,128)(2,1)}, bf16[3,400,128]{2,1,0:T(8,128)(2,1)S(1)}, u32[]{:S(2)}, u32[]{:S(2)}) collective-permute-start(bf16[3,400,128]{2,1,0:T(8,128)(2,1)} %get-tuple-element.78), channel_id=1, source_target_pairs={{0,14},{1,15},{2,12},{3,13},{4,10},{5,11},{6,8},{7,9},{8,6},{9,7},... | collective-permute-start | bytes 921608 | tf_op jit(solution)/shard_map/ppermute | solution.py:323
  71.2 1.2 copy-start.6
  71.2 4.9 %copy-start.5 = (bf16[3,272,128]{2,1,0:T(8,128)(2,1)S(1)}, bf16[3,272,128]{2,1,0:T(8,128)(2,1)}, u32[]{:S(2)}) copy-start(bf16[3,272,128]{2,1,0:T(8,128)(2,1)} %get-tuple-element.72) | copy-start | bytes 626692
  72.3 5.2 %collective-permute-start.10 = (bf16[8,2,384,128]{3,2,1,0:T(8,128)(2,1)S(1)}, bf16[8,2,384,128]{3,2,1,0:T(8,128)(2,1)S(1)}, u32[]{:S(2)}, u32[]{:S(2)}) collective-permute-start(bf16[8,2,384,128]{3,2,1,0:T(8,128)(2,1)S(1)} %gather_keys.2), channel_id=1, source_target_pairs={{0,1},{1,0},{2,3},{3,2},{4,5},{5,4},{6,7},{7,6},{8,9},{9,8},{10,11... | collective-permute-start | bytes 4718600 | tf_op jit(solution)/shard_map/ppermute | solution.py:349
  72.4 14.5 %copy-start.4 = (bf16[3,272,128]{2,1,0:T(8,128)(2,1)S(1)}, bf16[3,272,128]{2,1,0:T(8,128)(2,1)}, u32[]{:S(2)}) copy-start(bf16[3,272,128]{2,1,0:T(8,128)(2,1)} %get-tuple-element.89) | copy-start | bytes 626692
  72.4 19.3 %collective-permute-start.7 = (bf16[3,272,128]{2,1,0:T(8,128)(2,1)S(1)}, bf16[3,272,128]{2,1,0:T(8,128)(2,1)S(1)}, u32[]{:S(2)}, u32[]{:S(2)}) collective-permute-start(bf16[3,272,128]{2,1,0:T(8,128)(2,1)S(1)} %copy-done.6), channel_id=1, source_target_pairs={{0,12},{1,13},{2,14},{3,15},{4,8},{5,9},{6,10},{7,11},{8,4},{9,5},... | collective-permute-start | bytes 626696 | tf_op jit(solution)/shard_map/ppermute | solution.py:323
  76.1 25.7 %collective-permute-start.5 = (bf16[3,272,128]{2,1,0:T(8,128)(2,1)S(1)}, bf16[3,272,128]{2,1,0:T(8,128)(2,1)S(1)}, u32[]{:S(2)}, u32[]{:S(2)}) collective-permute-start(bf16[3,272,128]{2,1,0:T(8,128)(2,1)S(1)} %copy-done.5), channel_id=1, source_target_pairs={{0,10},{1,11},{2,8},{3,9},{4,14},{5,15},{6,12},{7,13},{8,2},{9,3},... | collective-permute-start | bytes 626696 | tf_op jit(solution)/shard_map/ppermute | solution.py:323
  86.9 14.9 %collective-permute-start.11 = (bf16[3,272,128]{2,1,0:T(8,128)(2,1)S(1)}, bf16[3,272,128]{2,1,0:T(8,128)(2,1)S(1)}, u32[]{:S(2)}, u32[]{:S(2)}) collective-permute-start(bf16[3,272,128]{2,1,0:T(8,128)(2,1)S(1)} %copy-done.4), channel_id=1, source_target_pairs={{0,14},{1,15},{2,12},{3,13},{4,10},{5,11},{6,8},{7,9},{8,6},{9,7},... | collective-permute-start | bytes 626696 | tf_op jit(solution)/shard_map/ppermute | solution.py:323
  90.8 11.0 %collective-permute-start.12 = (bf16[384,128]{1,0:T(8,128)(2,1)S(1)}, bf16[384,128]{1,0:T(8,128)(2,1)S(1)}, u32[]{:S(2)}, u32[]{:S(2)}) collective-permute-start(bf16[384,128]{1,0:T(8,128)(2,1)S(1)} %get-tuple-element.91), channel_id=1, source_target_pairs={{0,12},{1,13},{2,14},{3,15},{4,8},{5,9},{6,10},{7,11},{8,4},{9,5},... | collective-permute-start | bytes 294920 | tf_op jit(solution)/shard_map/ppermute | solution.py:323
  102.5 9.5 %collective-permute-start.13 = (bf16[8,2,256,128]{3,2,1,0:T(8,128)(2,1)S(1)}, bf16[8,2,256,128]{3,2,1,0:T(8,128)(2,1)S(1)}, u32[]{:S(2)}, u32[]{:S(2)}) collective-permute-start(bf16[8,2,256,128]{3,2,1,0:T(8,128)(2,1)S(1)} %gather_keys.3), channel_id=1, source_target_pairs={{0,1},{1,0},{2,3},{3,2},{4,5},{5,4},{6,7},{7,6},{8,9},{9,8},{10,11... | collective-permute-start | bytes 3145736 | tf_op jit(solution)/shard_map/ppermute | solution.py:349
  102.7 17.1 %collective-permute-start.18 = (bf16[384,128]{1,0:T(8,128)(2,1)S(1)}, bf16[384,128]{1,0:T(8,128)(2,1)S(1)}, u32[]{:S(2)}, u32[]{:S(2)}) collective-permute-start(bf16[384,128]{1,0:T(8,128)(2,1)S(1)} %get-tuple-element.113), channel_id=1, source_target_pairs={{0,10},{1,11},{2,8},{3,9},{4,14},{5,15},{6,12},{7,13},{8,2},{9,3},... | collective-permute-start | bytes 294920 | tf_op jit(solution)/shard_map/ppermute | solution.py:323
  111.9 9.8 %collective-permute-start.15 = (bf16[384,128]{1,0:T(8,128)(2,1)S(1)}, bf16[384,128]{1,0:T(8,128)(2,1)S(1)}, u32[]{:S(2)}, u32[]{:S(2)}) collective-permute-start(bf16[384,128]{1,0:T(8,128)(2,1)S(1)} %get-tuple-element.108), channel_id=1, source_target_pairs={{0,8},{1,9},{2,10},{3,11},{4,12},{5,13},{6,14},{7,15},{8,0},{9,1},... | collective-permute-start | bytes 294920 | tf_op jit(solution)/shard_map/ppermute | solution.py:323
  119.7 8.2 %collective-permute-start.23 = (bf16[256,128]{1,0:T(8,128)(2,1)S(1)}, bf16[256,128]{1,0:T(8,128)(2,1)S(1)}, u32[]{:S(2)}, u32[]{:S(2)}) collective-permute-start(bf16[256,128]{1,0:T(8,128)(2,1)S(1)} %get-tuple-element.124), channel_id=1, source_target_pairs={{0,14},{1,15},{2,12},{3,13},{4,10},{5,11},{6,8},{7,9},{8,6},{9,7},... | collective-permute-start | bytes 196616 | tf_op jit(solution)/shard_map/ppermute | solution.py:323
  121.7 7.1 %collective-permute-start.22 = (bf16[256,128]{1,0:T(8,128)(2,1)S(1)}, bf16[256,128]{1,0:T(8,128)(2,1)S(1)}, u32[]{:S(2)}, u32[]{:S(2)}) collective-permute-start(bf16[256,128]{1,0:T(8,128)(2,1)S(1)} %get-tuple-element.122), channel_id=1, source_target_pairs={{0,12},{1,13},{2,14},{3,15},{4,8},{5,9},{6,10},{7,11},{8,4},{9,5},... | collective-permute-start | bytes 196616 | tf_op jit(solution)/shard_map/ppermute | solution.py:323
  124.5 16.3 %collective-permute-start.17 = (bf16[640,128]{1,0:T(8,128)(2,1)S(1)}, bf16[640,128]{1,0:T(8,128)(2,1)S(1)}, u32[]{:S(2)}, u32[]{:S(2)}) collective-permute-start(bf16[640,128]{1,0:T(8,128)(2,1)S(1)} %get-tuple-element.111), channel_id=1, source_target_pairs={{0,6},{1,7},{2,4},{3,5},{4,2},{5,3},{6,0},{7,1},{8,14},{9,15},{10,... | collective-permute-start | bytes 491528 | tf_op jit(solution)/shard_map/ppermute | solution.py:323
  124.5 16.3 %collective-permute-start.16 = (bf16[640,128]{1,0:T(8,128)(2,1)S(1)}, bf16[640,128]{1,0:T(8,128)(2,1)S(1)}, u32[]{:S(2)}, u32[]{:S(2)}) collective-permute-start(bf16[640,128]{1,0:T(8,128)(2,1)S(1)} %get-tuple-element.109), channel_id=1, source_target_pairs={{0,4},{1,5},{2,6},{3,7},{4,0},{5,1},{6,2},{7,3},{8,12},{9,13},{10,... | collective-permute-start | bytes 491528 | tf_op jit(solution)/shard_map/ppermute | solution.py:323
  126.5 14.3 %collective-permute-start.14 = (bf16[640,128]{1,0:T(8,128)(2,1)S(1)}, bf16[640,128]{1,0:T(8,128)(2,1)S(1)}, u32[]{:S(2)}, u32[]{:S(2)}) collective-permute-start(bf16[640,128]{1,0:T(8,128)(2,1)S(1)} %get-tuple-element.105), channel_id=1, source_target_pairs={{0,2},{1,3},{2,0},{3,1},{4,6},{5,7},{6,4},{7,5},{8,10},{9,11},{10,... | collective-permute-start | bytes 491528 | tf_op jit(solution)/shard_map/ppermute | solution.py:323
  128.0 7.0 %collective-permute-start.21 = (bf16[256,128]{1,0:T(8,128)(2,1)S(1)}, bf16[256,128]{1,0:T(8,128)(2,1)S(1)}, u32[]{:S(2)}, u32[]{:S(2)}) collective-permute-start(bf16[256,128]{1,0:T(8,128)(2,1)S(1)} %get-tuple-element.120), channel_id=1, source_target_pairs={{0,10},{1,11},{2,8},{3,9},{4,14},{5,15},{6,12},{7,13},{8,2},{9,3},... | collective-permute-start | bytes 196616 | tf_op jit(solution)/shard_map/ppermute | solution.py:323
  128.8 12.0 %collective-permute-start.19 = (bf16[384,128]{1,0:T(8,128)(2,1)S(1)}, bf16[384,128]{1,0:T(8,128)(2,1)S(1)}, u32[]{:S(2)}, u32[]{:S(2)}) collective-permute-start(bf16[384,128]{1,0:T(8,128)(2,1)S(1)} %get-tuple-element.116), channel_id=1, source_target_pairs={{0,14},{1,15},{2,12},{3,13},{4,10},{5,11},{6,8},{7,9},{8,6},{9,7},... | collective-permute-start | bytes 294920 | tf_op jit(solution)/shard_map/ppermute | solution.py:323
  135.0 5.8 %collective-permute-start.20 = (bf16[256,128]{1,0:T(8,128)(2,1)S(1)}, bf16[256,128]{1,0:T(8,128)(2,1)S(1)}, u32[]{:S(2)}, u32[]{:S(2)}) collective-permute-start(bf16[256,128]{1,0:T(8,128)(2,1)S(1)} %get-tuple-element.118), channel_id=1, source_target_pairs={{0,8},{1,9},{2,10},{3,11},{4,12},{5,13},{6,14},{7,15},{8,0},{9,1},... | collective-permute-start | bytes 196616 | tf_op jit(solution)/shard_map/ppermute | solution.py:323

commit v4 on v3

--- a/solution.py
+++ b/solution.py
@@ -11,19 +11,19 @@
 F32, BF16, I32 = jnp.float32, jnp.bfloat16, jnp.int32
 DEAD = -1e30
 VMEM_BYTES = 48 << 20
-PACK_BYTES = 60 << 20
-MIX_BACK = True
 INFO_ROWS = 16
 GROUP = 4
+CUT = 3
 WINDOW = 8
 LATE_A = 3
 SEEN_A = 0
-LATE_B = 3
-SEEN_B = 2
-
-
-def params(limit=VMEM_BYTES):
-    return pltpu.CompilerParams(vmem_limit_bytes=limit)
+LATE_B = 5
+SEEN_B = 1
+WINDOW_LAST = 99
+
+
+def params():
+    return pltpu.CompilerParams(vmem_limit_bytes=VMEM_BYTES)
 
 
 def cost(flops, count):
@@ -41,7 +41,7 @@
         assert lists * self.bits + lists.bit_length() < 31 and lists < INFO_ROWS
         self.near = list(range(max(1, self.chips // 2)))
         self.far = list(range(len(self.near), self.chips))
-        cut = -(-self.per_chip * 3 // 5)
+        cut = -(-self.per_chip * CUT // 5)
         self.pieces = [(0, cut)]
         if cut < self.per_chip:
             self.pieces.append((cut, self.per_chip - cut))
@@ -112,7 +112,7 @@
             ],
         ),
         out_shape=[jax.ShapeDtypeStruct((kinds, d, dim), BF16) for d in depths],
-        compiler_params=params(PACK_BYTES),
+        compiler_params=params(),
         cost_estimate=cost(0, 8 << 20),
         name="pack",
     )(me, by_kind, block_ids, counts)
@@ -165,40 +165,45 @@
     return [(m / t).astype(BF16) for m, t in zip(mixed, totals)]
 
 
-def attend_kernel(plan, piece, scale, held_rows, me_ref, *refs):
+def attend_kernel(plan, piece, scale, me_ref, *refs):
     chips, rows, lists, bits = plan.chips, plan.rows, plan.lists, plan.bits
     first, size = piece
-    near, far_ref, refs = refs[:chips], refs[chips], refs[chips + 1 :]
-    helds = refs[: len(plan.near)] if held_rows else []
-    refs = refs[len(helds) :]
-    outs, refs = refs[:chips], refs[chips:]
-    queries, keys, values, info, bias, code, scalars, sem = refs
+    came, mine_ref, far_ref, refs = refs[:chips], refs[chips], refs[chips + 1], refs[chips + 2 :]
+    outs, (queries, pairs, info, bias, code, scalars, sem, slot_sem) = refs[:chips], refs[chips:]
     chip, core = me_ref[0] // 2, me_ref[0] % 2
 
-    copies = []
-    for step, (ref, (begin, end)) in enumerate(zip(near, spans_of(plan, piece))):
+    info_copies, query_copies = [], []
+    for step, (ref, (begin, end)) in enumerate(zip(came, spans_of(plan, piece))):
         last = ref.shape[1] - INFO_ROWS
-        moves = [
-            (ref.at[0, last:], info.at[step]),
-            (ref.at[0, begin:end], queries.at[step]),
-            (ref.at[1, begin:end], keys.at[2 * step]),
-            (ref.at[2, begin:end], values.at[2 * step]),
-            (far_ref.at[step, 0], keys.at[2 * step + 1]),
-            (far_ref.at[step, 1], values.at[2 * step + 1]),
+        info_copies.append(
+            pltpu.make_async_copy(ref.at[0, last:], info.at[step], sem.at[0, step])
+        )
+        query_copies.append(
+            pltpu.make_async_copy(ref.at[0, begin:end], queries.at[step], sem.at[1, step])
+        )
+
+    def span_of(slot):
+        return pl.ds(pl.multiple_of(slot * rows, rows), rows)
+
+    def pair_copies(slot):
+        span = span_of(slot)
+        return [
+            pltpu.make_async_copy(
+                ref.at[:, :, span], pairs.at[at, :, :, span], slot_sem.at[at, slot]
+            )
+            for at, ref in enumerate((mine_ref, far_ref))
         ]
-        copies += [
-            pltpu.make_async_copy(source, target, sem.at[step, at])
-            for at, (source, target) in enumerate(moves)
-        ]
-    for copy in copies:
+
+    for copy in info_copies + query_copies:
         copy.start()
+    for slot in range(size):
+        for copy in pair_copies(slot):
+            copy.start()
 
     count = lax.broadcasted_iota(I32, bias.shape, 0)
     entry = lax.broadcasted_iota(I32, bias.shape, 1) // rows
     bias[...] = jnp.where((entry < count) | (entry == 0), 0.0, DEAD).astype(F32)
-    for held, out in zip(helds, outs):
-        out[:held_rows, :] = held[...]
-    for copy in copies:
+    for copy in info_copies:
         copy.wait()
 
     for step in range(chips):
@@ -210,65 +215,64 @@
     copy = pltpu.make_async_copy(code, scalars, sem.at[0, 0])
     copy.start()
     copy.wait()
+    for copy in query_copies:
+        copy.wait()
 
     mask = (1 << bits) - 1
-
-    def place(block):
-        return ((block // 2) ^ chip) * 2 + ((block % 2) ^ core)
 
     def one_slot(slot, carry):
         head = jnp.minimum(plan.head(chip, first + slot), plan.heads - 1)
-        span = pl.ds(pl.multiple_of(slot * rows, rows), rows)
-        below = pl.ds(pl.multiple_of(held_rows + slot * rows, rows), rows)
+        span = span_of(slot)
+        for copy in pair_copies(slot):
+            copy.wait()
+
+        def pick(block, kind):
+            return pairs[(block % 2) ^ core, (block // 2) ^ chip, kind, span, :]
+
         for start in range(0, chips, GROUP):
             steps, units = range(start, min(start + GROUP, chips)), []
             for step in steps:
                 number = scalars[step, head]
-                places = [place((number >> (j * bits)) & mask) for j in range(lists)]
+                blocks = [(number >> (j * bits)) & mask for j in range(lists)]
                 live = number >> (lists * bits)
                 units.append(
                     (
                         queries[step, span, :],
-                        jnp.concatenate([keys[c, span, :] for c in places], axis=0),
-                        jnp.concatenate([values[c, span, :] for c in places], axis=0),
+                        jnp.concatenate([pick(block, 0) for block in blocks], axis=0),
+                        jnp.concatenate([pick(block, 1) for block in blocks], axis=0),
                         bias[pl.ds(live, 1), :],
                     )
                 )
             for step, result in zip(steps, attend_group(units, scale)):
-                outs[step][below if step in plan.near else span, :] = result
+                outs[step][span, :] = result
         return carry
 
     lax.fori_loop(0, size, one_slot, 0)
 
 
-def attend(plan, piece, me, came, far, helds, scale):
+def attend(plan, piece, me, came, mine, far, scale):
     chips, dim, depth = plan.chips, plan.dim, piece[1] * plan.rows
-    held_rows = helds[0].shape[0] if helds else 0
     bias_rows = -(-(plan.lists + 1) // 8) * 8
-    any_spec = pl.BlockSpec(memory_space=pl.ANY)
-    vmem_spec = pl.BlockSpec(memory_space=pltpu.VMEM)
-    depths = [depth + (held_rows if step in plan.near else 0) for step in range(chips)]
     return pl.pallas_call(
-        functools.partial(attend_kernel, plan, piece, scale, held_rows),
+        functools.partial(attend_kernel, plan, piece, scale),
         in_specs=[pl.BlockSpec(memory_space=pltpu.SMEM)]
-        + [any_spec] * (chips + 1)
-        + [vmem_spec] * len(helds),
-        out_specs=[vmem_spec] * chips,
-        out_shape=[jax.ShapeDtypeStruct((d, dim), BF16) for d in depths],
+        + [pl.BlockSpec(memory_space=pl.ANY)] * (chips + 2),
+        out_specs=[pl.BlockSpec(memory_space=pltpu.VMEM)] * chips,
+        out_shape=[jax.ShapeDtypeStruct((depth, dim), BF16)] * chips,
         scratch_shapes=[
             pltpu.VMEM((chips, depth, dim), BF16),
-            pltpu.VMEM((2 * chips, depth, dim), BF16),
-            pltpu.VMEM((2 * chips, depth, dim), BF16),
+            pltpu.VMEM((2, chips, 2, depth, dim), BF16),
             pltpu.VMEM((chips, INFO_ROWS, dim), BF16),
             pltpu.VMEM((bias_rows, plan.lists * plan.rows), F32),
             pltpu.VMEM((chips, dim), I32),
             pltpu.SMEM((chips, dim), I32),
-            pltpu.SemaphoreType.DMA((chips, 6)),
+            pltpu.SemaphoreType.DMA((2, chips)),
+            pltpu.SemaphoreType.DMA((2, piece[1])),
         ],
         compiler_params=params(),
         cost_estimate=cost(4 << 30, 8 << 20),
         name="attend",
-    )(me, *came, far, *helds)
+    )(me, *came, mine, far)
 
 
 def unpack_kernel(plan, items, me_ref, *refs):
@@ -315,11 +319,11 @@
     def __init__(self, seq):
         self.seq, self.ended = seq, []
 
-    def send(self, array, step, after=None):
+    def send(self, array, step, after=None, window=WINDOW):
         if after is not None:
             array, _ = lax.optimization_barrier((array, after))
-        if len(self.ended) >= WINDOW:
-            array, _ = lax.optimization_barrier((array, self.ended[-WINDOW]))
+        if len(self.ended) >= window:
+            array, _ = lax.optimization_barrier((array, self.ended[-window]))
         got = lax.ppermute(array, "seq", [(d, d ^ (2 * step)) for d in range(self.seq)])
         self.ended.append(got)
         return got
@@ -342,12 +346,12 @@
     near, far, pieces = plan.near, plan.far, plan.pieces
     sender = Sender(seq)
 
-    def work(piece, came, helds, sent):
+    def work(piece, came, sent):
         if sent is not None:
             came, _ = lax.optimization_barrier((came, sent))
-        swapped = gather_keys(plan, piece, came)
-        swapped = lax.ppermute(swapped, "seq", [(d, d ^ 1) for d in range(seq)])
-        return attend(plan, piece, me, came, swapped, helds, scale)
+        mine = gather_keys(plan, piece, came)
+        swapped = lax.ppermute(mine, "seq", [(d, d ^ 1) for d in range(seq)])
+        return attend(plan, piece, me, came, mine, swapped, scale)
 
     far_items = [[(step, *piece) for step in far] for piece in pieces]
     near_items = [(step, 0, plan.per_chip) for step in near]
@@ -358,24 +362,31 @@
     got = {step: sender.send(leaving[step], step) for step in mixed(far, near)}
     got[0] = rest[0]
     came = [got[step] for step in range(plan.chips)]
-    backs = []
+    items, backs = [], []
+
+    def keep(piece, got):
+        items.extend((step, *piece) for step in range(plan.chips))
+        backs.extend(got[step] for step in range(plan.chips))
+
     if len(pieces) == 1:
-        outs = work(pieces[0], came, [], None)
+        outs = work(pieces[0], came, None)
     else:
         last = rest[len(near) :]
         got = [sender.send(a, step) for a, step in zip(last[:LATE_A], far)]
-        held = work(pieces[0], came, [], got[SEEN_A])
+        held = work(pieces[0], came, got[SEEN_A])
         got += [sender.send(a, step, held[0]) for a, step in zip(last[LATE_A:], far[LATE_A:])]
         came = came[: len(near)] + got
-        leaving = held[len(near) :]
-        got = [sender.send(a, step) for a, step in zip(leaving[:LATE_B], far)]
-        outs = work(pieces[1], came, held[: len(near)], got[SEEN_B])
-        got += [sender.send(a, step, outs[0]) for a, step in zip(leaving[LATE_B:], far[LATE_B:])]
-        backs += got
-    got = {step: sender.send(outs[step], step) for step in (mixed(far, near) if MIX_BACK else far + near[1:])}
-    got[0] = outs[0]
-    items = near_items + (far_items[0] if len(pieces) > 1 else []) + far_items[-1]
-    backs = [got[step] for step in near] + backs + [got[step] for step in far]
+        got, order = {0: held[0]}, mixed(far, near)
+        for step in order[:LATE_B]:
+            got[step] = sender.send(held[step], step)
+        outs = work(pieces[1], came, got[order[SEEN_B]])
+        for step in order[LATE_B:]:
+            got[step] = sender.send(held[step], step, outs[0])
+        keep(pieces[0], got)
+    got = {0: outs[0]}
+    for step in mixed(far, near):
+        got[step] = sender.send(outs[step], step, window=WINDOW_LAST)
+    keep(pieces[-1], got)
     return unpack(plan, items, me, backs)
 
 

time: 143 us -> 141 us (0.986)
  Pallas kernels: 31 us -> 18.8 us
  waiting for transfers between devices: 62 us -> 73.8 us
  starting transfers between devices: 49.6 us -> 46 us
  local copies, waits for them, and re-layouts: 0.03 us -> 2.52 us
    ppermute x22 -> x25, waiting for transfers between devices: 62 us -> 73.8 us  [send(): lax.ppermute(array, 'seq', [(d, d ^ 2 * step) for d in range(self.seq)])]
    pallas_call x2, Pallas kernels: 16.1 us -> 9.04 us  [attend(): pl.pallas_call(functools.partial(attend_kernel, plan, piece, scale), in_s...]
    pallas_call x2, Pallas kernels: 11.1 us -> 5.99 us  [pack(): pl.pallas_call(functools.partial(pack_kernel, plan, items), grid_spec=plt...]
    ppermute x22 -> x25, starting transfers between devices: 49.4 us -> 45.8 us  [send(): lax.ppermute(array, 'seq', [(d, d ^ 2 * step) for d in range(self.seq)])]
    unnamed x14 -> x8, local copies, waits for them, and re-layouts: 0.03 us -> 2.52 us
  transfers between devices with their start and end apart: 24 -> 27, of which waited for: 12 -> 10; matrix products, arithmetic and copies ran while one was open for 0% -> 0% of each run, Pallas kernels for 15% -> 8%
where the time goes in v4:
time: 141 us
  waiting for transfers between devices  73.8 us (52%)
  starting transfers between devices  46 us (33%)
  Pallas kernels  18.8 us (13%)
  local copies, waits for them, and re-layouts  2.52 us (2%)
    ppermute x25, waiting for transfers between devices, send(): lax.ppermute(array, 'seq', [(d, d ^ 2 * step) for d in range(self.seq)])  73.8 us
    ppermute x25, starting transfers between devices, send(): lax.ppermute(array, 'seq', [(d, d ^ 2 * step) for d in range(self.seq)])  45.8 us
    pallas_call x2, Pallas kernels, attend(): pl.pallas_call(functools.partial(attend_kernel, plan, piece, scale), in_s...  9.04 us
    pallas_call x2, Pallas kernels, pack(): pl.pallas_call(functools.partial(pack_kernel, plan, items), grid_spec=plt...  5.99 us
  transfers between devices with their start and end apart: 27, of which 10 were waited for; matrix products, arithmetic and copies ran while one was open for 0% of the time, Pallas kernels for 8%

profile of v4, /device:TPU:0, one launch (start us, length us, event | category | flops | bytes accessed | tf_op | source)
XLA Modules:
  0.0 141.2 jit_solution(16001007489168238611)
XLA Ops:
  1.3 4.3 %pack.2 = (bf16[3,656,128]{2,1,0:T(8,128)(2,1)S(1)}, bf16[3,656,128]{2,1,0:T(8,128)(2,1)S(1)}, bf16[3,656,128]{2,1,0:T(8,128)(2,1)S(1)}, bf16[3,656,128]{2,1,0:T...) custom-call(s32[1]{0:T(128)} %bitcast.me_ref, ...), custom_call_target="tpu_custom_call" | custom-call | bytes 8388608 | tf_op jit(solution)/shard_map/pack/pallas_call | solution.py:95
  5.6 4.1 %collective-permute-start.7 = (bf16[3,272,128]{2,1,0:T(8,128)(2,1)S(1)}, bf16[3,272,128]{2,1,0:T(8,128)(2,1)S(1)}, u32[]{:S(2)}, u32[]{:S(2)}) collective-permute-start(bf16[3,272,128]{2,1,0:T(8,128)(2,1)S(1)} %get-tuple-element.70), channel_id=1, source_target_pairs={{0,8},{1,9},{2,10},{3,11},{4,12},{5,13},{6,14},{7,15},{8,0},{9,1},... | collective-permute-start | bytes 626696 | tf_op jit(solution)/shard_map/ppermute | solution.py:327
  9.7 1.7 %pack.3 = (bf16[3,400,128]{2,1,0:T(8,128)(2,1)S(1)}, bf16[3,400,128]{2,1,0:T(8,128)(2,1)S(1)}, bf16[3,400,128]{2,1,0:T(8,128)(2,1)S(1)}, bf16[3,400,128]{2,1,0:T(8,128)(2,1)S(1)}) custom-call(s32[1]{0:T(128)} %bitcast.me_ref, bf16[128,3,40,128]{3,2,1,0:T(8,128)(2,1)S(1)} %bitcast.4, s32[1,4,40]{2,1,0:T(4,128)S(1)} %bitcast.6, s32[1,40]{1,0:T(1,128)S(1)} %copy-done.2), custom_call_target="tpu_custom_call" | custom-call | bytes 8388608 | tf_op jit(solution)/shard_map/pack/pallas_call | solution.py:95
  11.5 3.8 %collective-permute-start.4 = (bf16[3,400,128]{2,1,0:T(8,128)(2,1)S(1)}, bf16[3,400,128]{2,1,0:T(8,128)(2,1)S(1)}, u32[]{:S(2)}, u32[]{:S(2)}) collective-permute-start(bf16[3,400,128]{2,1,0:T(8,128)(2,1)S(1)} %get-tuple-element.67), channel_id=1, source_target_pairs={{0,10},{1,11},{2,8},{3,9},{4,14},{5,15},{6,12},{7,13},{8,2},{9,3},... | collective-permute-start | bytes 921608 | tf_op jit(solution)/shard_map/ppermute | solution.py:327
  15.9 1.6 %collective-permute-start.1 = (bf16[3,656,128]{2,1,0:T(8,128)(2,1)S(1)}, bf16[3,656,128]{2,1,0:T(8,128)(2,1)S(1)}, u32[]{:S(2)}, u32[]{:S(2)}) collective-permute-start(bf16[3,656,128]{2,1,0:T(8,128)(2,1)S(1)} %get-tuple-element.64), channel_id=1, source_target_pairs={{0,4},{1,5},{2,6},{3,7},{4,0},{5,1},{6,2},{7,3},{8,12},{9,13},{10,... | collective-permute-start | bytes 1511432 | tf_op jit(solution)/shard_map/ppermute | solution.py:327
  17.5 15.9 %collective-permute-done.7.refs_4_ = bf16[3,272,128]{2,1,0:T(8,128)(2,1)S(1)} collective-permute-done((bf16[3,272,128]{2,1,0:T(8,128)(2,1)S(1)}, bf16[3,272,128]{2,1,0:T(8,128)(2,1)S(1)}, u32[]{:S(2)}, u32[]{:S(2)}) %collective-permute-start.7) | collective-permute-done | bytes 208928 | tf_op jit(solution)/shard_map/ppermute | solution.py:327
  34.3 5.7 %collective-permute-done.3.refs_4_ = bf16[3,400,128]{2,1,0:T(8,128)(2,1)S(1)} collective-permute-done((bf16[3,400,128]{2,1,0:T(8,128)(2,1)S(1)}, bf16[3,400,128]{2,1,0:T(8,128)(2,1)S(1)}, u32[]{:S(2)}, u32[]{:S(2)}) %collective-permute-start.3) | collective-permute-done | bytes 307232 | tf_op jit(solution)/shard_map/ppermute | solution.py:327
  40.0 2.8 %collective-permute-start.5 = (bf16[3,400,128]{2,1,0:T(8,128)(2,1)S(1)}, bf16[3,400,128]{2,1,0:T(8,128)(2,1)S(1)}, u32[]{:S(2)}, u32[]{:S(2)}) collective-permute-start(bf16[3,400,128]{2,1,0:T(8,128)(2,1)S(1)} %get-tuple-element.68), channel_id=1, source_target_pairs={{0,12},{1,13},{2,14},{3,15},{4,8},{5,9},{6,10},{7,11},{8,4},{9,5},... | collective-permute-start | bytes 921608 | tf_op jit(solution)/shard_map/ppermute | solution.py:327
  42.8 5.0 %collective-permute-done.4.refs_5_ = bf16[3,400,128]{2,1,0:T(8,128)(2,1)S(1)} collective-permute-done((bf16[3,400,128]{2,1,0:T(8,128)(2,1)S(1)}, bf16[3,400,128]{2,1,0:T(8,128)(2,1)S(1)}, u32[]{:S(2)}, u32[]{:S(2)}) %collective-permute-start.4) | collective-permute-done | bytes 307232 | tf_op jit(solution)/shard_map/ppermute | solution.py:327
  47.9 2.4 %collective-permute-start.6 = (bf16[3,400,128]{2,1,0:T(8,128)(2,1)S(1)}, bf16[3,400,128]{2,1,0:T(8,128)(2,1)S(1)}, u32[]{:S(2)}, u32[]{:S(2)}) collective-permute-start(bf16[3,400,128]{2,1,0:T(8,128)(2,1)S(1)} %get-tuple-element.69), channel_id=1, source_target_pairs={{0,14},{1,15},{2,12},{3,13},{4,10},{5,11},{6,8},{7,9},{8,6},{9,7},... | collective-permute-start | bytes 921608 | tf_op jit(solution)/shard_map/ppermute | solution.py:327
  50.3 8.3 %collective-permute-done.5.refs_6_ = bf16[3,400,128]{2,1,0:T(8,128)(2,1)S(1)} collective-permute-done((bf16[3,400,128]{2,1,0:T(8,128)(2,1)S(1)}, bf16[3,400,128]{2,1,0:T(8,128)(2,1)S(1)}, u32[]{:S(2)}, u32[]{:S(2)}) %collective-permute-start.5) | collective-permute-done | bytes 307232 | tf_op jit(solution)/shard_map/ppermute | solution.py:327
  58.5 6.5 %collective-permute-done.6.refs_7_ = bf16[3,400,128]{2,1,0:T(8,128)(2,1)S(1)} collective-permute-done((bf16[3,400,128]{2,1,0:T(8,128)(2,1)S(1)}, bf16[3,400,128]{2,1,0:T(8,128)(2,1)S(1)}, u32[]{:S(2)}, u32[]{:S(2)}) %collective-permute-start.6) | collective-permute-done | bytes 307232 | tf_op jit(solution)/shard_map/ppermute | solution.py:327
  65.0 5.6 %collective-permute-done.2.refs_3_ = bf16[3,656,128]{2,1,0:T(8,128)(2,1)S(1)} collective-permute-done((bf16[3,656,128]{2,1,0:T(8,128)(2,1)S(1)}, bf16[3,656,128]{2,1,0:T(8,128)(2,1)S(1)}, u32[]{:S(2)}, u32[]{:S(2)}) %collective-permute-start.2) | collective-permute-done | bytes 503840 | tf_op jit(solution)/shard_map/ppermute | solution.py:327
  71.8 3.5 %collective-permute-start.12 = (bf16[3,272,128]{2,1,0:T(8,128)(2,1)S(1)}, bf16[3,272,128]{2,1,0:T(8,128)(2,1)S(1)}, u32[]{:S(2)}, u32[]{:S(2)}) collective-permute-start(bf16[3,272,128]{2,1,0:T(8,128)(2,1)S(1)} %get-tuple-element.88), channel_id=1, source_target_pairs={{0,12},{1,13},{2,14},{3,15},{4,8},{5,9},{6,10},{7,11},{8,4},{9,5},... | collective-permute-start | bytes 626696 | tf_op jit(solution)/shard_map/ppermute | solution.py:327
  75.4 1.6 %collective-permute-start.11 = (bf16[3,272,128]{2,1,0:T(8,128)(2,1)S(1)}, bf16[3,272,128]{2,1,0:T(8,128)(2,1)S(1)}, u32[]{:S(2)}, u32[]{:S(2)}) collective-permute-start(bf16[3,272,128]{2,1,0:T(8,128)(2,1)S(1)} %get-tuple-element.86), channel_id=1, source_target_pairs={{0,10},{1,11},{2,8},{3,9},{4,14},{5,15},{6,12},{7,13},{8,2},{9,3},... | collective-permute-start | bytes 626696 | tf_op jit(solution)/shard_map/ppermute | solution.py:327
  77.0 1.2 copy-done.3
  78.1 5.3 %attend.2 = (bf16[384,128]{1,0:T(8,128)(2,1)S(1)}, bf16[384,128]{1,0:T(8,128)(2,1)S(1)}, bf16[384,128]{1,0:T(8,128)(2,1)S(1)}, bf16[384,128]{1,0:T(8,128)(2,1)S(...) custom-call(s32[1]{0:T(128)} %bitcast.me_ref, ...), custom_call_target="tpu_custom_call" | custom-call | flops 4294967296 | bytes 8388608 | tf_op jit(solution)/shard_map/attend/pallas_call | solution.py:256
  83.5 3.9 %collective-permute-start.13 = (bf16[3,272,128]{2,1,0:T(8,128)(2,1)S(1)}, bf16[3,272,128]{2,1,0:T(8,128)(2,1)S(1)}, u32[]{:S(2)}, u32[]{:S(2)}) collective-permute-start(bf16[3,272,128]{2,1,0:T(8,128)(2,1)S(1)} %get-tuple-element.91), channel_id=1, source_target_pairs={{0,14},{1,15},{2,12},{3,13},{4,10},{5,11},{6,8},{7,9},{8,6},{9,7},... | collective-permute-start | bytes 626696 | tf_op jit(solution)/shard_map/ppermute | solution.py:327
  87.4 13.8 %collective-permute-done.11.refs_5_ = bf16[3,272,128]{2,1,0:T(8,128)(2,1)S(1)} collective-permute-done((bf16[3,272,128]{2,1,0:T(8,128)(2,1)S(1)}, bf16[3,272,128]{2,1,0:T(8,128)(2,1)S(1)}, u32[]{:S(2)}, u32[]{:S(2)}) %collective-permute-start.11) | collective-permute-done | bytes 208928 | tf_op jit(solution)/shard_map/ppermute | solution.py:327
  101.1 6.6 %collective-permute-done.14.refs_5_ = bf16[384,128]{1,0:T(8,128)(2,1)S(1)} collective-permute-done((bf16[384,128]{1,0:T(8,128)(2,1)S(1)}, bf16[384,128]{1,0:T(8,128)(2,1)S(1)}, u32[]{:S(2)}, u32[]{:S(2)}) %collective-permute-start.14) | collective-permute-done | bytes 98336 | tf_op jit(solution)/shard_map/ppermute | solution.py:327
  108.6 3.5 %collective-permute-start.18 = (bf16[384,128]{1,0:T(8,128)(2,1)S(1)}, bf16[384,128]{1,0:T(8,128)(2,1)S(1)}, u32[]{:S(2)}, u32[]{:S(2)}) collective-permute-start(bf16[384,128]{1,0:T(8,128)(2,1)S(1)} %get-tuple-element.108), channel_id=1, source_target_pairs={{0,12},{1,13},{2,14},{3,15},{4,8},{5,9},{6,10},{7,11},{8,4},{9,5},... | collective-permute-start | bytes 294920 | tf_op jit(solution)/shard_map/ppermute | solution.py:327
  113.0 1.6 %collective-permute-start.9 = (bf16[384,128]{1,0:T(8,128)(2,1)S(1)}, bf16[384,128]{1,0:T(8,128)(2,1)S(1)}, u32[]{:S(2)}, u32[]{:S(2)}) collective-permute-start(bf16[384,128]{1,0:T(8,128)(2,1)S(1)} %get-tuple-element.81), channel_id=1, source_target_pairs={{0,2},{1,3},{2,0},{3,1},{4,6},{5,7},{6,4},{7,5},{8,10},{9,11},{10,... | collective-permute-start | bytes 294920 | tf_op jit(solution)/shard_map/ppermute | solution.py:327
  114.6 3.7 %attend.3 = (bf16[256,128]{1,0:T(8,128)(2,1)S(1)}, bf16[256,128]{1,0:T(8,128)(2,1)S(1)}, bf16[256,128]{1,0:T(8,128)(2,1)S(1)}, bf16[256,128]{1,0:T(8,128)(2,1)S(...) custom-call(s32[1]{0:T(128)} %bitcast.me_ref, ...), custom_call_target="tpu_custom_call" | custom-call | flops 4294967296 | bytes 8388608 | tf_op jit(solution)/shard_map/attend/pallas_call | solution.py:256
  120.3 1.5 %collective-permute-start.22 = (bf16[256,128]{1,0:T(8,128)(2,1)S(1)}, bf16[256,128]{1,0:T(8,128)(2,1)S(1)}, u32[]{:S(2)}, u32[]{:S(2)}) collective-permute-start(bf16[256,128]{1,0:T(8,128)(2,1)S(1)} %get-tuple-element.114), channel_id=1, source_target_pairs={{0,6},{1,7},{2,4},{3,5},{4,2},{5,3},{6,0},{7,1},{8,14},{9,15},{10,... | collective-permute-start | bytes 196616 | tf_op jit(solution)/shard_map/ppermute | solution.py:327
  121.8 2.1 %collective-permute-start.23 = (bf16[256,128]{1,0:T(8,128)(2,1)S(1)}, bf16[256,128]{1,0:T(8,128)(2,1)S(1)}, u32[]{:S(2)}, u32[]{:S(2)}) collective-permute-start(bf16[256,128]{1,0:T(8,128)(2,1)S(1)} %get-tuple-element.115), channel_id=1, source_target_pairs={{0,8},{1,9},{2,10},{3,11},{4,12},{5,13},{6,14},{7,15},{8,0},{9,1},... | collective-permute-start | bytes 196616 | tf_op jit(solution)/shard_map/ppermute | solution.py:327
  124.0 1.9 %collective-permute-start.16 = (bf16[384,128]{1,0:T(8,128)(2,1)S(1)}, bf16[384,128]{1,0:T(8,128)(2,1)S(1)}, u32[]{:S(2)}, u32[]{:S(2)}) collective-permute-start(bf16[384,128]{1,0:T(8,128)(2,1)S(1)} %get-tuple-element.104), channel_id=1, source_target_pairs={{0,6},{1,7},{2,4},{3,5},{4,2},{5,3},{6,0},{7,1},{8,14},{9,15},{10,... | collective-permute-start | bytes 294920 | tf_op jit(solution)/shard_map/ppermute | solution.py:327
  125.8 1.3 collective-permute-start.19
  127.1 1.2 collective-permute-start.24
  128.3 2.4 %collective-permute-start.25 = (bf16[256,128]{1,0:T(8,128)(2,1)S(1)}, bf16[256,128]{1,0:T(8,128)(2,1)S(1)}, u32[]{:S(2)}, u32[]{:S(2)}) collective-permute-start(bf16[256,128]{1,0:T(8,128)(2,1)S(1)} %get-tuple-element.117), channel_id=1, source_target_pairs={{0,12},{1,13},{2,14},{3,15},{4,8},{5,9},{6,10},{7,11},{8,4},{9,5},... | collective-permute-start | bytes 196616 | tf_op jit(solution)/shard_map/ppermute | solution.py:327
  130.7 2.5 %collective-permute-start.26 = (bf16[256,128]{1,0:T(8,128)(2,1)S(1)}, bf16[256,128]{1,0:T(8,128)(2,1)S(1)}, u32[]{:S(2)}, u32[]{:S(2)}) collective-permute-start(bf16[256,128]{1,0:T(8,128)(2,1)S(1)} %get-tuple-element.118), channel_id=1, source_target_pairs={{0,14},{1,15},{2,12},{3,13},{4,10},{5,11},{6,8},{7,9},{8,6},{9,7},... | collective-permute-start | bytes 196616 | tf_op jit(solution)/shard_map/ppermute | solution.py:327
  133.2 6.1 %collective-permute-done.24.refs_13_ = bf16[256,128]{1,0:T(8,128)(2,1)S(1)} collective-permute-done((bf16[256,128]{1,0:T(8,128)(2,1)S(1)}, bf16[256,128]{1,0:T(8,128)(2,1)S(1)}, u32[]{:S(2)}, u32[]{:S(2)}) %collective-permute-start.24) | collective-permute-done | bytes 65568 | tf_op jit(solution)/shard_map/ppermute | solution.py:327
  139.2 1.9 %unpack.1 = bf16[128,40,128]{2,1,0:T(8,128)(2,1)} custom-call(s32[1]{0:T(128)} %bitcast.me_ref, bf16[384,128]{1,0:T(8,128)(2,1)S(1)} %get-tuple-element.79.refs_0_, bf16[384,128]{1,0:T(8,128)(2,1)S(1)} %collective-permute-done.9.refs_1_, bf16[384,128]{1,0:T(8,128)(2,1)S(1)} %collective-permute-done.10.refs_2_, ...), custom_call_target="tpu_custom_call" | custom-call | bytes 4194304 | tf_op jit(solution)/shard_map/unpack/pallas_call | solution.py:306
  (37 shorter events, 7.9 us)
Async XLA Ops:
  0.0 0.7 copy-start.1
  0.7 0.7 copy-start.2
  1.3 8.4 %copy-start = (bf16[128,40,3,128]{3,1,2,0:T(8,128)(2,1)S(1)}, bf16[128,40,3,128]{3,1,2,0:T(8,128)(2,1)}, u32[]{:S(2)}) copy-start(bf16[128,40,3,128]{3,1,2,0:T(8,128)(2,1)} %param.3) | copy-start | bytes 11796484
  5.6 27.7 %collective-permute-start.7 = (bf16[3,272,128]{2,1,0:T(8,128)(2,1)S(1)}, bf16[3,272,128]{2,1,0:T(8,128)(2,1)S(1)}, u32[]{:S(2)}, u32[]{:S(2)}) collective-permute-start(bf16[3,272,128]{2,1,0:T(8,128)(2,1)S(1)} %get-tuple-element.70), channel_id=1, source_target_pairs={{0,8},{1,9},{2,10},{3,11},{4,12},{5,13},{6,14},{7,15},{8,0},{9,1},... | collective-permute-start | bytes 626696 | tf_op jit(solution)/shard_map/ppermute | solution.py:327
  11.4 28.6 %collective-permute-start.3 = (bf16[3,400,128]{2,1,0:T(8,128)(2,1)S(1)}, bf16[3,400,128]{2,1,0:T(8,128)(2,1)S(1)}, u32[]{:S(2)}, u32[]{:S(2)}) collective-permute-start(bf16[3,400,128]{2,1,0:T(8,128)(2,1)S(1)} %get-tuple-element.66), channel_id=1, source_target_pairs={{0,8},{1,9},{2,10},{3,11},{4,12},{5,13},{6,14},{7,15},{8,0},{9,1},... | collective-permute-start | bytes 921608 | tf_op jit(solution)/shard_map/ppermute | solution.py:327
  11.5 36.3 %collective-permute-start.4 = (bf16[3,400,128]{2,1,0:T(8,128)(2,1)S(1)}, bf16[3,400,128]{2,1,0:T(8,128)(2,1)S(1)}, u32[]{:S(2)}, u32[]{:S(2)}) collective-permute-start(bf16[3,400,128]{2,1,0:T(8,128)(2,1)S(1)} %get-tuple-element.67), channel_id=1, source_target_pairs={{0,10},{1,11},{2,8},{3,9},{4,14},{5,15},{6,12},{7,13},{8,2},{9,3},... | collective-permute-start | bytes 921608 | tf_op jit(solution)/shard_map/ppermute | solution.py:327
  15.4 49.6 %collective-permute-start = (bf16[3,656,128]{2,1,0:T(8,128)(2,1)S(1)}, bf16[3,656,128]{2,1,0:T(8,128)(2,1)S(1)}, u32[]{:S(2)}, u32[]{:S(2)}) collective-permute-start(bf16[3,656,128]{2,1,0:T(8,128)(2,1)S(1)} %get-tuple-element.63), channel_id=1, source_target_pairs={{0,2},{1,3},{2,0},{3,1},{4,6},{5,7},{6,4},{7,5},{8,10},{9,11},{10,... | collective-permute-start | bytes 1511432 | tf_op jit(solution)/shard_map/ppermute | solution.py:327
  15.9 49.1 %collective-permute-start.1 = (bf16[3,656,128]{2,1,0:T(8,128)(2,1)S(1)}, bf16[3,656,128]{2,1,0:T(8,128)(2,1)S(1)}, u32[]{:S(2)}, u32[]{:S(2)}) collective-permute-start(bf16[3,656,128]{2,1,0:T(8,128)(2,1)S(1)} %get-tuple-element.64), channel_id=1, source_target_pairs={{0,4},{1,5},{2,6},{3,7},{4,0},{5,1},{6,2},{7,3},{8,12},{9,13},{10,... | collective-permute-start | bytes 1511432 | tf_op jit(solution)/shard_map/ppermute | solution.py:327
  33.4 37.3 %collective-permute-start.2 = (bf16[3,656,128]{2,1,0:T(8,128)(2,1)S(1)}, bf16[3,656,128]{2,1,0:T(8,128)(2,1)S(1)}, u32[]{:S(2)}, u32[]{:S(2)}) collective-permute-start(bf16[3,656,128]{2,1,0:T(8,128)(2,1)S(1)} %get-tuple-element.65), channel_id=1, source_target_pairs={{0,6},{1,7},{2,4},{3,5},{4,2},{5,3},{6,0},{7,1},{8,14},{9,15},{10,... | collective-permute-start | bytes 1511432 | tf_op jit(solution)/shard_map/ppermute | solution.py:327
  40.0 18.5 %collective-permute-start.5 = (bf16[3,400,128]{2,1,0:T(8,128)(2,1)S(1)}, bf16[3,400,128]{2,1,0:T(8,128)(2,1)S(1)}, u32[]{:S(2)}, u32[]{:S(2)}) collective-permute-start(bf16[3,400,128]{2,1,0:T(8,128)(2,1)S(1)} %get-tuple-element.68), channel_id=1, source_target_pairs={{0,12},{1,13},{2,14},{3,15},{4,8},{5,9},{6,10},{7,11},{8,4},{9,5},... | collective-permute-start | bytes 921608 | tf_op jit(solution)/shard_map/ppermute | solution.py:327
  47.9 17.2 %collective-permute-start.6 = (bf16[3,400,128]{2,1,0:T(8,128)(2,1)S(1)}, bf16[3,400,128]{2,1,0:T(8,128)(2,1)S(1)}, u32[]{:S(2)}, u32[]{:S(2)}) collective-permute-start(bf16[3,400,128]{2,1,0:T(8,128)(2,1)S(1)} %get-tuple-element.69), channel_id=1, source_target_pairs={{0,14},{1,15},{2,12},{3,13},{4,10},{5,11},{6,8},{7,9},{8,6},{9,7},... | collective-permute-start | bytes 921608 | tf_op jit(solution)/shard_map/ppermute | solution.py:327
  71.7 5.2 %collective-permute-start.8 = (bf16[8,2,384,128]{3,2,1,0:T(8,128)(2,1)S(1)}, bf16[8,2,384,128]{3,2,1,0:T(8,128)(2,1)S(1)}, u32[]{:S(2)}, u32[]{:S(2)}) collective-permute-start(bf16[8,2,384,128]{3,2,1,0:T(8,128)(2,1)S(1)} %gather_keys.2.refs_8_), channel_id=1, source_target_pairs={{0,1},{1,0},{2,3},{3,2},{4,5},{5,4},{6,7},{7,6},{8,9},{9,8},{10,11... | collective-permute-start | bytes 4718600 | tf_op jit(solution)/shard_map/ppermute | solution.py:353
  71.8 15.5 %collective-permute-start.12 = (bf16[3,272,128]{2,1,0:T(8,128)(2,1)S(1)}, bf16[3,272,128]{2,1,0:T(8,128)(2,1)S(1)}, u32[]{:S(2)}, u32[]{:S(2)}) collective-permute-start(bf16[3,272,128]{2,1,0:T(8,128)(2,1)S(1)} %get-tuple-element.88), channel_id=1, source_target_pairs={{0,12},{1,13},{2,14},{3,15},{4,8},{5,9},{6,10},{7,11},{8,4},{9,5},... | collective-permute-start | bytes 626696 | tf_op jit(solution)/shard_map/ppermute | solution.py:327
  75.4 25.7 %collective-permute-start.11 = (bf16[3,272,128]{2,1,0:T(8,128)(2,1)S(1)}, bf16[3,272,128]{2,1,0:T(8,128)(2,1)S(1)}, u32[]{:S(2)}, u32[]{:S(2)}) collective-permute-start(bf16[3,272,128]{2,1,0:T(8,128)(2,1)S(1)} %get-tuple-element.86), channel_id=1, source_target_pairs={{0,10},{1,11},{2,8},{3,9},{4,14},{5,15},{6,12},{7,13},{8,2},{9,3},... | collective-permute-start | bytes 626696 | tf_op jit(solution)/shard_map/ppermute | solution.py:327
  77.0 1.2 copy-start.3
  83.5 24.2 %collective-permute-start.13 = (bf16[3,272,128]{2,1,0:T(8,128)(2,1)S(1)}, bf16[3,272,128]{2,1,0:T(8,128)(2,1)S(1)}, u32[]{:S(2)}, u32[]{:S(2)}) collective-permute-start(bf16[3,272,128]{2,1,0:T(8,128)(2,1)S(1)} %get-tuple-element.91), channel_id=1, source_target_pairs={{0,14},{1,15},{2,12},{3,13},{4,10},{5,11},{6,8},{7,9},{8,6},{9,7},... | collective-permute-start | bytes 626696 | tf_op jit(solution)/shard_map/ppermute | solution.py:327
  87.4 20.3 %collective-permute-start.14 = (bf16[384,128]{1,0:T(8,128)(2,1)S(1)}, bf16[384,128]{1,0:T(8,128)(2,1)S(1)}, u32[]{:S(2)}, u32[]{:S(2)}) collective-permute-start(bf16[384,128]{1,0:T(8,128)(2,1)S(1)} %get-tuple-element.93), channel_id=1, source_target_pairs={{0,10},{1,11},{2,8},{3,9},{4,14},{5,15},{6,12},{7,13},{8,2},{9,3},... | collective-permute-start | bytes 294920 | tf_op jit(solution)/shard_map/ppermute | solution.py:327
  108.4 6.1 %collective-permute-start.15 = (bf16[8,2,256,128]{3,2,1,0:T(8,128)(2,1)S(1)}, bf16[8,2,256,128]{3,2,1,0:T(8,128)(2,1)S(1)}, u32[]{:S(2)}, u32[]{:S(2)}) collective-permute-start(bf16[8,2,256,128]{3,2,1,0:T(8,128)(2,1)S(1)} %gather_keys.3.refs_8_), channel_id=1, source_target_pairs={{0,1},{1,0},{2,3},{3,2},{4,5},{5,4},{6,7},{7,6},{8,9},{9,8},{10,11... | collective-permute-start | bytes 3145736 | tf_op jit(solution)/shard_map/ppermute | solution.py:353
  108.6 10.2 %collective-permute-start.18 = (bf16[384,128]{1,0:T(8,128)(2,1)S(1)}, bf16[384,128]{1,0:T(8,128)(2,1)S(1)}, u32[]{:S(2)}, u32[]{:S(2)}) collective-permute-start(bf16[384,128]{1,0:T(8,128)(2,1)S(1)} %get-tuple-element.108), channel_id=1, source_target_pairs={{0,12},{1,13},{2,14},{3,15},{4,8},{5,9},{6,10},{7,11},{8,4},{9,5},... | collective-permute-start | bytes 294920 | tf_op jit(solution)/shard_map/ppermute | solution.py:327
  112.1 8.2 %collective-permute-start.17 = (bf16[384,128]{1,0:T(8,128)(2,1)S(1)}, bf16[384,128]{1,0:T(8,128)(2,1)S(1)}, u32[]{:S(2)}, u32[]{:S(2)}) collective-permute-start(bf16[384,128]{1,0:T(8,128)(2,1)S(1)} %get-tuple-element.106), channel_id=1, source_target_pairs={{0,8},{1,9},{2,10},{3,11},{4,12},{5,13},{6,14},{7,15},{8,0},{9,1},... | collective-permute-start | bytes 294920 | tf_op jit(solution)/shard_map/ppermute | solution.py:327
  112.1 9.7 %collective-permute-start.10 = (bf16[384,128]{1,0:T(8,128)(2,1)S(1)}, bf16[384,128]{1,0:T(8,128)(2,1)S(1)}, u32[]{:S(2)}, u32[]{:S(2)}) collective-permute-start(bf16[384,128]{1,0:T(8,128)(2,1)S(1)} %get-tuple-element.83), channel_id=1, source_target_pairs={{0,4},{1,5},{2,6},{3,7},{4,0},{5,1},{6,2},{7,3},{8,12},{9,13},{10,... | collective-permute-start | bytes 294920 | tf_op jit(solution)/shard_map/ppermute | solution.py:327
  113.0 11.0 %collective-permute-start.9 = (bf16[384,128]{1,0:T(8,128)(2,1)S(1)}, bf16[384,128]{1,0:T(8,128)(2,1)S(1)}, u32[]{:S(2)}, u32[]{:S(2)}) collective-permute-start(bf16[384,128]{1,0:T(8,128)(2,1)S(1)} %get-tuple-element.81), channel_id=1, source_target_pairs={{0,2},{1,3},{2,0},{3,1},{4,6},{5,7},{6,4},{7,5},{8,10},{9,11},{10,... | collective-permute-start | bytes 294920 | tf_op jit(solution)/shard_map/ppermute | solution.py:327
  118.3 7.6 %collective-permute-start.20 = (bf16[256,128]{1,0:T(8,128)(2,1)S(1)}, bf16[256,128]{1,0:T(8,128)(2,1)S(1)}, u32[]{:S(2)}, u32[]{:S(2)}) collective-permute-start(bf16[256,128]{1,0:T(8,128)(2,1)S(1)} %get-tuple-element.112), channel_id=1, source_target_pairs={{0,2},{1,3},{2,0},{3,1},{4,6},{5,7},{6,4},{7,5},{8,10},{9,11},{10,... | collective-permute-start | bytes 196616 | tf_op jit(solution)/shard_map/ppermute | solution.py:327
  118.8 8.3 %collective-permute-start.21 = (bf16[256,128]{1,0:T(8,128)(2,1)S(1)}, bf16[256,128]{1,0:T(8,128)(2,1)S(1)}, u32[]{:S(2)}, u32[]{:S(2)}) collective-permute-start(bf16[256,128]{1,0:T(8,128)(2,1)S(1)} %get-tuple-element.113), channel_id=1, source_target_pairs={{0,4},{1,5},{2,6},{3,7},{4,0},{5,1},{6,2},{7,3},{8,12},{9,13},{10,... | collective-permute-start | bytes 196616 | tf_op jit(solution)/shard_map/ppermute | solution.py:327
  120.3 8.0 %collective-permute-start.22 = (bf16[256,128]{1,0:T(8,128)(2,1)S(1)}, bf16[256,128]{1,0:T(8,128)(2,1)S(1)}, u32[]{:S(2)}, u32[]{:S(2)}) collective-permute-start(bf16[256,128]{1,0:T(8,128)(2,1)S(1)} %get-tuple-element.114), channel_id=1, source_target_pairs={{0,6},{1,7},{2,4},{3,5},{4,2},{5,3},{6,0},{7,1},{8,14},{9,15},{10,... | collective-permute-start | bytes 196616 | tf_op jit(solution)/shard_map/ppermute | solution.py:327
  121.8 8.9 %collective-permute-start.23 = (bf16[256,128]{1,0:T(8,128)(2,1)S(1)}, bf16[256,128]{1,0:T(8,128)(2,1)S(1)}, u32[]{:S(2)}, u32[]{:S(2)}) collective-permute-start(bf16[256,128]{1,0:T(8,128)(2,1)S(1)} %get-tuple-element.115), channel_id=1, source_target_pairs={{0,8},{1,9},{2,10},{3,11},{4,12},{5,13},{6,14},{7,15},{8,0},{9,1},... | collective-permute-start | bytes 196616 | tf_op jit(solution)/shard_map/ppermute | solution.py:327
  124.0 15.3 %collective-permute-start.16 = (bf16[384,128]{1,0:T(8,128)(2,1)S(1)}, bf16[384,128]{1,0:T(8,128)(2,1)S(1)}, u32[]{:S(2)}, u32[]{:S(2)}) collective-permute-start(bf16[384,128]{1,0:T(8,128)(2,1)S(1)} %get-tuple-element.104), channel_id=1, source_target_pairs={{0,6},{1,7},{2,4},{3,5},{4,2},{5,3},{6,0},{7,1},{8,14},{9,15},{10,... | collective-permute-start | bytes 294920 | tf_op jit(solution)/shard_map/ppermute | solution.py:327
  125.8 13.4 %collective-permute-start.19 = (bf16[384,128]{1,0:T(8,128)(2,1)S(1)}, bf16[384,128]{1,0:T(8,128)(2,1)S(1)}, u32[]{:S(2)}, u32[]{:S(2)}) collective-permute-start(bf16[384,128]{1,0:T(8,128)(2,1)S(1)} %get-tuple-element.111), channel_id=1, source_target_pairs={{0,14},{1,15},{2,12},{3,13},{4,10},{5,11},{6,8},{7,9},{8,6},{9,7},... | collective-permute-start | bytes 294920 | tf_op jit(solution)/shard_map/ppermute | solution.py:327
  127.1 12.1 %collective-permute-start.24 = (bf16[256,128]{1,0:T(8,128)(2,1)S(1)}, bf16[256,128]{1,0:T(8,128)(2,1)S(1)}, u32[]{:S(2)}, u32[]{:S(2)}) collective-permute-start(bf16[256,128]{1,0:T(8,128)(2,1)S(1)} %get-tuple-element.116), channel_id=1, source_target_pairs={{0,10},{1,11},{2,8},{3,9},{4,14},{5,15},{6,12},{7,13},{8,2},{9,3},... | collective-permute-start | bytes 196616 | tf_op jit(solution)/shard_map/ppermute | solution.py:327
  128.3 10.9 %collective-permute-start.25 = (bf16[256,128]{1,0:T(8,128)(2,1)S(1)}, bf16[256,128]{1,0:T(8,128)(2,1)S(1)}, u32[]{:S(2)}, u32[]{:S(2)}) collective-permute-start(bf16[256,128]{1,0:T(8,128)(2,1)S(1)} %get-tuple-element.117), channel_id=1, source_target_pairs={{0,12},{1,13},{2,14},{3,15},{4,8},{5,9},{6,10},{7,11},{8,4},{9,5},... | collective-permute-start | bytes 196616 | tf_op jit(solution)/shard_map/ppermute | solution.py:327
  130.7 8.5 %collective-permute-start.26 = (bf16[256,128]{1,0:T(8,128)(2,1)S(1)}, bf16[256,128]{1,0:T(8,128)(2,1)S(1)}, u32[]{:S(2)}, u32[]{:S(2)}) collective-permute-start(bf16[256,128]{1,0:T(8,128)(2,1)S(1)} %get-tuple-element.118), channel_id=1, source_target_pairs={{0,14},{1,15},{2,12},{3,13},{4,10},{5,11},{6,8},{7,9},{8,6},{9,7},... | collective-permute-start | bytes 196616 | tf_op jit(solution)/shard_map/ppermute | solution.py:327

commit v5 on v4

--- a/solution.py
+++ b/solution.py
@@ -330,6 +330,7 @@
 
 
 def mixed(far, near):
+    far = far[::-1]
     order, far, near = far[:2], far[2:], near[1:]
     while far or near:
         order += near[:1] + far[:1]

time: 141 us -> 140 us (level)
  waiting for transfers between devices: 73.8 us -> 66 us
  starting transfers between devices: 46 us -> 52.8 us
    ppermute x25, waiting for transfers between devices: 73.8 us -> 66 us  [send(): lax.ppermute(array, 'seq', [(d, d ^ 2 * step) for d in range(self.seq)])]
    ppermute x25, starting transfers between devices: 45.8 us -> 52.6 us  [send(): lax.ppermute(array, 'seq', [(d, d ^ 2 * step) for d in range(self.seq)])]
  transfers between devices with their start and end apart: 27 -> 27, of which waited for: 10 -> 8; matrix products, arithmetic and copies ran while one was open for 0% -> 0% of each run, Pallas kernels for 8% -> 8%
where the time goes in v5:
time: 140 us
  waiting for transfers between devices  66 us (47%)
  starting transfers between devices  52.8 us (38%)
  Pallas kernels  18.8 us (13%)
  local copies, waits for them, and re-layouts  2.52 us (2%)
    ppermute x25, waiting for transfers between devices, send(): lax.ppermute(array, 'seq', [(d, d ^ 2 * step) for d in range(self.seq)])  66 us
    ppermute x25, starting transfers between devices, send(): lax.ppermute(array, 'seq', [(d, d ^ 2 * step) for d in range(self.seq)])  52.6 us
    pallas_call x2, Pallas kernels, attend(): pl.pallas_call(functools.partial(attend_kernel, plan, piece, scale), in_s...  9.04 us
    pallas_call x2, Pallas kernels, pack(): pl.pallas_call(functools.partial(pack_kernel, plan, items), grid_spec=plt...  5.99 us
  transfers between devices with their start and end apart: 27, of which 8 were waited for; matrix products, arithmetic and copies ran while one was open for 0% of the time, Pallas kernels for 8%

profile of v5, /device:TPU:0, one launch (start us, length us, event | category | flops | bytes accessed | tf_op | source)
XLA Modules:
  0.0 140.2 jit_solution(11979101031231140544)
XLA Ops:
  1.3 4.3 %pack.2 = (bf16[3,656,128]{2,1,0:T(8,128)(2,1)S(1)}, bf16[3,656,128]{2,1,0:T(8,128)(2,1)S(1)}, bf16[3,656,128]{2,1,0:T(8,128)(2,1)S(1)}, bf16[3,656,128]{2,1,0:T...) custom-call(s32[1]{0:T(128)} %bitcast.me_ref, ...), custom_call_target="tpu_custom_call" | custom-call | bytes 8388608 | tf_op jit(solution)/shard_map/pack/pallas_call | solution.py:95
  5.6 4.1 %collective-permute-start.7 = (bf16[3,272,128]{2,1,0:T(8,128)(2,1)S(1)}, bf16[3,272,128]{2,1,0:T(8,128)(2,1)S(1)}, u32[]{:S(2)}, u32[]{:S(2)}) collective-permute-start(bf16[3,272,128]{2,1,0:T(8,128)(2,1)S(1)} %get-tuple-element.70), channel_id=1, source_target_pairs={{0,8},{1,9},{2,10},{3,11},{4,12},{5,13},{6,14},{7,15},{8,0},{9,1},... | collective-permute-start | bytes 626696 | tf_op jit(solution)/shard_map/ppermute | solution.py:327
  9.7 1.7 %pack.3 = (bf16[3,400,128]{2,1,0:T(8,128)(2,1)S(1)}, bf16[3,400,128]{2,1,0:T(8,128)(2,1)S(1)}, bf16[3,400,128]{2,1,0:T(8,128)(2,1)S(1)}, bf16[3,400,128]{2,1,0:T(8,128)(2,1)S(1)}) custom-call(s32[1]{0:T(128)} %bitcast.me_ref, bf16[128,3,40,128]{3,2,1,0:T(8,128)(2,1)S(1)} %bitcast.4, s32[1,4,40]{2,1,0:T(4,128)S(1)} %bitcast.6, s32[1,40]{1,0:T(1,128)S(1)} %copy-done.2), custom_call_target="tpu_custom_call" | custom-call | bytes 8388608 | tf_op jit(solution)/shard_map/pack/pallas_call | solution.py:95
  11.5 3.8 %collective-permute-start.4 = (bf16[3,400,128]{2,1,0:T(8,128)(2,1)S(1)}, bf16[3,400,128]{2,1,0:T(8,128)(2,1)S(1)}, u32[]{:S(2)}, u32[]{:S(2)}) collective-permute-start(bf16[3,400,128]{2,1,0:T(8,128)(2,1)S(1)} %get-tuple-element.67), channel_id=1, source_target_pairs={{0,10},{1,11},{2,8},{3,9},{4,14},{5,15},{6,12},{7,13},{8,2},{9,3},... | collective-permute-start | bytes 921608 | tf_op jit(solution)/shard_map/ppermute | solution.py:327
  15.9 1.6 %collective-permute-start.1 = (bf16[3,656,128]{2,1,0:T(8,128)(2,1)S(1)}, bf16[3,656,128]{2,1,0:T(8,128)(2,1)S(1)}, u32[]{:S(2)}, u32[]{:S(2)}) collective-permute-start(bf16[3,656,128]{2,1,0:T(8,128)(2,1)S(1)} %get-tuple-element.64), channel_id=1, source_target_pairs={{0,4},{1,5},{2,6},{3,7},{4,0},{5,1},{6,2},{7,3},{8,12},{9,13},{10,... | collective-permute-start | bytes 1511432 | tf_op jit(solution)/shard_map/ppermute | solution.py:327
  17.5 15.9 %collective-permute-done.7.refs_4_ = bf16[3,272,128]{2,1,0:T(8,128)(2,1)S(1)} collective-permute-done((bf16[3,272,128]{2,1,0:T(8,128)(2,1)S(1)}, bf16[3,272,128]{2,1,0:T(8,128)(2,1)S(1)}, u32[]{:S(2)}, u32[]{:S(2)}) %collective-permute-start.7) | collective-permute-done | bytes 208928 | tf_op jit(solution)/shard_map/ppermute | solution.py:327
  34.3 5.7 %collective-permute-done.3.refs_4_ = bf16[3,400,128]{2,1,0:T(8,128)(2,1)S(1)} collective-permute-done((bf16[3,400,128]{2,1,0:T(8,128)(2,1)S(1)}, bf16[3,400,128]{2,1,0:T(8,128)(2,1)S(1)}, u32[]{:S(2)}, u32[]{:S(2)}) %collective-permute-start.3) | collective-permute-done | bytes 307232 | tf_op jit(solution)/shard_map/ppermute | solution.py:327
  40.0 2.8 %collective-permute-start.5 = (bf16[3,400,128]{2,1,0:T(8,128)(2,1)S(1)}, bf16[3,400,128]{2,1,0:T(8,128)(2,1)S(1)}, u32[]{:S(2)}, u32[]{:S(2)}) collective-permute-start(bf16[3,400,128]{2,1,0:T(8,128)(2,1)S(1)} %get-tuple-element.68), channel_id=1, source_target_pairs={{0,12},{1,13},{2,14},{3,15},{4,8},{5,9},{6,10},{7,11},{8,4},{9,5},... | collective-permute-start | bytes 921608 | tf_op jit(solution)/shard_map/ppermute | solution.py:327
  42.8 5.0 %collective-permute-done.4.refs_5_ = bf16[3,400,128]{2,1,0:T(8,128)(2,1)S(1)} collective-permute-done((bf16[3,400,128]{2,1,0:T(8,128)(2,1)S(1)}, bf16[3,400,128]{2,1,0:T(8,128)(2,1)S(1)}, u32[]{:S(2)}, u32[]{:S(2)}) %collective-permute-start.4) | collective-permute-done | bytes 307232 | tf_op jit(solution)/shard_map/ppermute | solution.py:327
  47.9 2.4 %collective-permute-start.6 = (bf16[3,400,128]{2,1,0:T(8,128)(2,1)S(1)}, bf16[3,400,128]{2,1,0:T(8,128)(2,1)S(1)}, u32[]{:S(2)}, u32[]{:S(2)}) collective-permute-start(bf16[3,400,128]{2,1,0:T(8,128)(2,1)S(1)} %get-tuple-element.69), channel_id=1, source_target_pairs={{0,14},{1,15},{2,12},{3,13},{4,10},{5,11},{6,8},{7,9},{8,6},{9,7},... | collective-permute-start | bytes 921608 | tf_op jit(solution)/shard_map/ppermute | solution.py:327
  50.3 8.3 %collective-permute-done.5.refs_6_ = bf16[3,400,128]{2,1,0:T(8,128)(2,1)S(1)} collective-permute-done((bf16[3,400,128]{2,1,0:T(8,128)(2,1)S(1)}, bf16[3,400,128]{2,1,0:T(8,128)(2,1)S(1)}, u32[]{:S(2)}, u32[]{:S(2)}) %collective-permute-start.5) | collective-permute-done | bytes 307232 | tf_op jit(solution)/shard_map/ppermute | solution.py:327
  58.5 6.5 %collective-permute-done.6.refs_7_ = bf16[3,400,128]{2,1,0:T(8,128)(2,1)S(1)} collective-permute-done((bf16[3,400,128]{2,1,0:T(8,128)(2,1)S(1)}, bf16[3,400,128]{2,1,0:T(8,128)(2,1)S(1)}, u32[]{:S(2)}, u32[]{:S(2)}) %collective-permute-start.6) | collective-permute-done | bytes 307232 | tf_op jit(solution)/shard_map/ppermute | solution.py:327
  65.0 5.6 %collective-permute-done.2.refs_3_ = bf16[3,656,128]{2,1,0:T(8,128)(2,1)S(1)} collective-permute-done((bf16[3,656,128]{2,1,0:T(8,128)(2,1)S(1)}, bf16[3,656,128]{2,1,0:T(8,128)(2,1)S(1)}, u32[]{:S(2)}, u32[]{:S(2)}) %collective-permute-start.2) | collective-permute-done | bytes 503840 | tf_op jit(solution)/shard_map/ppermute | solution.py:327
  70.7 1.1 gather_keys.2.refs_8_
  71.8 3.5 %collective-permute-start.12 = (bf16[3,272,128]{2,1,0:T(8,128)(2,1)S(1)}, bf16[3,272,128]{2,1,0:T(8,128)(2,1)S(1)}, u32[]{:S(2)}, u32[]{:S(2)}) collective-permute-start(bf16[3,272,128]{2,1,0:T(8,128)(2,1)S(1)} %get-tuple-element.88), channel_id=1, source_target_pairs={{0,12},{1,13},{2,14},{3,15},{4,8},{5,9},{6,10},{7,11},{8,4},{9,5},... | collective-permute-start | bytes 626696 | tf_op jit(solution)/shard_map/ppermute | solution.py:327
  75.4 1.6 %collective-permute-start.11 = (bf16[3,272,128]{2,1,0:T(8,128)(2,1)S(1)}, bf16[3,272,128]{2,1,0:T(8,128)(2,1)S(1)}, u32[]{:S(2)}, u32[]{:S(2)}) collective-permute-start(bf16[3,272,128]{2,1,0:T(8,128)(2,1)S(1)} %get-tuple-element.86), channel_id=1, source_target_pairs={{0,10},{1,11},{2,8},{3,9},{4,14},{5,15},{6,12},{7,13},{8,2},{9,3},... | collective-permute-start | bytes 626696 | tf_op jit(solution)/shard_map/ppermute | solution.py:327
  77.0 1.2 copy-done.3
  78.1 5.3 %attend.2 = (bf16[384,128]{1,0:T(8,128)(2,1)S(1)}, bf16[384,128]{1,0:T(8,128)(2,1)S(1)}, bf16[384,128]{1,0:T(8,128)(2,1)S(1)}, bf16[384,128]{1,0:T(8,128)(2,1)S(...) custom-call(s32[1]{0:T(128)} %bitcast.me_ref, ...), custom_call_target="tpu_custom_call" | custom-call | flops 4294967296 | bytes 8388608 | tf_op jit(solution)/shard_map/attend/pallas_call | solution.py:256
  83.5 3.9 %collective-permute-start.13 = (bf16[3,272,128]{2,1,0:T(8,128)(2,1)S(1)}, bf16[3,272,128]{2,1,0:T(8,128)(2,1)S(1)}, u32[]{:S(2)}, u32[]{:S(2)}) collective-permute-start(bf16[3,272,128]{2,1,0:T(8,128)(2,1)S(1)} %get-tuple-element.91), channel_id=1, source_target_pairs={{0,14},{1,15},{2,12},{3,13},{4,10},{5,11},{6,8},{7,9},{8,6},{9,7},... | collective-permute-start | bytes 626696 | tf_op jit(solution)/shard_map/ppermute | solution.py:327
  88.3 12.8 %collective-permute-done.11.refs_5_ = bf16[3,272,128]{2,1,0:T(8,128)(2,1)S(1)} collective-permute-done((bf16[3,272,128]{2,1,0:T(8,128)(2,1)S(1)}, bf16[3,272,128]{2,1,0:T(8,128)(2,1)S(1)}, u32[]{:S(2)}, u32[]{:S(2)}) %collective-permute-start.11) | collective-permute-done | bytes 208928 | tf_op jit(solution)/shard_map/ppermute | solution.py:327
  102.0 4.5 %collective-permute-start.19 = (bf16[384,128]{1,0:T(8,128)(2,1)S(1)}, bf16[384,128]{1,0:T(8,128)(2,1)S(1)}, u32[]{:S(2)}, u32[]{:S(2)}) collective-permute-start(bf16[384,128]{1,0:T(8,128)(2,1)S(1)} %get-tuple-element.111), channel_id=1, source_target_pairs={{0,14},{1,15},{2,12},{3,13},{4,10},{5,11},{6,8},{7,9},{8,6},{9,7},... | collective-permute-start | bytes 294920 | tf_op jit(solution)/shard_map/ppermute | solution.py:327
  106.6 5.2 %collective-permute-start.18 = (bf16[384,128]{1,0:T(8,128)(2,1)S(1)}, bf16[384,128]{1,0:T(8,128)(2,1)S(1)}, u32[]{:S(2)}, u32[]{:S(2)}) collective-permute-start(bf16[384,128]{1,0:T(8,128)(2,1)S(1)} %get-tuple-element.109), channel_id=1, source_target_pairs={{0,10},{1,11},{2,8},{3,9},{4,14},{5,15},{6,12},{7,13},{8,2},{9,3},... | collective-permute-start | bytes 294920 | tf_op jit(solution)/shard_map/ppermute | solution.py:327
  111.8 1.5 %collective-permute-start.9 = (bf16[384,128]{1,0:T(8,128)(2,1)S(1)}, bf16[384,128]{1,0:T(8,128)(2,1)S(1)}, u32[]{:S(2)}, u32[]{:S(2)}) collective-permute-start(bf16[384,128]{1,0:T(8,128)(2,1)S(1)} %get-tuple-element.81), channel_id=1, source_target_pairs={{0,2},{1,3},{2,0},{3,1},{4,6},{5,7},{6,4},{7,5},{8,10},{9,11},{10,... | collective-permute-start | bytes 294920 | tf_op jit(solution)/shard_map/ppermute | solution.py:327
  113.3 3.7 %attend.3 = (bf16[256,128]{1,0:T(8,128)(2,1)S(1)}, bf16[256,128]{1,0:T(8,128)(2,1)S(1)}, bf16[256,128]{1,0:T(8,128)(2,1)S(1)}, bf16[256,128]{1,0:T(8,128)(2,1)S(...) custom-call(s32[1]{0:T(128)} %bitcast.me_ref, ...), custom_call_target="tpu_custom_call" | custom-call | flops 4294967296 | bytes 8388608 | tf_op jit(solution)/shard_map/attend/pallas_call | solution.py:256
  117.6 2.0 %collective-permute-start.21 = (bf16[256,128]{1,0:T(8,128)(2,1)S(1)}, bf16[256,128]{1,0:T(8,128)(2,1)S(1)}, u32[]{:S(2)}, u32[]{:S(2)}) collective-permute-start(bf16[256,128]{1,0:T(8,128)(2,1)S(1)} %get-tuple-element.113), channel_id=1, source_target_pairs={{0,4},{1,5},{2,6},{3,7},{4,0},{5,1},{6,2},{7,3},{8,12},{9,13},{10,... | collective-permute-start | bytes 196616 | tf_op jit(solution)/shard_map/ppermute | solution.py:327
  120.6 2.9 %collective-permute-start.23 = (bf16[256,128]{1,0:T(8,128)(2,1)S(1)}, bf16[256,128]{1,0:T(8,128)(2,1)S(1)}, u32[]{:S(2)}, u32[]{:S(2)}) collective-permute-start(bf16[256,128]{1,0:T(8,128)(2,1)S(1)} %get-tuple-element.115), channel_id=1, source_target_pairs={{0,8},{1,9},{2,10},{3,11},{4,12},{5,13},{6,14},{7,15},{8,0},{9,1},... | collective-permute-start | bytes 196616 | tf_op jit(solution)/shard_map/ppermute | solution.py:327
  123.5 1.0 collective-permute-start.16
  125.4 2.0 %collective-permute-start.24 = (bf16[256,128]{1,0:T(8,128)(2,1)S(1)}, bf16[256,128]{1,0:T(8,128)(2,1)S(1)}, u32[]{:S(2)}, u32[]{:S(2)}) collective-permute-start(bf16[256,128]{1,0:T(8,128)(2,1)S(1)} %get-tuple-element.116), channel_id=1, source_target_pairs={{0,10},{1,11},{2,8},{3,9},{4,14},{5,15},{6,12},{7,13},{8,2},{9,3},... | collective-permute-start | bytes 196616 | tf_op jit(solution)/shard_map/ppermute | solution.py:327
  127.4 2.4 %collective-permute-start.25 = (bf16[256,128]{1,0:T(8,128)(2,1)S(1)}, bf16[256,128]{1,0:T(8,128)(2,1)S(1)}, u32[]{:S(2)}, u32[]{:S(2)}) collective-permute-start(bf16[256,128]{1,0:T(8,128)(2,1)S(1)} %get-tuple-element.117), channel_id=1, source_target_pairs={{0,12},{1,13},{2,14},{3,15},{4,8},{5,9},{6,10},{7,11},{8,4},{9,5},... | collective-permute-start | bytes 196616 | tf_op jit(solution)/shard_map/ppermute | solution.py:327
  129.9 2.3 %collective-permute-start.26 = (bf16[256,128]{1,0:T(8,128)(2,1)S(1)}, bf16[256,128]{1,0:T(8,128)(2,1)S(1)}, u32[]{:S(2)}, u32[]{:S(2)}) collective-permute-start(bf16[256,128]{1,0:T(8,128)(2,1)S(1)} %get-tuple-element.118), channel_id=1, source_target_pairs={{0,14},{1,15},{2,12},{3,13},{4,10},{5,11},{6,8},{7,9},{8,6},{9,7},... | collective-permute-start | bytes 196616 | tf_op jit(solution)/shard_map/ppermute | solution.py:327
  132.1 6.1 %collective-permute-done.24.refs_13_ = bf16[256,128]{1,0:T(8,128)(2,1)S(1)} collective-permute-done((bf16[256,128]{1,0:T(8,128)(2,1)S(1)}, bf16[256,128]{1,0:T(8,128)(2,1)S(1)}, u32[]{:S(2)}, u32[]{:S(2)}) %collective-permute-start.24) | collective-permute-done | bytes 65568 | tf_op jit(solution)/shard_map/ppermute | solution.py:327
  138.3 1.9 %unpack.1 = bf16[128,40,128]{2,1,0:T(8,128)(2,1)} custom-call(s32[1]{0:T(128)} %bitcast.me_ref, bf16[384,128]{1,0:T(8,128)(2,1)S(1)} %get-tuple-element.79.refs_0_, bf16[384,128]{1,0:T(8,128)(2,1)S(1)} %collective-permute-done.9.refs_1_, bf16[384,128]{1,0:T(8,128)(2,1)S(1)} %collective-permute-done.10.refs_2_, ...), custom_call_target="tpu_custom_call" | custom-call | bytes 4194304 | tf_op jit(solution)/shard_map/unpack/pallas_call | solution.py:306
  (37 shorter events, 7.5 us)
Async XLA Ops:
  0.0 0.7 copy-start.1
  0.7 0.7 copy-start.2
  1.3 8.4 %copy-start = (bf16[128,40,3,128]{3,1,2,0:T(8,128)(2,1)S(1)}, bf16[128,40,3,128]{3,1,2,0:T(8,128)(2,1)}, u32[]{:S(2)}) copy-start(bf16[128,40,3,128]{3,1,2,0:T(8,128)(2,1)} %param.3) | copy-start | bytes 11796484
  5.6 27.7 %collective-permute-start.7 = (bf16[3,272,128]{2,1,0:T(8,128)(2,1)S(1)}, bf16[3,272,128]{2,1,0:T(8,128)(2,1)S(1)}, u32[]{:S(2)}, u32[]{:S(2)}) collective-permute-start(bf16[3,272,128]{2,1,0:T(8,128)(2,1)S(1)} %get-tuple-element.70), channel_id=1, source_target_pairs={{0,8},{1,9},{2,10},{3,11},{4,12},{5,13},{6,14},{7,15},{8,0},{9,1},... | collective-permute-start | bytes 626696 | tf_op jit(solution)/shard_map/ppermute | solution.py:327
  11.4 28.6 %collective-permute-start.3 = (bf16[3,400,128]{2,1,0:T(8,128)(2,1)S(1)}, bf16[3,400,128]{2,1,0:T(8,128)(2,1)S(1)}, u32[]{:S(2)}, u32[]{:S(2)}) collective-permute-start(bf16[3,400,128]{2,1,0:T(8,128)(2,1)S(1)} %get-tuple-element.66), channel_id=1, source_target_pairs={{0,8},{1,9},{2,10},{3,11},{4,12},{5,13},{6,14},{7,15},{8,0},{9,1},... | collective-permute-start | bytes 921608 | tf_op jit(solution)/shard_map/ppermute | solution.py:327
  11.5 36.3 %collective-permute-start.4 = (bf16[3,400,128]{2,1,0:T(8,128)(2,1)S(1)}, bf16[3,400,128]{2,1,0:T(8,128)(2,1)S(1)}, u32[]{:S(2)}, u32[]{:S(2)}) collective-permute-start(bf16[3,400,128]{2,1,0:T(8,128)(2,1)S(1)} %get-tuple-element.67), channel_id=1, source_target_pairs={{0,10},{1,11},{2,8},{3,9},{4,14},{5,15},{6,12},{7,13},{8,2},{9,3},... | collective-permute-start | bytes 921608 | tf_op jit(solution)/shard_map/ppermute | solution.py:327
  15.4 49.6 %collective-permute-start = (bf16[3,656,128]{2,1,0:T(8,128)(2,1)S(1)}, bf16[3,656,128]{2,1,0:T(8,128)(2,1)S(1)}, u32[]{:S(2)}, u32[]{:S(2)}) collective-permute-start(bf16[3,656,128]{2,1,0:T(8,128)(2,1)S(1)} %get-tuple-element.63), channel_id=1, source_target_pairs={{0,2},{1,3},{2,0},{3,1},{4,6},{5,7},{6,4},{7,5},{8,10},{9,11},{10,... | collective-permute-start | bytes 1511432 | tf_op jit(solution)/shard_map/ppermute | solution.py:327
  15.9 49.1 %collective-permute-start.1 = (bf16[3,656,128]{2,1,0:T(8,128)(2,1)S(1)}, bf16[3,656,128]{2,1,0:T(8,128)(2,1)S(1)}, u32[]{:S(2)}, u32[]{:S(2)}) collective-permute-start(bf16[3,656,128]{2,1,0:T(8,128)(2,1)S(1)} %get-tuple-element.64), channel_id=1, source_target_pairs={{0,4},{1,5},{2,6},{3,7},{4,0},{5,1},{6,2},{7,3},{8,12},{9,13},{10,... | collective-permute-start | bytes 1511432 | tf_op jit(solution)/shard_map/ppermute | solution.py:327
  33.4 37.3 %collective-permute-start.2 = (bf16[3,656,128]{2,1,0:T(8,128)(2,1)S(1)}, bf16[3,656,128]{2,1,0:T(8,128)(2,1)S(1)}, u32[]{:S(2)}, u32[]{:S(2)}) collective-permute-start(bf16[3,656,128]{2,1,0:T(8,128)(2,1)S(1)} %get-tuple-element.65), channel_id=1, source_target_pairs={{0,6},{1,7},{2,4},{3,5},{4,2},{5,3},{6,0},{7,1},{8,14},{9,15},{10,... | collective-permute-start | bytes 1511432 | tf_op jit(solution)/shard_map/ppermute | solution.py:327
  40.0 18.5 %collective-permute-start.5 = (bf16[3,400,128]{2,1,0:T(8,128)(2,1)S(1)}, bf16[3,400,128]{2,1,0:T(8,128)(2,1)S(1)}, u32[]{:S(2)}, u32[]{:S(2)}) collective-permute-start(bf16[3,400,128]{2,1,0:T(8,128)(2,1)S(1)} %get-tuple-element.68), channel_id=1, source_target_pairs={{0,12},{1,13},{2,14},{3,15},{4,8},{5,9},{6,10},{7,11},{8,4},{9,5},... | collective-permute-start | bytes 921608 | tf_op jit(solution)/shard_map/ppermute | solution.py:327
  47.9 17.2 %collective-permute-start.6 = (bf16[3,400,128]{2,1,0:T(8,128)(2,1)S(1)}, bf16[3,400,128]{2,1,0:T(8,128)(2,1)S(1)}, u32[]{:S(2)}, u32[]{:S(2)}) collective-permute-start(bf16[3,400,128]{2,1,0:T(8,128)(2,1)S(1)} %get-tuple-element.69), channel_id=1, source_target_pairs={{0,14},{1,15},{2,12},{3,13},{4,10},{5,11},{6,8},{7,9},{8,6},{9,7},... | collective-permute-start | bytes 921608 | tf_op jit(solution)/shard_map/ppermute | solution.py:327
  71.7 5.2 %collective-permute-start.8 = (bf16[8,2,384,128]{3,2,1,0:T(8,128)(2,1)S(1)}, bf16[8,2,384,128]{3,2,1,0:T(8,128)(2,1)S(1)}, u32[]{:S(2)}, u32[]{:S(2)}) collective-permute-start(bf16[8,2,384,128]{3,2,1,0:T(8,128)(2,1)S(1)} %gather_keys.2.refs_8_), channel_id=1, source_target_pairs={{0,1},{1,0},{2,3},{3,2},{4,5},{5,4},{6,7},{7,6},{8,9},{9,8},{10,11... | collective-permute-start | bytes 4718600 | tf_op jit(solution)/shard_map/ppermute | solution.py:354
  71.8 16.5 %collective-permute-start.12 = (bf16[3,272,128]{2,1,0:T(8,128)(2,1)S(1)}, bf16[3,272,128]{2,1,0:T(8,128)(2,1)S(1)}, u32[]{:S(2)}, u32[]{:S(2)}) collective-permute-start(bf16[3,272,128]{2,1,0:T(8,128)(2,1)S(1)} %get-tuple-element.88), channel_id=1, source_target_pairs={{0,12},{1,13},{2,14},{3,15},{4,8},{5,9},{6,10},{7,11},{8,4},{9,5},... | collective-permute-start | bytes 626696 | tf_op jit(solution)/shard_map/ppermute | solution.py:327
  75.4 25.7 %collective-permute-start.11 = (bf16[3,272,128]{2,1,0:T(8,128)(2,1)S(1)}, bf16[3,272,128]{2,1,0:T(8,128)(2,1)S(1)}, u32[]{:S(2)}, u32[]{:S(2)}) collective-permute-start(bf16[3,272,128]{2,1,0:T(8,128)(2,1)S(1)} %get-tuple-element.86), channel_id=1, source_target_pairs={{0,10},{1,11},{2,8},{3,9},{4,14},{5,15},{6,12},{7,13},{8,2},{9,3},... | collective-permute-start | bytes 626696 | tf_op jit(solution)/shard_map/ppermute | solution.py:327
  77.0 1.2 copy-start.3
  83.5 17.6 %collective-permute-start.13 = (bf16[3,272,128]{2,1,0:T(8,128)(2,1)S(1)}, bf16[3,272,128]{2,1,0:T(8,128)(2,1)S(1)}, u32[]{:S(2)}, u32[]{:S(2)}) collective-permute-start(bf16[3,272,128]{2,1,0:T(8,128)(2,1)S(1)} %get-tuple-element.91), channel_id=1, source_target_pairs={{0,14},{1,15},{2,12},{3,13},{4,10},{5,11},{6,8},{7,9},{8,6},{9,7},... | collective-permute-start | bytes 626696 | tf_op jit(solution)/shard_map/ppermute | solution.py:327
  87.4 13.8 %collective-permute-start.14 = (bf16[384,128]{1,0:T(8,128)(2,1)S(1)}, bf16[384,128]{1,0:T(8,128)(2,1)S(1)}, u32[]{:S(2)}, u32[]{:S(2)}) collective-permute-start(bf16[384,128]{1,0:T(8,128)(2,1)S(1)} %get-tuple-element.93), channel_id=1, source_target_pairs={{0,12},{1,13},{2,14},{3,15},{4,8},{5,9},{6,10},{7,11},{8,4},{9,5},... | collective-permute-start | bytes 294920 | tf_op jit(solution)/shard_map/ppermute | solution.py:327
  101.9 11.4 %collective-permute-start.15 = (bf16[8,2,256,128]{3,2,1,0:T(8,128)(2,1)S(1)}, bf16[8,2,256,128]{3,2,1,0:T(8,128)(2,1)S(1)}, u32[]{:S(2)}, u32[]{:S(2)}) collective-permute-start(bf16[8,2,256,128]{3,2,1,0:T(8,128)(2,1)S(1)} %gather_keys.3.refs_8_), channel_id=1, source_target_pairs={{0,1},{1,0},{2,3},{3,2},{4,5},{5,4},{6,7},{7,6},{8,9},{9,8},{10,11... | collective-permute-start | bytes 3145736 | tf_op jit(solution)/shard_map/ppermute | solution.py:354
  102.0 15.6 %collective-permute-start.19 = (bf16[384,128]{1,0:T(8,128)(2,1)S(1)}, bf16[384,128]{1,0:T(8,128)(2,1)S(1)}, u32[]{:S(2)}, u32[]{:S(2)}) collective-permute-start(bf16[384,128]{1,0:T(8,128)(2,1)S(1)} %get-tuple-element.111), channel_id=1, source_target_pairs={{0,14},{1,15},{2,12},{3,13},{4,10},{5,11},{6,8},{7,9},{8,6},{9,7},... | collective-permute-start | bytes 294920 | tf_op jit(solution)/shard_map/ppermute | solution.py:327
  106.6 13.0 %collective-permute-start.18 = (bf16[384,128]{1,0:T(8,128)(2,1)S(1)}, bf16[384,128]{1,0:T(8,128)(2,1)S(1)}, u32[]{:S(2)}, u32[]{:S(2)}) collective-permute-start(bf16[384,128]{1,0:T(8,128)(2,1)S(1)} %get-tuple-element.109), channel_id=1, source_target_pairs={{0,10},{1,11},{2,8},{3,9},{4,14},{5,15},{6,12},{7,13},{8,2},{9,3},... | collective-permute-start | bytes 294920 | tf_op jit(solution)/shard_map/ppermute | solution.py:327
  111.7 8.9 %collective-permute-start.10 = (bf16[384,128]{1,0:T(8,128)(2,1)S(1)}, bf16[384,128]{1,0:T(8,128)(2,1)S(1)}, u32[]{:S(2)}, u32[]{:S(2)}) collective-permute-start(bf16[384,128]{1,0:T(8,128)(2,1)S(1)} %get-tuple-element.83), channel_id=1, source_target_pairs={{0,4},{1,5},{2,6},{3,7},{4,0},{5,1},{6,2},{7,3},{8,12},{9,13},{10,... | collective-permute-start | bytes 294920 | tf_op jit(solution)/shard_map/ppermute | solution.py:327
  111.8 11.7 %collective-permute-start.9 = (bf16[384,128]{1,0:T(8,128)(2,1)S(1)}, bf16[384,128]{1,0:T(8,128)(2,1)S(1)}, u32[]{:S(2)}, u32[]{:S(2)}) collective-permute-start(bf16[384,128]{1,0:T(8,128)(2,1)S(1)} %get-tuple-element.81), channel_id=1, source_target_pairs={{0,2},{1,3},{2,0},{3,1},{4,6},{5,7},{6,4},{7,5},{8,10},{9,11},{10,... | collective-permute-start | bytes 294920 | tf_op jit(solution)/shard_map/ppermute | solution.py:327
  117.0 7.5 %collective-permute-start.20 = (bf16[256,128]{1,0:T(8,128)(2,1)S(1)}, bf16[256,128]{1,0:T(8,128)(2,1)S(1)}, u32[]{:S(2)}, u32[]{:S(2)}) collective-permute-start(bf16[256,128]{1,0:T(8,128)(2,1)S(1)} %get-tuple-element.112), channel_id=1, source_target_pairs={{0,2},{1,3},{2,0},{3,1},{4,6},{5,7},{6,4},{7,5},{8,10},{9,11},{10,... | collective-permute-start | bytes 196616 | tf_op jit(solution)/shard_map/ppermute | solution.py:327
  117.6 7.8 %collective-permute-start.21 = (bf16[256,128]{1,0:T(8,128)(2,1)S(1)}, bf16[256,128]{1,0:T(8,128)(2,1)S(1)}, u32[]{:S(2)}, u32[]{:S(2)}) collective-permute-start(bf16[256,128]{1,0:T(8,128)(2,1)S(1)} %get-tuple-element.113), channel_id=1, source_target_pairs={{0,4},{1,5},{2,6},{3,7},{4,0},{5,1},{6,2},{7,3},{8,12},{9,13},{10,... | collective-permute-start | bytes 196616 | tf_op jit(solution)/shard_map/ppermute | solution.py:327
  119.6 7.9 %collective-permute-start.22 = (bf16[256,128]{1,0:T(8,128)(2,1)S(1)}, bf16[256,128]{1,0:T(8,128)(2,1)S(1)}, u32[]{:S(2)}, u32[]{:S(2)}) collective-permute-start(bf16[256,128]{1,0:T(8,128)(2,1)S(1)} %get-tuple-element.114), channel_id=1, source_target_pairs={{0,6},{1,7},{2,4},{3,5},{4,2},{5,3},{6,0},{7,1},{8,14},{9,15},{10,... | collective-permute-start | bytes 196616 | tf_op jit(solution)/shard_map/ppermute | solution.py:327
  120.6 9.3 %collective-permute-start.23 = (bf16[256,128]{1,0:T(8,128)(2,1)S(1)}, bf16[256,128]{1,0:T(8,128)(2,1)S(1)}, u32[]{:S(2)}, u32[]{:S(2)}) collective-permute-start(bf16[256,128]{1,0:T(8,128)(2,1)S(1)} %get-tuple-element.115), channel_id=1, source_target_pairs={{0,8},{1,9},{2,10},{3,11},{4,12},{5,13},{6,14},{7,15},{8,0},{9,1},... | collective-permute-start | bytes 196616 | tf_op jit(solution)/shard_map/ppermute | solution.py:327
  123.5 14.8 %collective-permute-start.16 = (bf16[384,128]{1,0:T(8,128)(2,1)S(1)}, bf16[384,128]{1,0:T(8,128)(2,1)S(1)}, u32[]{:S(2)}, u32[]{:S(2)}) collective-permute-start(bf16[384,128]{1,0:T(8,128)(2,1)S(1)} %get-tuple-element.104), channel_id=1, source_target_pairs={{0,6},{1,7},{2,4},{3,5},{4,2},{5,3},{6,0},{7,1},{8,14},{9,15},{10,... | collective-permute-start | bytes 294920 | tf_op jit(solution)/shard_map/ppermute | solution.py:327
  124.5 13.8 %collective-permute-start.17 = (bf16[384,128]{1,0:T(8,128)(2,1)S(1)}, bf16[384,128]{1,0:T(8,128)(2,1)S(1)}, u32[]{:S(2)}, u32[]{:S(2)}) collective-permute-start(bf16[384,128]{1,0:T(8,128)(2,1)S(1)} %get-tuple-element.107), channel_id=1, source_target_pairs={{0,8},{1,9},{2,10},{3,11},{4,12},{5,13},{6,14},{7,15},{8,0},{9,1},... | collective-permute-start | bytes 294920 | tf_op jit(solution)/shard_map/ppermute | solution.py:327
  125.4 12.8 %collective-permute-start.24 = (bf16[256,128]{1,0:T(8,128)(2,1)S(1)}, bf16[256,128]{1,0:T(8,128)(2,1)S(1)}, u32[]{:S(2)}, u32[]{:S(2)}) collective-permute-start(bf16[256,128]{1,0:T(8,128)(2,1)S(1)} %get-tuple-element.116), channel_id=1, source_target_pairs={{0,10},{1,11},{2,8},{3,9},{4,14},{5,15},{6,12},{7,13},{8,2},{9,3},... | collective-permute-start | bytes 196616 | tf_op jit(solution)/shard_map/ppermute | solution.py:327
  127.4 10.8 %collective-permute-start.25 = (bf16[256,128]{1,0:T(8,128)(2,1)S(1)}, bf16[256,128]{1,0:T(8,128)(2,1)S(1)}, u32[]{:S(2)}, u32[]{:S(2)}) collective-permute-start(bf16[256,128]{1,0:T(8,128)(2,1)S(1)} %get-tuple-element.117), channel_id=1, source_target_pairs={{0,12},{1,13},{2,14},{3,15},{4,8},{5,9},{6,10},{7,11},{8,4},{9,5},... | collective-permute-start | bytes 196616 | tf_op jit(solution)/shard_map/ppermute | solution.py:327
  129.9 8.4 %collective-permute-start.26 = (bf16[256,128]{1,0:T(8,128)(2,1)S(1)}, bf16[256,128]{1,0:T(8,128)(2,1)S(1)}, u32[]{:S(2)}, u32[]{:S(2)}) collective-permute-start(bf16[256,128]{1,0:T(8,128)(2,1)S(1)} %get-tuple-element.118), channel_id=1, source_target_pairs={{0,14},{1,15},{2,12},{3,13},{4,10},{5,11},{6,8},{7,9},{8,6},{9,7},... | collective-permute-start | bytes 196616 | tf_op jit(solution)/shard_map/ppermute | solution.py:327

commit v6 on v5

--- a/solution.py
+++ b/solution.py
@@ -15,10 +15,10 @@
 GROUP = 4
 CUT = 3
 WINDOW = 8
-LATE_A = 3
+LATE_A = 4
 SEEN_A = 0
 LATE_B = 5
-SEEN_B = 1
+SEEN_B = 2
 WINDOW_LAST = 99
 
 

time: 140 us -> 139 us (level)
  transfers between devices with their start and end apart: 27 -> 27, of which waited for: 8 -> 9; matrix products, arithmetic and copies ran while one was open for 0% -> 0% of each run, Pallas kernels for 8% -> 8%
where the time goes in v6:
time: 139 us
  waiting for transfers between devices  65.6 us (47%)
  starting transfers between devices  51.8 us (37%)
  Pallas kernels  18.8 us (14%)
  local copies, waits for them, and re-layouts  2.52 us (2%)
    ppermute x25, waiting for transfers between devices, send(): lax.ppermute(array, 'seq', [(d, d ^ 2 * step) for d in range(self.seq)])  65.6 us
    ppermute x25, starting transfers between devices, send(): lax.ppermute(array, 'seq', [(d, d ^ 2 * step) for d in range(self.seq)])  51.6 us
    pallas_call x2, Pallas kernels, attend(): pl.pallas_call(functools.partial(attend_kernel, plan, piece, scale), in_s...  9.06 us
    pallas_call x2, Pallas kernels, pack(): pl.pallas_call(functools.partial(pack_kernel, plan, items), grid_spec=plt...  5.99 us
  transfers between devices with their start and end apart: 27, of which 9 were waited for; matrix products, arithmetic and copies ran while one was open for 0% of the time, Pallas kernels for 8%

profile of v6, /device:TPU:0, one launch (start us, length us, event | category | flops | bytes accessed | tf_op | source)
XLA Modules:
  0.0 138.8 jit_solution(12583894173367337254)
XLA Ops:
  1.3 4.3 %pack.2 = (bf16[3,656,128]{2,1,0:T(8,128)(2,1)S(1)}, bf16[3,656,128]{2,1,0:T(8,128)(2,1)S(1)}, bf16[3,656,128]{2,1,0:T(8,128)(2,1)S(1)}, bf16[3,656,128]{2,1,0:T...) custom-call(s32[1]{0:T(128)} %bitcast.me_ref, ...), custom_call_target="tpu_custom_call" | custom-call | bytes 8388608 | tf_op jit(solution)/shard_map/pack/pallas_call | solution.py:95
  5.6 4.1 %collective-permute-start.7 = (bf16[3,272,128]{2,1,0:T(8,128)(2,1)S(1)}, bf16[3,272,128]{2,1,0:T(8,128)(2,1)S(1)}, u32[]{:S(2)}, u32[]{:S(2)}) collective-permute-start(bf16[3,272,128]{2,1,0:T(8,128)(2,1)S(1)} %get-tuple-element.69), channel_id=1, source_target_pairs={{0,8},{1,9},{2,10},{3,11},{4,12},{5,13},{6,14},{7,15},{8,0},{9,1},... | collective-permute-start | bytes 626696 | tf_op jit(solution)/shard_map/ppermute | solution.py:327
  9.7 1.7 %pack.3 = (bf16[3,400,128]{2,1,0:T(8,128)(2,1)S(1)}, bf16[3,400,128]{2,1,0:T(8,128)(2,1)S(1)}, bf16[3,400,128]{2,1,0:T(8,128)(2,1)S(1)}, bf16[3,400,128]{2,1,0:T(8,128)(2,1)S(1)}) custom-call(s32[1]{0:T(128)} %bitcast.me_ref, bf16[128,3,40,128]{3,2,1,0:T(8,128)(2,1)S(1)} %bitcast.4, s32[1,4,40]{2,1,0:T(4,128)S(1)} %bitcast.6, s32[1,40]{1,0:T(1,128)S(1)} %copy-done.2), custom_call_target="tpu_custom_call" | custom-call | bytes 8388608 | tf_op jit(solution)/shard_map/pack/pallas_call | solution.py:95
  11.5 3.8 %collective-permute-start.4 = (bf16[3,400,128]{2,1,0:T(8,128)(2,1)S(1)}, bf16[3,400,128]{2,1,0:T(8,128)(2,1)S(1)}, u32[]{:S(2)}, u32[]{:S(2)}) collective-permute-start(bf16[3,400,128]{2,1,0:T(8,128)(2,1)S(1)} %get-tuple-element.66), channel_id=1, source_target_pairs={{0,10},{1,11},{2,8},{3,9},{4,14},{5,15},{6,12},{7,13},{8,2},{9,3},... | collective-permute-start | bytes 921608 | tf_op jit(solution)/shard_map/ppermute | solution.py:327
  15.9 1.6 %collective-permute-start.1 = (bf16[3,656,128]{2,1,0:T(8,128)(2,1)S(1)}, bf16[3,656,128]{2,1,0:T(8,128)(2,1)S(1)}, u32[]{:S(2)}, u32[]{:S(2)}) collective-permute-start(bf16[3,656,128]{2,1,0:T(8,128)(2,1)S(1)} %get-tuple-element.63), channel_id=1, source_target_pairs={{0,4},{1,5},{2,6},{3,7},{4,0},{5,1},{6,2},{7,3},{8,12},{9,13},{10,... | collective-permute-start | bytes 1511432 | tf_op jit(solution)/shard_map/ppermute | solution.py:327
  17.5 15.9 %collective-permute-done.7.refs_4_ = bf16[3,272,128]{2,1,0:T(8,128)(2,1)S(1)} collective-permute-done((bf16[3,272,128]{2,1,0:T(8,128)(2,1)S(1)}, bf16[3,272,128]{2,1,0:T(8,128)(2,1)S(1)}, u32[]{:S(2)}, u32[]{:S(2)}) %collective-permute-start.7) | collective-permute-done | bytes 208928 | tf_op jit(solution)/shard_map/ppermute | solution.py:327
  34.3 5.7 %collective-permute-done.3.refs_4_ = bf16[3,400,128]{2,1,0:T(8,128)(2,1)S(1)} collective-permute-done((bf16[3,400,128]{2,1,0:T(8,128)(2,1)S(1)}, bf16[3,400,128]{2,1,0:T(8,128)(2,1)S(1)}, u32[]{:S(2)}, u32[]{:S(2)}) %collective-permute-start.3) | collective-permute-done | bytes 307232 | tf_op jit(solution)/shard_map/ppermute | solution.py:327
  40.0 2.8 %collective-permute-start.5 = (bf16[3,400,128]{2,1,0:T(8,128)(2,1)S(1)}, bf16[3,400,128]{2,1,0:T(8,128)(2,1)S(1)}, u32[]{:S(2)}, u32[]{:S(2)}) collective-permute-start(bf16[3,400,128]{2,1,0:T(8,128)(2,1)S(1)} %get-tuple-element.67), channel_id=1, source_target_pairs={{0,12},{1,13},{2,14},{3,15},{4,8},{5,9},{6,10},{7,11},{8,4},{9,5},... | collective-permute-start | bytes 921608 | tf_op jit(solution)/shard_map/ppermute | solution.py:327
  42.8 5.0 %collective-permute-done.4.refs_5_ = bf16[3,400,128]{2,1,0:T(8,128)(2,1)S(1)} collective-permute-done((bf16[3,400,128]{2,1,0:T(8,128)(2,1)S(1)}, bf16[3,400,128]{2,1,0:T(8,128)(2,1)S(1)}, u32[]{:S(2)}, u32[]{:S(2)}) %collective-permute-start.4) | collective-permute-done | bytes 307232 | tf_op jit(solution)/shard_map/ppermute | solution.py:327
  47.9 2.4 %collective-permute-start.6 = (bf16[3,400,128]{2,1,0:T(8,128)(2,1)S(1)}, bf16[3,400,128]{2,1,0:T(8,128)(2,1)S(1)}, u32[]{:S(2)}, u32[]{:S(2)}) collective-permute-start(bf16[3,400,128]{2,1,0:T(8,128)(2,1)S(1)} %get-tuple-element.68), channel_id=1, source_target_pairs={{0,14},{1,15},{2,12},{3,13},{4,10},{5,11},{6,8},{7,9},{8,6},{9,7},... | collective-permute-start | bytes 921608 | tf_op jit(solution)/shard_map/ppermute | solution.py:327
  50.3 8.3 %collective-permute-done.5.refs_6_ = bf16[3,400,128]{2,1,0:T(8,128)(2,1)S(1)} collective-permute-done((bf16[3,400,128]{2,1,0:T(8,128)(2,1)S(1)}, bf16[3,400,128]{2,1,0:T(8,128)(2,1)S(1)}, u32[]{:S(2)}, u32[]{:S(2)}) %collective-permute-start.5) | collective-permute-done | bytes 307232 | tf_op jit(solution)/shard_map/ppermute | solution.py:327
  58.5 6.5 %collective-permute-done.6.refs_7_ = bf16[3,400,128]{2,1,0:T(8,128)(2,1)S(1)} collective-permute-done((bf16[3,400,128]{2,1,0:T(8,128)(2,1)S(1)}, bf16[3,400,128]{2,1,0:T(8,128)(2,1)S(1)}, u32[]{:S(2)}, u32[]{:S(2)}) %collective-permute-start.6) | collective-permute-done | bytes 307232 | tf_op jit(solution)/shard_map/ppermute | solution.py:327
  65.0 5.6 %collective-permute-done.2.refs_3_ = bf16[3,656,128]{2,1,0:T(8,128)(2,1)S(1)} collective-permute-done((bf16[3,656,128]{2,1,0:T(8,128)(2,1)S(1)}, bf16[3,656,128]{2,1,0:T(8,128)(2,1)S(1)}, u32[]{:S(2)}, u32[]{:S(2)}) %collective-permute-start.2) | collective-permute-done | bytes 503840 | tf_op jit(solution)/shard_map/ppermute | solution.py:327
  70.7 1.1 gather_keys.2.refs_8_
  71.8 3.5 %collective-permute-start.12 = (bf16[3,272,128]{2,1,0:T(8,128)(2,1)S(1)}, bf16[3,272,128]{2,1,0:T(8,128)(2,1)S(1)}, u32[]{:S(2)}, u32[]{:S(2)}) collective-permute-start(bf16[3,272,128]{2,1,0:T(8,128)(2,1)S(1)} %get-tuple-element.87), channel_id=1, source_target_pairs={{0,12},{1,13},{2,14},{3,15},{4,8},{5,9},{6,10},{7,11},{8,4},{9,5},... | collective-permute-start | bytes 626696 | tf_op jit(solution)/shard_map/ppermute | solution.py:327
  75.4 1.6 %collective-permute-start.11 = (bf16[3,272,128]{2,1,0:T(8,128)(2,1)S(1)}, bf16[3,272,128]{2,1,0:T(8,128)(2,1)S(1)}, u32[]{:S(2)}, u32[]{:S(2)}) collective-permute-start(bf16[3,272,128]{2,1,0:T(8,128)(2,1)S(1)} %get-tuple-element.85), channel_id=1, source_target_pairs={{0,10},{1,11},{2,8},{3,9},{4,14},{5,15},{6,12},{7,13},{8,2},{9,3},... | collective-permute-start | bytes 626696 | tf_op jit(solution)/shard_map/ppermute | solution.py:327
  77.0 3.8 %collective-permute-start.13 = (bf16[3,272,128]{2,1,0:T(8,128)(2,1)S(1)}, bf16[3,272,128]{2,1,0:T(8,128)(2,1)S(1)}, u32[]{:S(2)}, u32[]{:S(2)}) collective-permute-start(bf16[3,272,128]{2,1,0:T(8,128)(2,1)S(1)} %get-tuple-element.89), channel_id=1, source_target_pairs={{0,14},{1,15},{2,12},{3,13},{4,10},{5,11},{6,8},{7,9},{8,6},{9,7},... | collective-permute-start | bytes 626696 | tf_op jit(solution)/shard_map/ppermute | solution.py:327
  80.8 1.2 copy-done.3
  81.9 5.3 %attend.2 = (bf16[384,128]{1,0:T(8,128)(2,1)S(1)}, bf16[384,128]{1,0:T(8,128)(2,1)S(1)}, bf16[384,128]{1,0:T(8,128)(2,1)S(1)}, bf16[384,128]{1,0:T(8,128)(2,1)S(...) custom-call(s32[1]{0:T(128)} %bitcast.me_ref, ...), custom_call_target="tpu_custom_call" | custom-call | flops 4294967296 | bytes 8388608 | tf_op jit(solution)/shard_map/attend/pallas_call | solution.py:256
  87.9 11.1 %collective-permute-done.11.refs_5_ = bf16[3,272,128]{2,1,0:T(8,128)(2,1)S(1)} collective-permute-done((bf16[3,272,128]{2,1,0:T(8,128)(2,1)S(1)}, bf16[3,272,128]{2,1,0:T(8,128)(2,1)S(1)}, u32[]{:S(2)}, u32[]{:S(2)}) %collective-permute-start.11) | collective-permute-done | bytes 208928 | tf_op jit(solution)/shard_map/ppermute | solution.py:327
  99.9 4.5 %collective-permute-start.19 = (bf16[384,128]{1,0:T(8,128)(2,1)S(1)}, bf16[384,128]{1,0:T(8,128)(2,1)S(1)}, u32[]{:S(2)}, u32[]{:S(2)}) collective-permute-start(bf16[384,128]{1,0:T(8,128)(2,1)S(1)} %get-tuple-element.109), channel_id=1, source_target_pairs={{0,14},{1,15},{2,12},{3,13},{4,10},{5,11},{6,8},{7,9},{8,6},{9,7},... | collective-permute-start | bytes 294920 | tf_op jit(solution)/shard_map/ppermute | solution.py:327
  104.8 5.2 %collective-permute-start.17 = (bf16[384,128]{1,0:T(8,128)(2,1)S(1)}, bf16[384,128]{1,0:T(8,128)(2,1)S(1)}, u32[]{:S(2)}, u32[]{:S(2)}) collective-permute-start(bf16[384,128]{1,0:T(8,128)(2,1)S(1)} %get-tuple-element.105), channel_id=1, source_target_pairs={{0,10},{1,11},{2,8},{3,9},{4,14},{5,15},{6,12},{7,13},{8,2},{9,3},... | collective-permute-start | bytes 294920 | tf_op jit(solution)/shard_map/ppermute | solution.py:327
  109.9 3.7 %attend.3 = (bf16[256,128]{1,0:T(8,128)(2,1)S(1)}, bf16[256,128]{1,0:T(8,128)(2,1)S(1)}, bf16[256,128]{1,0:T(8,128)(2,1)S(1)}, bf16[256,128]{1,0:T(8,128)(2,1)S(...) custom-call(s32[1]{0:T(128)} %bitcast.me_ref, ...), custom_call_target="tpu_custom_call" | custom-call | flops 4294967296 | bytes 8388608 | tf_op jit(solution)/shard_map/attend/pallas_call | solution.py:256
  113.7 1.6 %collective-permute-start.20 = (bf16[256,128]{1,0:T(8,128)(2,1)S(1)}, bf16[256,128]{1,0:T(8,128)(2,1)S(1)}, u32[]{:S(2)}, u32[]{:S(2)}) collective-permute-start(bf16[256,128]{1,0:T(8,128)(2,1)S(1)} %get-tuple-element.110), channel_id=1, source_target_pairs={{0,2},{1,3},{2,0},{3,1},{4,6},{5,7},{6,4},{7,5},{8,10},{9,11},{10,... | collective-permute-start | bytes 196616 | tf_op jit(solution)/shard_map/ppermute | solution.py:327
  115.3 2.0 %collective-permute-start.21 = (bf16[256,128]{1,0:T(8,128)(2,1)S(1)}, bf16[256,128]{1,0:T(8,128)(2,1)S(1)}, u32[]{:S(2)}, u32[]{:S(2)}) collective-permute-start(bf16[256,128]{1,0:T(8,128)(2,1)S(1)} %get-tuple-element.111), channel_id=1, source_target_pairs={{0,4},{1,5},{2,6},{3,7},{4,0},{5,1},{6,2},{7,3},{8,12},{9,13},{10,... | collective-permute-start | bytes 196616 | tf_op jit(solution)/shard_map/ppermute | solution.py:327
  118.0 1.7 %collective-permute-done.17.refs_5_ = bf16[384,128]{1,0:T(8,128)(2,1)S(1)} collective-permute-done((bf16[384,128]{1,0:T(8,128)(2,1)S(1)}, bf16[384,128]{1,0:T(8,128)(2,1)S(1)}, u32[]{:S(2)}, u32[]{:S(2)}) %collective-permute-start.17) | collective-permute-done | bytes 98336 | tf_op jit(solution)/shard_map/ppermute | solution.py:327
  119.8 3.7 %collective-permute-start.15 = (bf16[384,128]{1,0:T(8,128)(2,1)S(1)}, bf16[384,128]{1,0:T(8,128)(2,1)S(1)}, u32[]{:S(2)}, u32[]{:S(2)}) collective-permute-start(bf16[384,128]{1,0:T(8,128)(2,1)S(1)} %get-tuple-element.100), channel_id=1, source_target_pairs={{0,6},{1,7},{2,4},{3,5},{4,2},{5,3},{6,0},{7,1},{8,14},{9,15},{10,... | collective-permute-start | bytes 294920 | tf_op jit(solution)/shard_map/ppermute | solution.py:327
  123.5 2.9 %collective-permute-start.24 = (bf16[256,128]{1,0:T(8,128)(2,1)S(1)}, bf16[256,128]{1,0:T(8,128)(2,1)S(1)}, u32[]{:S(2)}, u32[]{:S(2)}) collective-permute-start(bf16[256,128]{1,0:T(8,128)(2,1)S(1)} %get-tuple-element.114), channel_id=1, source_target_pairs={{0,10},{1,11},{2,8},{3,9},{4,14},{5,15},{6,12},{7,13},{8,2},{9,3},... | collective-permute-start | bytes 196616 | tf_op jit(solution)/shard_map/ppermute | solution.py:327
  126.4 1.5 %collective-permute-start.25 = (bf16[256,128]{1,0:T(8,128)(2,1)S(1)}, bf16[256,128]{1,0:T(8,128)(2,1)S(1)}, u32[]{:S(2)}, u32[]{:S(2)}) collective-permute-start(bf16[256,128]{1,0:T(8,128)(2,1)S(1)} %get-tuple-element.115), channel_id=1, source_target_pairs={{0,12},{1,13},{2,14},{3,15},{4,8},{5,9},{6,10},{7,11},{8,4},{9,5},... | collective-permute-start | bytes 196616 | tf_op jit(solution)/shard_map/ppermute | solution.py:327
  127.9 3.3 %collective-permute-start.26 = (bf16[256,128]{1,0:T(8,128)(2,1)S(1)}, bf16[256,128]{1,0:T(8,128)(2,1)S(1)}, u32[]{:S(2)}, u32[]{:S(2)}) collective-permute-start(bf16[256,128]{1,0:T(8,128)(2,1)S(1)} %get-tuple-element.116), channel_id=1, source_target_pairs={{0,14},{1,15},{2,12},{3,13},{4,10},{5,11},{6,8},{7,9},{8,6},{9,7},... | collective-permute-start | bytes 196616 | tf_op jit(solution)/shard_map/ppermute | solution.py:327
  131.2 5.7 %collective-permute-done.24.refs_13_ = bf16[256,128]{1,0:T(8,128)(2,1)S(1)} collective-permute-done((bf16[256,128]{1,0:T(8,128)(2,1)S(1)}, bf16[256,128]{1,0:T(8,128)(2,1)S(1)}, u32[]{:S(2)}, u32[]{:S(2)}) %collective-permute-start.24) | collective-permute-done | bytes 65568 | tf_op jit(solution)/shard_map/ppermute | solution.py:327
  136.9 1.9 %unpack.1 = bf16[128,40,128]{2,1,0:T(8,128)(2,1)} custom-call(s32[1]{0:T(128)} %bitcast.me_ref, bf16[384,128]{1,0:T(8,128)(2,1)S(1)} %get-tuple-element.78.refs_0_, bf16[384,128]{1,0:T(8,128)(2,1)S(1)} %collective-permute-done.9.refs_1_, bf16[384,128]{1,0:T(8,128)(2,1)S(1)} %collective-permute-done.10.refs_2_, ...), custom_call_target="tpu_custom_call" | custom-call | bytes 4194304 | tf_op jit(solution)/shard_map/unpack/pallas_call | solution.py:306
  (37 shorter events, 5.7 us)
Async XLA Ops:
  0.0 0.7 copy-start.1
  0.7 0.7 copy-start.2
  1.3 8.4 %copy-start = (bf16[128,40,3,128]{3,1,2,0:T(8,128)(2,1)S(1)}, bf16[128,40,3,128]{3,1,2,0:T(8,128)(2,1)}, u32[]{:S(2)}) copy-start(bf16[128,40,3,128]{3,1,2,0:T(8,128)(2,1)} %param.3) | copy-start | bytes 11796484
  5.6 27.7 %collective-permute-start.7 = (bf16[3,272,128]{2,1,0:T(8,128)(2,1)S(1)}, bf16[3,272,128]{2,1,0:T(8,128)(2,1)S(1)}, u32[]{:S(2)}, u32[]{:S(2)}) collective-permute-start(bf16[3,272,128]{2,1,0:T(8,128)(2,1)S(1)} %get-tuple-element.69), channel_id=1, source_target_pairs={{0,8},{1,9},{2,10},{3,11},{4,12},{5,13},{6,14},{7,15},{8,0},{9,1},... | collective-permute-start | bytes 626696 | tf_op jit(solution)/shard_map/ppermute | solution.py:327
  11.4 28.6 %collective-permute-start.3 = (bf16[3,400,128]{2,1,0:T(8,128)(2,1)S(1)}, bf16[3,400,128]{2,1,0:T(8,128)(2,1)S(1)}, u32[]{:S(2)}, u32[]{:S(2)}) collective-permute-start(bf16[3,400,128]{2,1,0:T(8,128)(2,1)S(1)} %get-tuple-element.65), channel_id=1, source_target_pairs={{0,8},{1,9},{2,10},{3,11},{4,12},{5,13},{6,14},{7,15},{8,0},{9,1},... | collective-permute-start | bytes 921608 | tf_op jit(solution)/shard_map/ppermute | solution.py:327
  11.5 36.3 %collective-permute-start.4 = (bf16[3,400,128]{2,1,0:T(8,128)(2,1)S(1)}, bf16[3,400,128]{2,1,0:T(8,128)(2,1)S(1)}, u32[]{:S(2)}, u32[]{:S(2)}) collective-permute-start(bf16[3,400,128]{2,1,0:T(8,128)(2,1)S(1)} %get-tuple-element.66), channel_id=1, source_target_pairs={{0,10},{1,11},{2,8},{3,9},{4,14},{5,15},{6,12},{7,13},{8,2},{9,3},... | collective-permute-start | bytes 921608 | tf_op jit(solution)/shard_map/ppermute | solution.py:327
  15.4 49.6 %collective-permute-start = (bf16[3,656,128]{2,1,0:T(8,128)(2,1)S(1)}, bf16[3,656,128]{2,1,0:T(8,128)(2,1)S(1)}, u32[]{:S(2)}, u32[]{:S(2)}) collective-permute-start(bf16[3,656,128]{2,1,0:T(8,128)(2,1)S(1)} %get-tuple-element.62), channel_id=1, source_target_pairs={{0,2},{1,3},{2,0},{3,1},{4,6},{5,7},{6,4},{7,5},{8,10},{9,11},{10,... | collective-permute-start | bytes 1511432 | tf_op jit(solution)/shard_map/ppermute | solution.py:327
  15.9 49.1 %collective-permute-start.1 = (bf16[3,656,128]{2,1,0:T(8,128)(2,1)S(1)}, bf16[3,656,128]{2,1,0:T(8,128)(2,1)S(1)}, u32[]{:S(2)}, u32[]{:S(2)}) collective-permute-start(bf16[3,656,128]{2,1,0:T(8,128)(2,1)S(1)} %get-tuple-element.63), channel_id=1, source_target_pairs={{0,4},{1,5},{2,6},{3,7},{4,0},{5,1},{6,2},{7,3},{8,12},{9,13},{10,... | collective-permute-start | bytes 1511432 | tf_op jit(solution)/shard_map/ppermute | solution.py:327
  33.4 37.3 %collective-permute-start.2 = (bf16[3,656,128]{2,1,0:T(8,128)(2,1)S(1)}, bf16[3,656,128]{2,1,0:T(8,128)(2,1)S(1)}, u32[]{:S(2)}, u32[]{:S(2)}) collective-permute-start(bf16[3,656,128]{2,1,0:T(8,128)(2,1)S(1)} %get-tuple-element.64), channel_id=1, source_target_pairs={{0,6},{1,7},{2,4},{3,5},{4,2},{5,3},{6,0},{7,1},{8,14},{9,15},{10,... | collective-permute-start | bytes 1511432 | tf_op jit(solution)/shard_map/ppermute | solution.py:327
  40.0 18.5 %collective-permute-start.5 = (bf16[3,400,128]{2,1,0:T(8,128)(2,1)S(1)}, bf16[3,400,128]{2,1,0:T(8,128)(2,1)S(1)}, u32[]{:S(2)}, u32[]{:S(2)}) collective-permute-start(bf16[3,400,128]{2,1,0:T(8,128)(2,1)S(1)} %get-tuple-element.67), channel_id=1, source_target_pairs={{0,12},{1,13},{2,14},{3,15},{4,8},{5,9},{6,10},{7,11},{8,4},{9,5},... | collective-permute-start | bytes 921608 | tf_op jit(solution)/shard_map/ppermute | solution.py:327
  47.9 17.2 %collective-permute-start.6 = (bf16[3,400,128]{2,1,0:T(8,128)(2,1)S(1)}, bf16[3,400,128]{2,1,0:T(8,128)(2,1)S(1)}, u32[]{:S(2)}, u32[]{:S(2)}) collective-permute-start(bf16[3,400,128]{2,1,0:T(8,128)(2,1)S(1)} %get-tuple-element.68), channel_id=1, source_target_pairs={{0,14},{1,15},{2,12},{3,13},{4,10},{5,11},{6,8},{7,9},{8,6},{9,7},... | collective-permute-start | bytes 921608 | tf_op jit(solution)/shard_map/ppermute | solution.py:327
  71.7 9.0 %collective-permute-start.8 = (bf16[8,2,384,128]{3,2,1,0:T(8,128)(2,1)S(1)}, bf16[8,2,384,128]{3,2,1,0:T(8,128)(2,1)S(1)}, u32[]{:S(2)}, u32[]{:S(2)}) collective-permute-start(bf16[8,2,384,128]{3,2,1,0:T(8,128)(2,1)S(1)} %gather_keys.2.refs_8_), channel_id=1, source_target_pairs={{0,1},{1,0},{2,3},{3,2},{4,5},{5,4},{6,7},{7,6},{8,9},{9,8},{10,11... | collective-permute-start | bytes 4718600 | tf_op jit(solution)/shard_map/ppermute | solution.py:354
  71.8 16.1 %collective-permute-start.12 = (bf16[3,272,128]{2,1,0:T(8,128)(2,1)S(1)}, bf16[3,272,128]{2,1,0:T(8,128)(2,1)S(1)}, u32[]{:S(2)}, u32[]{:S(2)}) collective-permute-start(bf16[3,272,128]{2,1,0:T(8,128)(2,1)S(1)} %get-tuple-element.87), channel_id=1, source_target_pairs={{0,12},{1,13},{2,14},{3,15},{4,8},{5,9},{6,10},{7,11},{8,4},{9,5},... | collective-permute-start | bytes 626696 | tf_op jit(solution)/shard_map/ppermute | solution.py:327
  75.4 23.6 %collective-permute-start.11 = (bf16[3,272,128]{2,1,0:T(8,128)(2,1)S(1)}, bf16[3,272,128]{2,1,0:T(8,128)(2,1)S(1)}, u32[]{:S(2)}, u32[]{:S(2)}) collective-permute-start(bf16[3,272,128]{2,1,0:T(8,128)(2,1)S(1)} %get-tuple-element.85), channel_id=1, source_target_pairs={{0,10},{1,11},{2,8},{3,9},{4,14},{5,15},{6,12},{7,13},{8,2},{9,3},... | collective-permute-start | bytes 626696 | tf_op jit(solution)/shard_map/ppermute | solution.py:327
  77.0 22.1 %collective-permute-start.13 = (bf16[3,272,128]{2,1,0:T(8,128)(2,1)S(1)}, bf16[3,272,128]{2,1,0:T(8,128)(2,1)S(1)}, u32[]{:S(2)}, u32[]{:S(2)}) collective-permute-start(bf16[3,272,128]{2,1,0:T(8,128)(2,1)S(1)} %get-tuple-element.89), channel_id=1, source_target_pairs={{0,14},{1,15},{2,12},{3,13},{4,10},{5,11},{6,8},{7,9},{8,6},{9,7},... | collective-permute-start | bytes 626696 | tf_op jit(solution)/shard_map/ppermute | solution.py:327
  80.8 1.2 copy-start.3
  87.3 11.7 %collective-permute-start.9 = (bf16[384,128]{1,0:T(8,128)(2,1)S(1)}, bf16[384,128]{1,0:T(8,128)(2,1)S(1)}, u32[]{:S(2)}, u32[]{:S(2)}) collective-permute-start(bf16[384,128]{1,0:T(8,128)(2,1)S(1)} %get-tuple-element.80), channel_id=1, source_target_pairs={{0,2},{1,3},{2,0},{3,1},{4,6},{5,7},{6,4},{7,5},{8,10},{9,11},{10,... | collective-permute-start | bytes 294920 | tf_op jit(solution)/shard_map/ppermute | solution.py:327
  99.8 10.2 %collective-permute-start.14 = (bf16[8,2,256,128]{3,2,1,0:T(8,128)(2,1)S(1)}, bf16[8,2,256,128]{3,2,1,0:T(8,128)(2,1)S(1)}, u32[]{:S(2)}, u32[]{:S(2)}) collective-permute-start(bf16[8,2,256,128]{3,2,1,0:T(8,128)(2,1)S(1)} %gather_keys.3.refs_8_), channel_id=1, source_target_pairs={{0,1},{1,0},{2,3},{3,2},{4,5},{5,4},{6,7},{7,6},{8,9},{9,8},{10,11... | collective-permute-start | bytes 3145736 | tf_op jit(solution)/shard_map/ppermute | solution.py:354
  99.9 15.3 %collective-permute-start.19 = (bf16[384,128]{1,0:T(8,128)(2,1)S(1)}, bf16[384,128]{1,0:T(8,128)(2,1)S(1)}, u32[]{:S(2)}, u32[]{:S(2)}) collective-permute-start(bf16[384,128]{1,0:T(8,128)(2,1)S(1)} %get-tuple-element.109), channel_id=1, source_target_pairs={{0,14},{1,15},{2,12},{3,13},{4,10},{5,11},{6,8},{7,9},{8,6},{9,7},... | collective-permute-start | bytes 294920 | tf_op jit(solution)/shard_map/ppermute | solution.py:327
  104.4 12.8 %collective-permute-start.18 = (bf16[384,128]{1,0:T(8,128)(2,1)S(1)}, bf16[384,128]{1,0:T(8,128)(2,1)S(1)}, u32[]{:S(2)}, u32[]{:S(2)}) collective-permute-start(bf16[384,128]{1,0:T(8,128)(2,1)S(1)} %get-tuple-element.107), channel_id=1, source_target_pairs={{0,12},{1,13},{2,14},{3,15},{4,8},{5,9},{6,10},{7,11},{8,4},{9,5},... | collective-permute-start | bytes 294920 | tf_op jit(solution)/shard_map/ppermute | solution.py:327
  104.8 14.9 %collective-permute-start.17 = (bf16[384,128]{1,0:T(8,128)(2,1)S(1)}, bf16[384,128]{1,0:T(8,128)(2,1)S(1)}, u32[]{:S(2)}, u32[]{:S(2)}) collective-permute-start(bf16[384,128]{1,0:T(8,128)(2,1)S(1)} %get-tuple-element.105), channel_id=1, source_target_pairs={{0,10},{1,11},{2,8},{3,9},{4,14},{5,15},{6,12},{7,13},{8,2},{9,3},... | collective-permute-start | bytes 294920 | tf_op jit(solution)/shard_map/ppermute | solution.py:327
  109.9 9.9 %collective-permute-start.10 = (bf16[384,128]{1,0:T(8,128)(2,1)S(1)}, bf16[384,128]{1,0:T(8,128)(2,1)S(1)}, u32[]{:S(2)}, u32[]{:S(2)}) collective-permute-start(bf16[384,128]{1,0:T(8,128)(2,1)S(1)} %get-tuple-element.82), channel_id=1, source_target_pairs={{0,4},{1,5},{2,6},{3,7},{4,0},{5,1},{6,2},{7,3},{8,12},{9,13},{10,... | collective-permute-start | bytes 294920 | tf_op jit(solution)/shard_map/ppermute | solution.py:327
  113.7 9.8 %collective-permute-start.20 = (bf16[256,128]{1,0:T(8,128)(2,1)S(1)}, bf16[256,128]{1,0:T(8,128)(2,1)S(1)}, u32[]{:S(2)}, u32[]{:S(2)}) collective-permute-start(bf16[256,128]{1,0:T(8,128)(2,1)S(1)} %get-tuple-element.110), channel_id=1, source_target_pairs={{0,2},{1,3},{2,0},{3,1},{4,6},{5,7},{6,4},{7,5},{8,10},{9,11},{10,... | collective-permute-start | bytes 196616 | tf_op jit(solution)/shard_map/ppermute | solution.py:327
  115.3 8.3 %collective-permute-start.21 = (bf16[256,128]{1,0:T(8,128)(2,1)S(1)}, bf16[256,128]{1,0:T(8,128)(2,1)S(1)}, u32[]{:S(2)}, u32[]{:S(2)}) collective-permute-start(bf16[256,128]{1,0:T(8,128)(2,1)S(1)} %get-tuple-element.111), channel_id=1, source_target_pairs={{0,4},{1,5},{2,6},{3,7},{4,0},{5,1},{6,2},{7,3},{8,12},{9,13},{10,... | collective-permute-start | bytes 196616 | tf_op jit(solution)/shard_map/ppermute | solution.py:327
  117.3 9.1 %collective-permute-start.22 = (bf16[256,128]{1,0:T(8,128)(2,1)S(1)}, bf16[256,128]{1,0:T(8,128)(2,1)S(1)}, u32[]{:S(2)}, u32[]{:S(2)}) collective-permute-start(bf16[256,128]{1,0:T(8,128)(2,1)S(1)} %get-tuple-element.112), channel_id=1, source_target_pairs={{0,6},{1,7},{2,4},{3,5},{4,2},{5,3},{6,0},{7,1},{8,14},{9,15},{10,... | collective-permute-start | bytes 196616 | tf_op jit(solution)/shard_map/ppermute | solution.py:327
  119.6 8.2 %collective-permute-start.23 = (bf16[256,128]{1,0:T(8,128)(2,1)S(1)}, bf16[256,128]{1,0:T(8,128)(2,1)S(1)}, u32[]{:S(2)}, u32[]{:S(2)}) collective-permute-start(bf16[256,128]{1,0:T(8,128)(2,1)S(1)} %get-tuple-element.113), channel_id=1, source_target_pairs={{0,8},{1,9},{2,10},{3,11},{4,12},{5,13},{6,14},{7,15},{8,0},{9,1},... | collective-permute-start | bytes 196616 | tf_op jit(solution)/shard_map/ppermute | solution.py:327
  119.8 17.1 %collective-permute-start.15 = (bf16[384,128]{1,0:T(8,128)(2,1)S(1)}, bf16[384,128]{1,0:T(8,128)(2,1)S(1)}, u32[]{:S(2)}, u32[]{:S(2)}) collective-permute-start(bf16[384,128]{1,0:T(8,128)(2,1)S(1)} %get-tuple-element.100), channel_id=1, source_target_pairs={{0,6},{1,7},{2,4},{3,5},{4,2},{5,3},{6,0},{7,1},{8,14},{9,15},{10,... | collective-permute-start | bytes 294920 | tf_op jit(solution)/shard_map/ppermute | solution.py:327
  123.5 13.4 %collective-permute-start.16 = (bf16[384,128]{1,0:T(8,128)(2,1)S(1)}, bf16[384,128]{1,0:T(8,128)(2,1)S(1)}, u32[]{:S(2)}, u32[]{:S(2)}) collective-permute-start(bf16[384,128]{1,0:T(8,128)(2,1)S(1)} %get-tuple-element.103), channel_id=1, source_target_pairs={{0,8},{1,9},{2,10},{3,11},{4,12},{5,13},{6,14},{7,15},{8,0},{9,1},... | collective-permute-start | bytes 294920 | tf_op jit(solution)/shard_map/ppermute | solution.py:327
  123.5 13.3 %collective-permute-start.24 = (bf16[256,128]{1,0:T(8,128)(2,1)S(1)}, bf16[256,128]{1,0:T(8,128)(2,1)S(1)}, u32[]{:S(2)}, u32[]{:S(2)}) collective-permute-start(bf16[256,128]{1,0:T(8,128)(2,1)S(1)} %get-tuple-element.114), channel_id=1, source_target_pairs={{0,10},{1,11},{2,8},{3,9},{4,14},{5,15},{6,12},{7,13},{8,2},{9,3},... | collective-permute-start | bytes 196616 | tf_op jit(solution)/shard_map/ppermute | solution.py:327
  126.4 10.5 %collective-permute-start.25 = (bf16[256,128]{1,0:T(8,128)(2,1)S(1)}, bf16[256,128]{1,0:T(8,128)(2,1)S(1)}, u32[]{:S(2)}, u32[]{:S(2)}) collective-permute-start(bf16[256,128]{1,0:T(8,128)(2,1)S(1)} %get-tuple-element.115), channel_id=1, source_target_pairs={{0,12},{1,13},{2,14},{3,15},{4,8},{5,9},{6,10},{7,11},{8,4},{9,5},... | collective-permute-start | bytes 196616 | tf_op jit(solution)/shard_map/ppermute | solution.py:327
  127.9 9.0 %collective-permute-start.26 = (bf16[256,128]{1,0:T(8,128)(2,1)S(1)}, bf16[256,128]{1,0:T(8,128)(2,1)S(1)}, u32[]{:S(2)}, u32[]{:S(2)}) collective-permute-start(bf16[256,128]{1,0:T(8,128)(2,1)S(1)} %get-tuple-element.116), channel_id=1, source_target_pairs={{0,14},{1,15},{2,12},{3,13},{4,10},{5,11},{6,8},{7,9},{8,6},{9,7},... | collective-permute-start | bytes 196616 | tf_op jit(solution)/shard_map/ppermute | solution.py:327
